TPU v7x, 256 devices: a whole 4x4x8 slice. The times are simulated.
256 devices in a mesh: gx: 32 (over y, z), gy: 8 (over x, core).
Axes of the slice: x: 4, y: 4, z: 8, core: 2. Of those that a mesh axis runs over, the one named last changes fastest.
Arguments:
- right_side: float32 [64, 256, 1024], P(None, 'gx', 'gy'), may hold values from -6 to 6
- conductivity: float32 [64, 256, 1024], P(None, 'gx', 'gy'), may hold values from 0.1 to 10
Outputs:
- pressure: float32 [64, 256, 1024], P(None, 'gx', 'gy')
- residual: float32 [64, 256, 1024], P(None, 'gx', 'gy')
All inputs are finite; a program needn't handle non-finite values.
Results may differ from a plain program's by a relative error of at most 0.0003.
Values sent between devices are 32-bit elements; how exact they have to be, the bound alone decides.
No kernel may reach another device: no remote copies, remote signals or barrier semaphores. Data moves between devices by JAX's collectives and lax.ppermute only.
A program may use at most 128 MiB of HBM per device.

v0:
```python
import jax
import jax.numpy as jnp
from jax import lax
from jax.sharding import PartitionSpec as P

COARSE = 8


LOW_BOUND = 0.3
HIGH_BOUND = 2.0
COARSE_LOW = 0.02


def extended(value, sides, width):
    for axis, dim in sides:
        size, length = (lax.axis_size(axis), value.shape[dim])
        up = [(i, (i + 1) % size) for i in range(size - 1)]
        down = [(j, i) for i, j in up]
        last = lax.slice_in_dim(value, length - width, length, axis=dim)
        initial = lax.slice_in_dim(value, 0, width, axis=dim)
        before = lax.ppermute(last, axis, up)
        after = lax.ppermute(initial, axis, down)
        value = jnp.concatenate([before, value, after], axis=dim)
    return value


def neighbours(padded):
    return [
        padded[2:, 1:-1, 1:-1],
        padded[:-2, 1:-1, 1:-1],
        padded[1:-1, 2:, 1:-1],
        padded[1:-1, :-2, 1:-1],
        padded[1:-1, 1:-1, 2:],
        padded[1:-1, 1:-1, :-2],
    ]


def make_operator(padded_conduct, factor):
    centre = padded_conduct[1:-1, 1:-1, 1:-1]
    weights = [0.5 * (centre + other) for other in neighbours(padded_conduct)]
    diagonal = factor * (
        weights[0] + weights[1] + weights[2] + weights[3] + weights[4] + weights[5]
    )
    return (weights, diagonal, factor)


def stencil(field, padded_field, operator):
    weights, diagonal, factor = operator
    others = neighbours(padded_field)
    total = weights[0] * others[0]
    for index in range(1, 6):
        total = total + weights[index] * others[index]
    return diagonal * field - factor * total


def coarsen(field):
    shape = field.shape
    blocks = field.reshape(shape[0] // 2, 2, shape[1] // 2, 2, shape[2] // 2, 2)
    return jnp.mean(blocks, axis=(1, 3, 5))


def refine(field):
    return jnp.repeat(jnp.repeat(jnp.repeat(field, 2, axis=0), 2, axis=1), 2, axis=2)


def smooth(operate, diagonal, source, start, sweeps, lower):
    middle = (HIGH_BOUND + lower) / 2
    half_width = (HIGH_BOUND - lower) / 2
    ratio_mid = middle / half_width
    cheb_rho = 1 / ratio_mid
    residue = source if start is None else source - operate(start)
    update = residue / diagonal / middle
    iterate = update if start is None else start + update
    for sweep in range(sweeps - 1):
        residue = source - operate(iterate)
        rho_next = 1 / (2 * ratio_mid - cheb_rho)
        update = rho_next * cheb_rho * update + 2 * rho_next / half_width * (residue / diagonal)
        iterate = iterate + update
        cheb_rho = rho_next
    return iterate


def halo_field(field):
    rims = extended(field, (("gx", 1), ("gy", 2)), 1)
    return jnp.pad(rims, ((1, 1), (0, 0), (0, 0)))


def halo_conduct(conduct):
    rims = extended(conduct, (("gx", 1), ("gy", 2)), 1)
    return jnp.pad(rims, ((1, 1), (0, 0), (0, 0)))


def on_device(right_side, conductivity):
    conducts = [conductivity]
    for grid_level in range(3):
        conducts.append(coarsen(conducts[-1]))
    plain_ops = {}

    def operator_at(grid_level):
        if grid_level not in plain_ops:
            plain_ops[grid_level] = make_operator(
                halo_conduct(conducts[grid_level]), 0.25**grid_level
            )
        return plain_ops[grid_level]

    def operate_at(grid_level):
        operator = operator_at(grid_level)
        return lambda field: stencil(field, halo_field(field), operator)

    def coarse_solve(source):
        operator = make_operator(halo_conduct(conducts[3]), 0.25**3)
        return smooth(
            lambda field: stencil(field, halo_field(field), operator),
            operator[1],
            source,
            None,
            COARSE,
            COARSE_LOW,
        )

    def vcycle(grid_level, source):
        if grid_level == 3:
            return coarse_solve(source)
        diagonal = operator_at(grid_level)[1]
        operate = operate_at(grid_level)
        iterate = smooth(operate, diagonal, source, None, 2, LOW_BOUND)
        residue = source - operate(iterate)
        iterate = iterate + refine(vcycle(grid_level + 1, coarsen(residue)))
        return smooth(operate, diagonal, source, iterate, 2, LOW_BOUND)

    pressure = vcycle(0, right_side)
    return (pressure, right_side - operate_at(0)(pressure))


def solution(mesh):
    in_specs = (P(None, "gx", "gy"), P(None, "gx", "gy"))
    out_specs = (P(None, "gx", "gy"), P(None, "gx", "gy"))
    return jax.shard_map(
        on_device, mesh=mesh, in_specs=in_specs, out_specs=out_specs, check_vma=False
    )
```

profile of v0, /device:TPU:1, one launch (start us, length us, event | category | flops | bytes accessed | tf_op | source)
XLA Modules:
  0.0 470.2 jit_solution(18358708826623093540)
XLA Ops:
  2.0 4.4 collective-permute-start
  7.7 18.1 %reshape.71 = f32[32,2,4,2,64,2]{5,4,3,2,1,0:T(8,128)} reshape(f32[64,8,128]{2,1,0:T(8,128)S(1)} %copy-done) | data formatting | bytes 524288 | tf_op jit(solution)/shard_map/reshape | solution.py:58
  25.8 7.0 %reduce_sum.69 = f32[32,4,64]{2,1,0:T(4,128)S(1)} reduce(f32[32,2,4,2,64,2]{5,4,3,2,1,0:T(8,128)} %reshape.71, f32[]{:T(128)} %constant.24.clone.1), dimensions={1,3,5}, to_apply=%region_1.0 | reduce | flops 57344 | bytes 294916 | tf_op jit(solution)/shard_map/reduce_sum | solution.py:59
  54.6 5.0 %collective-permute-done.5 = f32[64,1,128]{0,1,2:T(1,128)S(1)} collective-permute-done((f32[64,1,128]{0,1,2:T(1,128)S(1)}, f32[64,1,128]{0,1,2:T(1,128)S(1)}, u32[]{:S(2)}, u32[]{:S(2)}) %collective-permute-start.5) | collective-permute-done | bytes 32800 | tf_op jit(solution)/shard_map/ppermute | solution.py:22
  61.5 5.1 %collective-permute-start.6 = (f32[64,10,1]{0,1,2:T(8,128)S(1)}, f32[64,10,1]{0,1,2:T(8,128)S(1)}, u32[]{:S(2)}, u32[]{:S(2)}) collective-permute-start(f32[64,10,1]{0,1,2:T(8,128)S(1)} %get-tuple-element.58), channel_id=1, source_target_pairs={{0,1},{1,2},{2,3},{3,4},{4,5},{5,6},{6,7},{8,9},{9,10},{10,11},{11... | collective-permute-start | bytes 7688 | tf_op jit(solution)/shard_map/ppermute | solution.py:21
  69.3 4.9 %collective-permute-start.8 = (f32[64,1,128]{0,1,2:T(1,128)S(1)}, f32[64,1,128]{0,1,2:T(1,128)S(1)}, u32[]{:S(2)}, u32[]{:S(2)}) collective-permute-start(f32[64,1,128]{0,1,2:T(1,128)S(1)} %get-tuple-element.67), channel_id=1, source_target_pairs={{0,8},{8,16},{16,24},{24,32},{32,40},{40,48},{48,56},{56,64},{64,7... | collective-permute-start | bytes 98312 | tf_op jit(solution)/shard_map/ppermute | solution.py:21
  75.6 4.5 collective-permute-start.14
  91.8 18.8 %reshape.70 = f32[32,2,4,2,64,2]{5,4,3,2,1,0:T(8,128)} reshape(f32[64,8,128]{2,1,0:T(8,128)} %copy.224) | data formatting | bytes 524288 | tf_op jit(solution)/shard_map/reshape | solution.py:58
  110.6 7.0 %reduce_sum.68 = f32[32,4,64]{2,1,0:T(4,128)S(1)} reduce(f32[32,2,4,2,64,2]{5,4,3,2,1,0:T(8,128)} %reshape.70, f32[]{:T(128)} %constant.24.clone.1), dimensions={1,3,5}, to_apply=%region_0.0 | reduce | flops 57344 | bytes 294916 | tf_op jit(solution)/shard_map/reduce_sum | solution.py:59
  119.2 5.1 %collective-permute-start.16 = (f32[32,1,64]{2,1,0:T(1,128)S(1)}, f32[32,1,64]{2,1,0:T(1,128)S(1)}, u32[]{:S(2)}, u32[]{:S(2)}) collective-permute-start(f32[32,1,64]{2,1,0:T(1,128)S(1)} %get-tuple-element.89), channel_id=1, source_target_pairs={{0,8},{8,16},{16,24},{24,32},{32,40},{40,48},{48,56},{56,64},{64,7... | collective-permute-start | bytes 24584 | tf_op jit(solution)/shard_map/ppermute | solution.py:21
  125.6 5.5 %collective-permute-start.24 = (f32[16,1,32]{2,0,1:T(8,128)S(1)}, f32[16,1,32]{2,0,1:T(8,128)S(1)}, u32[]{:S(2)}, u32[]{:S(2)}) collective-permute-start(f32[16,1,32]{2,0,1:T(8,128)S(1)} %get-tuple-element.112), channel_id=1, source_target_pairs={{0,8},{8,16},{16,24},{24,32},{32,40},{40,48},{48,56},{56,64},{64,7... | collective-permute-start | bytes 6152 | tf_op jit(solution)/shard_map/ppermute | solution.py:21
  134.5 4.4 collective-permute-start.18
  147.2 4.6 collective-permute-start.26
  176.0 5.3 %collective-permute-start.36 = (f32[8,1,16]{2,0,1:T(8,128)S(1)}, f32[8,1,16]{2,0,1:T(8,128)S(1)}, u32[]{:S(2)}, u32[]{:S(2)}) collective-permute-start(f32[8,1,16]{2,0,1:T(8,128)S(1)} %multiply_bitcast_fusion), channel_id=1, source_target_pairs={{0,8},{8,16},{16,24},{24,32},{32,40},{40,48},{48,56},{56,64},{64,7... | collective-permute-start | bytes 1544 | tf_op jit(solution)/shard_map/ppermute | solution.py:21
  183.4 4.9 %collective-permute-start.30 = (f32[16,4,1]{2,0,1:T(8,128)S(1)}, f32[16,4,1]{2,0,1:T(8,128)S(1)}, u32[]{:S(2)}, u32[]{:S(2)}) collective-permute-start(f32[16,4,1]{2,0,1:T(8,128)S(1)} %get-tuple-element.100), channel_id=1, source_target_pairs={{0,1},{1,2},{2,3},{3,4},{4,5},{5,6},{6,7},{8,9},{9,10},{10,11},{11... | collective-permute-start | bytes 776 | tf_op jit(solution)/shard_map/ppermute | solution.py:21
  190.3 4.9 %collective-permute-start.32 = (f32[16,1,32]{2,0,1:T(8,128)S(1)}, f32[16,1,32]{2,0,1:T(8,128)S(1)}, u32[]{:S(2)}, u32[]{:S(2)}) collective-permute-start(f32[16,1,32]{2,0,1:T(8,128)S(1)} %get-tuple-element.108), channel_id=1, source_target_pairs={{0,8},{8,16},{16,24},{24,32},{32,40},{40,48},{48,56},{56,64},{64,7... | collective-permute-start | bytes 6152 | tf_op jit(solution)/shard_map/ppermute | solution.py:21
  196.5 4.5 collective-permute-start.38
  213.5 6.1 %collective-permute-start.40 = (f32[8,1,16]{2,0,1:T(8,128)S(1)}, f32[8,1,16]{2,0,1:T(8,128)S(1)}, u32[]{:S(2)}, u32[]{:S(2)}) collective-permute-start(f32[8,1,16]{2,0,1:T(8,128)S(1)} %get-tuple-element.28), channel_id=1, source_target_pairs={{0,8},{8,16},{16,24},{24,32},{32,40},{40,48},{48,56},{56,64},{64,7... | collective-permute-start | bytes 1544 | tf_op jit(solution)/shard_map/ppermute | solution.py:21
  222.4 5.1 %collective-permute-start.42 = (f32[8,3,1]{2,0,1:T(8,128)S(1)}, f32[8,3,1]{2,0,1:T(8,128)S(1)}, u32[]{:S(2)}, u32[]{:S(2)}) collective-permute-start(f32[8,3,1]{2,0,1:T(8,128)S(1)} %get-tuple-element.127), channel_id=1, source_target_pairs={{0,1},{1,2},{2,3},{3,4},{4,5},{5,6},{6,7},{8,9},{9,10},{10,11},{11... | collective-permute-start | bytes 296 | tf_op jit(solution)/shard_map/ppermute | solution.py:21
  229.8 5.5 %collective-permute-start.44 = (f32[8,1,16]{2,0,1:T(8,128)S(1)}, f32[8,1,16]{2,0,1:T(8,128)S(1)}, u32[]{:S(2)}, u32[]{:S(2)}) collective-permute-start(f32[8,1,16]{2,0,1:T(8,128)S(1)} %get-tuple-element.26), channel_id=1, source_target_pairs={{0,8},{8,16},{16,24},{24,32},{32,40},{40,48},{48,56},{56,64},{64,7... | collective-permute-start | bytes 1544 | tf_op jit(solution)/shard_map/ppermute | solution.py:21
  238.0 5.1 %collective-permute-start.46 = (f32[8,3,1]{2,0,1:T(8,128)S(1)}, f32[8,3,1]{2,0,1:T(8,128)S(1)}, u32[]{:S(2)}, u32[]{:S(2)}) collective-permute-start(f32[8,3,1]{2,0,1:T(8,128)S(1)} %get-tuple-element.125), channel_id=1, source_target_pairs={{0,1},{1,2},{2,3},{3,4},{4,5},{5,6},{6,7},{8,9},{9,10},{10,11},{11... | collective-permute-start | bytes 296 | tf_op jit(solution)/shard_map/ppermute | solution.py:21
  245.3 4.5 collective-permute-start.48
  252.6 5.1 %collective-permute-start.50 = (f32[8,3,1]{2,0,1:T(8,128)S(1)}, f32[8,3,1]{2,0,1:T(8,128)S(1)}, u32[]{:S(2)}, u32[]{:S(2)}) collective-permute-start(f32[8,3,1]{2,0,1:T(8,128)S(1)} %get-tuple-element.123), channel_id=1, source_target_pairs={{0,1},{1,2},{2,3},{3,4},{4,5},{5,6},{6,7},{8,9},{9,10},{10,11},{11... | collective-permute-start | bytes 296 | tf_op jit(solution)/shard_map/ppermute | solution.py:21
  259.9 5.2 %collective-permute-start.52 = (f32[8,1,16]{2,0,1:T(8,128)S(1)}, f32[8,1,16]{2,0,1:T(8,128)S(1)}, u32[]{:S(2)}, u32[]{:S(2)}) collective-permute-start(f32[8,1,16]{2,0,1:T(8,128)S(1)} %get-tuple-element.22), channel_id=1, source_target_pairs={{0,8},{8,16},{16,24},{24,32},{32,40},{40,48},{48,56},{56,64},{64,7... | collective-permute-start | bytes 1544 | tf_op jit(solution)/shard_map/ppermute | solution.py:21
  267.9 5.1 %collective-permute-start.54 = (f32[8,3,1]{2,0,1:T(8,128)S(1)}, f32[8,3,1]{2,0,1:T(8,128)S(1)}, u32[]{:S(2)}, u32[]{:S(2)}) collective-permute-start(f32[8,3,1]{2,0,1:T(8,128)S(1)} %get-tuple-element.121), channel_id=1, source_target_pairs={{0,1},{1,2},{2,3},{3,4},{4,5},{5,6},{6,7},{8,9},{9,10},{10,11},{11... | collective-permute-start | bytes 296 | tf_op jit(solution)/shard_map/ppermute | solution.py:21
  275.2 5.7 %collective-permute-start.56 = (f32[8,1,16]{2,0,1:T(8,128)S(1)}, f32[8,1,16]{2,0,1:T(8,128)S(1)}, u32[]{:S(2)}, u32[]{:S(2)}) collective-permute-start(f32[8,1,16]{2,0,1:T(8,128)S(1)} %get-tuple-element.20), channel_id=1, source_target_pairs={{0,8},{8,16},{16,24},{24,32},{32,40},{40,48},{48,56},{56,64},{64,7... | collective-permute-start | bytes 1544 | tf_op jit(solution)/shard_map/ppermute | solution.py:21
  283.9 5.1 %collective-permute-start.58 = (f32[8,3,1]{2,0,1:T(8,128)S(1)}, f32[8,3,1]{2,0,1:T(8,128)S(1)}, u32[]{:S(2)}, u32[]{:S(2)}) collective-permute-start(f32[8,3,1]{2,0,1:T(8,128)S(1)} %get-tuple-element.119), channel_id=1, source_target_pairs={{0,1},{1,2},{2,3},{3,4},{4,5},{5,6},{6,7},{8,9},{9,10},{10,11},{11... | collective-permute-start | bytes 296 | tf_op jit(solution)/shard_map/ppermute | solution.py:21
  291.3 5.7 %collective-permute-start.60 = (f32[8,1,16]{2,0,1:T(8,128)S(1)}, f32[8,1,16]{2,0,1:T(8,128)S(1)}, u32[]{:S(2)}, u32[]{:S(2)}) collective-permute-start(f32[8,1,16]{2,0,1:T(8,128)S(1)} %get-tuple-element.18), channel_id=1, source_target_pairs={{0,8},{8,16},{16,24},{24,32},{32,40},{40,48},{48,56},{56,64},{64,7... | collective-permute-start | bytes 1544 | tf_op jit(solution)/shard_map/ppermute | solution.py:21
  299.8 5.1 %collective-permute-start.62 = (f32[8,3,1]{2,0,1:T(8,128)S(1)}, f32[8,3,1]{2,0,1:T(8,128)S(1)}, u32[]{:S(2)}, u32[]{:S(2)}) collective-permute-start(f32[8,3,1]{2,0,1:T(8,128)S(1)} %get-tuple-element.117), channel_id=1, source_target_pairs={{0,1},{1,2},{2,3},{3,4},{4,5},{5,6},{6,7},{8,9},{9,10},{10,11},{11... | collective-permute-start | bytes 296 | tf_op jit(solution)/shard_map/ppermute | solution.py:21
  307.1 5.7 %collective-permute-start.64 = (f32[8,1,16]{2,0,1:T(8,128)S(1)}, f32[8,1,16]{2,0,1:T(8,128)S(1)}, u32[]{:S(2)}, u32[]{:S(2)}) collective-permute-start(f32[8,1,16]{2,0,1:T(8,128)S(1)} %get-tuple-element.16), channel_id=1, source_target_pairs={{0,8},{8,16},{16,24},{24,32},{32,40},{40,48},{48,56},{56,64},{64,7... | collective-permute-start | bytes 1544 | tf_op jit(solution)/shard_map/ppermute | solution.py:21
  315.6 5.1 %collective-permute-start.66 = (f32[8,3,1]{2,0,1:T(8,128)S(1)}, f32[8,3,1]{2,0,1:T(8,128)S(1)}, u32[]{:S(2)}, u32[]{:S(2)}) collective-permute-start(f32[8,3,1]{2,0,1:T(8,128)S(1)} %get-tuple-element.115), channel_id=1, source_target_pairs={{0,1},{1,2},{2,3},{3,4},{4,5},{5,6},{6,7},{8,9},{9,10},{10,11},{11... | collective-permute-start | bytes 296 | tf_op jit(solution)/shard_map/ppermute | solution.py:21
  321.8 5.1 %collective-permute-start.68 = (f32[16,1,32]{2,0,1:T(8,128)S(1)}, f32[16,1,32]{2,0,1:T(8,128)S(1)}, u32[]{:S(2)}, u32[]{:S(2)}) collective-permute-start(f32[16,1,32]{2,0,1:T(8,128)S(1)} %get-tuple-element.105), channel_id=1, source_target_pairs={{0,8},{8,16},{16,24},{24,32},{32,40},{40,48},{48,56},{56,64},{64,7... | collective-permute-start | bytes 6152 | tf_op jit(solution)/shard_map/ppermute | solution.py:21
  328.3 4.8 %collective-permute-done.69 = f32[16,1,32]{2,0,1:T(8,128)S(1)} collective-permute-done((f32[16,1,32]{2,0,1:T(8,128)S(1)}, f32[16,1,32]{2,0,1:T(8,128)S(1)}, u32[]{:S(2)}, u32[]{:S(2)}) %collective-permute-start.69) | collective-permute-done | bytes 2080 | tf_op jit(solution)/shard_map/ppermute | solution.py:22
  335.1 5.3 %collective-permute-start.70 = (f32[16,4,1]{2,0,1:T(8,128)S(1)}, f32[16,4,1]{2,0,1:T(8,128)S(1)}, u32[]{:S(2)}, u32[]{:S(2)}) collective-permute-start(f32[16,4,1]{2,0,1:T(8,128)S(1)} %get-tuple-element.96), channel_id=1, source_target_pairs={{0,1},{1,2},{2,3},{3,4},{4,5},{5,6},{6,7},{8,9},{9,10},{10,11},{11... | collective-permute-start | bytes 776 | tf_op jit(solution)/shard_map/ppermute | solution.py:21
  341.7 5.1 %collective-permute-start.72 = (f32[16,1,32]{2,0,1:T(8,128)S(1)}, f32[16,1,32]{2,0,1:T(8,128)S(1)}, u32[]{:S(2)}, u32[]{:S(2)}) collective-permute-start(f32[16,1,32]{2,0,1:T(8,128)S(1)} %get-tuple-element.103), channel_id=1, source_target_pairs={{0,8},{8,16},{16,24},{24,32},{32,40},{40,48},{48,56},{56,64},{64,7... | collective-permute-start | bytes 6152 | tf_op jit(solution)/shard_map/ppermute | solution.py:21
  348.1 4.8 %collective-permute-done.73 = f32[16,1,32]{2,0,1:T(8,128)S(1)} collective-permute-done((f32[16,1,32]{2,0,1:T(8,128)S(1)}, f32[16,1,32]{2,0,1:T(8,128)S(1)}, u32[]{:S(2)}, u32[]{:S(2)}) %collective-permute-start.73) | collective-permute-done | bytes 2080 | tf_op jit(solution)/shard_map/ppermute | solution.py:22
  355.0 5.4 %collective-permute-start.74 = (f32[16,4,1]{2,0,1:T(8,128)S(1)}, f32[16,4,1]{2,0,1:T(8,128)S(1)}, u32[]{:S(2)}, u32[]{:S(2)}) collective-permute-start(f32[16,4,1]{2,0,1:T(8,128)S(1)} %get-tuple-element.94), channel_id=1, source_target_pairs={{0,1},{1,2},{2,3},{3,4},{4,5},{5,6},{6,7},{8,9},{9,10},{10,11},{11... | collective-permute-start | bytes 776 | tf_op jit(solution)/shard_map/ppermute | solution.py:21
  361.9 6.0 %collective-permute-start.76 = (f32[32,1,64]{2,1,0:T(1,128)S(1)}, f32[32,1,64]{2,1,0:T(1,128)S(1)}, u32[]{:S(2)}, u32[]{:S(2)}) collective-permute-start(f32[32,1,64]{2,1,0:T(1,128)S(1)} %get-tuple-element.85), channel_id=1, source_target_pairs={{0,8},{8,16},{16,24},{24,32},{32,40},{40,48},{48,56},{56,64},{64,7... | collective-permute-start | bytes 24584 | tf_op jit(solution)/shard_map/ppermute | solution.py:21
  369.2 5.8 %collective-permute-done.77 = f32[32,1,64]{2,1,0:T(1,128)S(1)} collective-permute-done((f32[32,1,64]{2,1,0:T(1,128)S(1)}, f32[32,1,64]{2,1,0:T(1,128)S(1)}, u32[]{:S(2)}, u32[]{:S(2)}) %collective-permute-start.77) | collective-permute-done | bytes 8224 | tf_op jit(solution)/shard_map/ppermute | solution.py:22
  377.1 5.4 %collective-permute-start.78 = (f32[32,6,1]{2,1,0:T(8,128)S(1)}, f32[32,6,1]{2,1,0:T(8,128)S(1)}, u32[]{:S(2)}, u32[]{:S(2)}) collective-permute-start(f32[32,6,1]{2,1,0:T(8,128)S(1)} %get-tuple-element.76), channel_id=1, source_target_pairs={{0,1},{1,2},{2,3},{3,4},{4,5},{5,6},{6,7},{8,9},{9,10},{10,11},{11... | collective-permute-start | bytes 2312 | tf_op jit(solution)/shard_map/ppermute | solution.py:21
  385.1 6.0 %collective-permute-start.80 = (f32[32,1,64]{2,1,0:T(1,128)S(1)}, f32[32,1,64]{2,1,0:T(1,128)S(1)}, u32[]{:S(2)}, u32[]{:S(2)}) collective-permute-start(f32[32,1,64]{2,1,0:T(1,128)S(1)} %get-tuple-element.83), channel_id=1, source_target_pairs={{0,8},{8,16},{16,24},{24,32},{32,40},{40,48},{48,56},{56,64},{64,7... | collective-permute-start | bytes 24584 | tf_op jit(solution)/shard_map/ppermute | solution.py:21
  392.4 5.8 %collective-permute-done.81 = f32[32,1,64]{2,1,0:T(1,128)S(1)} collective-permute-done((f32[32,1,64]{2,1,0:T(1,128)S(1)}, f32[32,1,64]{2,1,0:T(1,128)S(1)}, u32[]{:S(2)}, u32[]{:S(2)}) %collective-permute-start.81) | collective-permute-done | bytes 8224 | tf_op jit(solution)/shard_map/ppermute | solution.py:22
  400.4 5.5 %collective-permute-start.82 = (f32[32,6,1]{2,1,0:T(8,128)S(1)}, f32[32,6,1]{2,1,0:T(8,128)S(1)}, u32[]{:S(2)}, u32[]{:S(2)}) collective-permute-start(f32[32,6,1]{2,1,0:T(8,128)S(1)} %get-tuple-element.74), channel_id=1, source_target_pairs={{0,1},{1,2},{2,3},{3,4},{4,5},{5,6},{6,7},{8,9},{9,10},{10,11},{11... | collective-permute-start | bytes 2312 | tf_op jit(solution)/shard_map/ppermute | solution.py:21
  408.9 5.8 %collective-permute-start.84 = (f32[64,1,128]{0,1,2:T(1,128)S(1)}, f32[64,1,128]{0,1,2:T(1,128)S(1)}, u32[]{:S(2)}, u32[]{:S(2)}) collective-permute-start(f32[64,1,128]{0,1,2:T(1,128)S(1)} %get-tuple-element.65), channel_id=1, source_target_pairs={{0,8},{8,16},{16,24},{24,32},{32,40},{40,48},{48,56},{56,64},{64,7... | collective-permute-start | bytes 98312 | tf_op jit(solution)/shard_map/ppermute | solution.py:21
  421.9 5.5 %collective-permute-start.86 = (f32[64,10,1]{0,1,2:T(8,128)S(1)}, f32[64,10,1]{0,1,2:T(8,128)S(1)}, u32[]{:S(2)}, u32[]{:S(2)}) collective-permute-start(f32[64,10,1]{0,1,2:T(8,128)S(1)} %get-tuple-element.54), channel_id=1, source_target_pairs={{0,1},{1,2},{2,3},{3,4},{4,5},{5,6},{6,7},{8,9},{9,10},{10,11},{11... | collective-permute-start | bytes 7688 | tf_op jit(solution)/shard_map/ppermute | solution.py:21
  430.1 4.9 %collective-permute-start.88 = (f32[64,1,128]{0,1,2:T(1,128)S(1)}, f32[64,1,128]{0,1,2:T(1,128)S(1)}, u32[]{:S(2)}, u32[]{:S(2)}) collective-permute-start(f32[64,1,128]{0,1,2:T(1,128)S(1)} %get-tuple-element.63), channel_id=1, source_target_pairs={{0,8},{8,16},{16,24},{24,32},{32,40},{40,48},{48,56},{56,64},{64,7... | collective-permute-start | bytes 98312 | tf_op jit(solution)/shard_map/ppermute | solution.py:21
  442.2 5.3 %collective-permute-start.90 = (f32[64,10,1]{0,1,2:T(8,128)S(1)}, f32[64,10,1]{0,1,2:T(8,128)S(1)}, u32[]{:S(2)}, u32[]{:S(2)}) collective-permute-start(f32[64,10,1]{0,1,2:T(8,128)S(1)} %get-tuple-element.52), channel_id=1, source_target_pairs={{0,1},{1,2},{2,3},{3,4},{4,5},{5,6},{6,7},{8,9},{9,10},{10,11},{11... | collective-permute-start | bytes 7688 | tf_op jit(solution)/shard_map/ppermute | solution.py:21
  461.3 5.3 %collective-permute-start.94 = (f32[64,10,1]{0,1,2:T(8,128)S(1)}, f32[64,10,1]{0,1,2:T(8,128)S(1)}, u32[]{:S(2)}, u32[]{:S(2)}) collective-permute-start(f32[64,10,1]{0,1,2:T(8,128)S(1)} %get-tuple-element.50), channel_id=1, source_target_pairs={{0,1},{1,2},{2,3},{3,4},{4,5},{5,6},{6,7},{8,9},{9,10},{10,11},{11... | collective-permute-start | bytes 7688 | tf_op jit(solution)/shard_map/ppermute | solution.py:21
  (320 shorter events, 187.8 us)
Async XLA Ops:
  2.0 30.8 %collective-permute-start = (f32[64,1,128]{0,1,2:T(1,128)S(1)}, f32[64,1,128]{0,1,2:T(1,128)S(1)}, u32[]{:S(2)}, u32[]{:S(2)}) collective-permute-start(f32[64,1,128]{0,1,2:T(1,128)S(1)} %get-tuple-element.71), channel_id=1, source_target_pairs={{0,8},{8,16},{16,24},{24,32},{32,40},{40,48},{48,56},{56,64},{64,7... | collective-permute-start | bytes 98312 | tf_op jit(solution)/shard_map/ppermute | solution.py:21
  6.4 26.5 %collective-permute-start.1 = (f32[64,1,128]{0,1,2:T(1,128)S(1)}, f32[64,1,128]{0,1,2:T(1,128)S(1)}, u32[]{:S(2)}, u32[]{:S(2)}) collective-permute-start(f32[64,1,128]{0,1,2:T(1,128)S(1)} %get-tuple-element.72), channel_id=1, source_target_pairs={{8,0},{16,8},{24,16},{32,24},{40,32},{48,40},{56,48},{64,56},{72,6... | collective-permute-start | bytes 98312 | tf_op jit(solution)/shard_map/ppermute | solution.py:22
  32.9 14.8 %collective-permute-start.2 = (f32[64,10,1]{0,1,2:T(8,128)S(1)}, f32[64,10,1]{0,1,2:T(8,128)S(1)}, u32[]{:S(2)}, u32[]{:S(2)}) collective-permute-start(f32[64,10,1]{0,1,2:T(8,128)S(1)} %get-tuple-element.59), channel_id=1, source_target_pairs={{0,1},{1,2},{2,3},{3,4},{4,5},{5,6},{6,7},{8,9},{9,10},{10,11},{11... | collective-permute-start | bytes 7688 | tf_op jit(solution)/shard_map/ppermute | solution.py:21
  36.8 10.8 %collective-permute-start.3 = (f32[64,10,1]{0,1,2:T(8,128)S(1)}, f32[64,10,1]{0,1,2:T(8,128)S(1)}, u32[]{:S(2)}, u32[]{:S(2)}) collective-permute-start(f32[64,10,1]{0,1,2:T(8,128)S(1)} %get-tuple-element.60), channel_id=1, source_target_pairs={{1,0},{2,1},{3,2},{4,3},{5,4},{6,5},{7,6},{9,8},{10,9},{11,10},{12... | collective-permute-start | bytes 7688 | tf_op jit(solution)/shard_map/ppermute | solution.py:22
  39.4 27.2 %collective-permute-start.12 = (f32[32,1,64]{2,1,0:T(1,128)}, f32[32,1,64]{2,1,0:T(1,128)S(1)}, u32[]{:S(2)}, u32[]{:S(2)}) collective-permute-start(f32[32,1,64]{2,1,0:T(1,128)} %get-tuple-element.91), channel_id=1, source_target_pairs={{0,8},{8,16},{16,24},{24,32},{32,40},{40,48},{48,56},{56,64},{64,7... | collective-permute-start | bytes 24584 | tf_op jit(solution)/shard_map/ppermute | solution.py:21
  43.7 23.0 %collective-permute-start.13 = (f32[32,1,64]{2,1,0:T(1,128)S(1)}, f32[32,1,64]{2,1,0:T(1,128)S(1)}, u32[]{:S(2)}, u32[]{:S(2)}) collective-permute-start(f32[32,1,64]{2,1,0:T(1,128)S(1)} %get-tuple-element.92), channel_id=1, source_target_pairs={{8,0},{16,8},{24,16},{32,24},{40,32},{48,40},{56,48},{64,56},{72,6... | collective-permute-start | bytes 24584 | tf_op jit(solution)/shard_map/ppermute | solution.py:22
  59.6 7.1 %collective-permute-start.7 = (f32[64,10,1]{0,1,2:T(8,128)S(1)}, f32[64,10,1]{0,1,2:T(8,128)S(1)}, u32[]{:S(2)}, u32[]{:S(2)}) collective-permute-start(f32[64,10,1]{0,1,2:T(8,128)S(1)} %get-tuple-element.57), channel_id=1, source_target_pairs={{1,0},{2,1},{3,2},{4,3},{5,4},{6,5},{7,6},{9,8},{10,9},{11,10},{12... | collective-permute-start | bytes 7688 | tf_op jit(solution)/shard_map/ppermute | solution.py:22
  69.3 12.7 %collective-permute-start.8 = (f32[64,1,128]{0,1,2:T(1,128)S(1)}, f32[64,1,128]{0,1,2:T(1,128)S(1)}, u32[]{:S(2)}, u32[]{:S(2)}) collective-permute-start(f32[64,1,128]{0,1,2:T(1,128)S(1)} %get-tuple-element.67), channel_id=1, source_target_pairs={{0,8},{8,16},{16,24},{24,32},{32,40},{40,48},{48,56},{56,64},{64,7... | collective-permute-start | bytes 98312 | tf_op jit(solution)/shard_map/ppermute | solution.py:21
  74.2 7.8 %collective-permute-start.9 = (f32[64,1,128]{0,1,2:T(1,128)S(1)}, f32[64,1,128]{0,1,2:T(1,128)S(1)}, u32[]{:S(2)}, u32[]{:S(2)}) collective-permute-start(f32[64,1,128]{0,1,2:T(1,128)S(1)} %get-tuple-element.68), channel_id=1, source_target_pairs={{8,0},{16,8},{24,16},{32,24},{40,32},{48,40},{56,48},{64,56},{72,6... | collective-permute-start | bytes 98312 | tf_op jit(solution)/shard_map/ppermute | solution.py:22
  75.6 12.6 %collective-permute-start.14 = (f32[32,6,1]{2,1,0:T(8,128)S(1)}, f32[32,6,1]{2,1,0:T(8,128)S(1)}, u32[]{:S(2)}, u32[]{:S(2)}) collective-permute-start(f32[32,6,1]{2,1,0:T(8,128)S(1)} %get-tuple-element.81), channel_id=1, source_target_pairs={{0,1},{1,2},{2,3},{3,4},{4,5},{5,6},{6,7},{8,9},{9,10},{10,11},{11... | collective-permute-start | bytes 2312 | tf_op jit(solution)/shard_map/ppermute | solution.py:21
  80.1 8.1 %collective-permute-start.15 = (f32[32,6,1]{2,1,0:T(8,128)S(1)}, f32[32,6,1]{2,1,0:T(8,128)S(1)}, u32[]{:S(2)}, u32[]{:S(2)}) collective-permute-start(f32[32,6,1]{2,1,0:T(8,128)S(1)} %get-tuple-element.82), channel_id=1, source_target_pairs={{1,0},{2,1},{3,2},{4,3},{5,4},{6,5},{7,6},{9,8},{10,9},{11,10},{12... | collective-permute-start | bytes 2312 | tf_op jit(solution)/shard_map/ppermute | solution.py:22
  82.0 7.0 %collective-permute-start.11 = (f32[64,10,1]{0,1,2:T(8,128)S(1)}, f32[64,10,1]{0,1,2:T(8,128)S(1)}, u32[]{:S(2)}, u32[]{:S(2)}) collective-permute-start(f32[64,10,1]{0,1,2:T(8,128)S(1)} %get-tuple-element.55), channel_id=1, source_target_pairs={{1,0},{2,1},{3,2},{4,3},{5,4},{6,5},{7,6},{9,8},{10,9},{11,10},{12... | collective-permute-start | bytes 7688 | tf_op jit(solution)/shard_map/ppermute | solution.py:22
  119.2 13.2 %collective-permute-start.16 = (f32[32,1,64]{2,1,0:T(1,128)S(1)}, f32[32,1,64]{2,1,0:T(1,128)S(1)}, u32[]{:S(2)}, u32[]{:S(2)}) collective-permute-start(f32[32,1,64]{2,1,0:T(1,128)S(1)} %get-tuple-element.89), channel_id=1, source_target_pairs={{0,8},{8,16},{16,24},{24,32},{32,40},{40,48},{48,56},{56,64},{64,7... | collective-permute-start | bytes 24584 | tf_op jit(solution)/shard_map/ppermute | solution.py:21
  124.3 8.1 %collective-permute-start.17 = (f32[32,1,64]{2,1,0:T(1,128)S(1)}, f32[32,1,64]{2,1,0:T(1,128)S(1)}, u32[]{:S(2)}, u32[]{:S(2)}) collective-permute-start(f32[32,1,64]{2,1,0:T(1,128)S(1)} %get-tuple-element.90), channel_id=1, source_target_pairs={{8,0},{16,8},{24,16},{32,24},{40,32},{48,40},{56,48},{64,56},{72,6... | collective-permute-start | bytes 24584 | tf_op jit(solution)/shard_map/ppermute | solution.py:22
  125.6 13.3 %collective-permute-start.24 = (f32[16,1,32]{2,0,1:T(8,128)S(1)}, f32[16,1,32]{2,0,1:T(8,128)S(1)}, u32[]{:S(2)}, u32[]{:S(2)}) collective-permute-start(f32[16,1,32]{2,0,1:T(8,128)S(1)} %get-tuple-element.112), channel_id=1, source_target_pairs={{0,8},{8,16},{16,24},{24,32},{32,40},{40,48},{48,56},{56,64},{64,7... | collective-permute-start | bytes 6152 | tf_op jit(solution)/shard_map/ppermute | solution.py:21
  131.1 7.9 %collective-permute-start.25 = (f32[16,1,32]{2,0,1:T(8,128)S(1)}, f32[16,1,32]{2,0,1:T(8,128)S(1)}, u32[]{:S(2)}, u32[]{:S(2)}) collective-permute-start(f32[16,1,32]{2,0,1:T(8,128)S(1)} %get-tuple-element.113), channel_id=1, source_target_pairs={{8,0},{16,8},{24,16},{32,24},{40,32},{48,40},{56,48},{64,56},{72,6... | collective-permute-start | bytes 6152 | tf_op jit(solution)/shard_map/ppermute | solution.py:22
  132.6 7.1 %collective-permute-start.19 = (f32[32,6,1]{2,1,0:T(8,128)S(1)}, f32[32,6,1]{2,1,0:T(8,128)S(1)}, u32[]{:S(2)}, u32[]{:S(2)}) collective-permute-start(f32[32,6,1]{2,1,0:T(8,128)S(1)} %get-tuple-element.79), channel_id=1, source_target_pairs={{1,0},{2,1},{3,2},{4,3},{5,4},{6,5},{7,6},{9,8},{10,9},{11,10},{12... | collective-permute-start | bytes 2312 | tf_op jit(solution)/shard_map/ppermute | solution.py:22
  141.6 12.2 %collective-permute-start.20 = (f32[32,1,64]{2,1,0:T(1,128)S(1)}, f32[32,1,64]{2,1,0:T(1,128)S(1)}, u32[]{:S(2)}, u32[]{:S(2)}) collective-permute-start(f32[32,1,64]{2,1,0:T(1,128)S(1)} %get-tuple-element.87), channel_id=1, source_target_pairs={{0,8},{8,16},{16,24},{24,32},{32,40},{40,48},{48,56},{56,64},{64,7... | collective-permute-start | bytes 24584 | tf_op jit(solution)/shard_map/ppermute | solution.py:21
  145.8 8.0 %collective-permute-start.21 = (f32[32,1,64]{2,1,0:T(1,128)S(1)}, f32[32,1,64]{2,1,0:T(1,128)S(1)}, u32[]{:S(2)}, u32[]{:S(2)}) collective-permute-start(f32[32,1,64]{2,1,0:T(1,128)S(1)} %get-tuple-element.88), channel_id=1, source_target_pairs={{8,0},{16,8},{24,16},{32,24},{40,32},{48,40},{56,48},{64,56},{72,6... | collective-permute-start | bytes 24584 | tf_op jit(solution)/shard_map/ppermute | solution.py:22
  147.2 12.3 %collective-permute-start.26 = (f32[16,4,1]{2,0,1:T(8,128)S(1)}, f32[16,4,1]{2,0,1:T(8,128)S(1)}, u32[]{:S(2)}, u32[]{:S(2)}) collective-permute-start(f32[16,4,1]{2,0,1:T(8,128)S(1)} %get-tuple-element.101), channel_id=1, source_target_pairs={{0,1},{1,2},{2,3},{3,4},{4,5},{5,6},{6,7},{8,9},{9,10},{10,11},{11... | collective-permute-start | bytes 776 | tf_op jit(solution)/shard_map/ppermute | solution.py:21
  151.9 7.7 %collective-permute-start.27 = (f32[16,4,1]{2,0,1:T(8,128)S(1)}, f32[16,4,1]{2,0,1:T(8,128)S(1)}, u32[]{:S(2)}, u32[]{:S(2)}) collective-permute-start(f32[16,4,1]{2,0,1:T(8,128)S(1)} %get-tuple-element.102), channel_id=1, source_target_pairs={{1,0},{2,1},{3,2},{4,3},{5,4},{6,5},{7,6},{9,8},{10,9},{11,10},{12... | collective-permute-start | bytes 776 | tf_op jit(solution)/shard_map/ppermute | solution.py:22
  168.9 12.4 %collective-permute-start.28 = (f32[16,1,32]{2,0,1:T(8,128)}, f32[16,1,32]{2,0,1:T(8,128)S(1)}, u32[]{:S(2)}, u32[]{:S(2)}) collective-permute-start(f32[16,1,32]{2,0,1:T(8,128)} %get-tuple-element.110), channel_id=1, source_target_pairs={{0,8},{8,16},{16,24},{24,32},{32,40},{40,48},{48,56},{56,64},{64,7... | collective-permute-start | bytes 6152 | tf_op jit(solution)/shard_map/ppermute | solution.py:21
  173.2 8.2 %collective-permute-start.29 = (f32[16,1,32]{2,0,1:T(8,128)S(1)}, f32[16,1,32]{2,0,1:T(8,128)S(1)}, u32[]{:S(2)}, u32[]{:S(2)}) collective-permute-start(f32[16,1,32]{2,0,1:T(8,128)S(1)} %get-tuple-element.111), channel_id=1, source_target_pairs={{8,0},{16,8},{24,16},{32,24},{40,32},{48,40},{56,48},{64,56},{72,6... | collective-permute-start | bytes 6152 | tf_op jit(solution)/shard_map/ppermute | solution.py:22
  174.7 13.6 %collective-permute-start.37 = (f32[8,1,16]{2,0,1:T(8,128)S(1)}, f32[8,1,16]{2,0,1:T(8,128)S(1)}, u32[]{:S(2)}, u32[]{:S(2)}) collective-permute-start(f32[8,1,16]{2,0,1:T(8,128)S(1)} %multiply_bitcast_fusion), channel_id=1, source_target_pairs={{8,0},{16,8},{24,16},{32,24},{40,32},{48,40},{56,48},{64,56},{72,6... | collective-permute-start | bytes 1544 | tf_op jit(solution)/shard_map/ppermute | solution.py:22
  176.0 12.3 %collective-permute-start.36 = (f32[8,1,16]{2,0,1:T(8,128)S(1)}, f32[8,1,16]{2,0,1:T(8,128)S(1)}, u32[]{:S(2)}, u32[]{:S(2)}) collective-permute-start(f32[8,1,16]{2,0,1:T(8,128)S(1)} %multiply_bitcast_fusion), channel_id=1, source_target_pairs={{0,8},{8,16},{16,24},{24,32},{32,40},{40,48},{48,56},{56,64},{64,7... | collective-permute-start | bytes 1544 | tf_op jit(solution)/shard_map/ppermute | solution.py:21
  190.3 12.7 %collective-permute-start.32 = (f32[16,1,32]{2,0,1:T(8,128)S(1)}, f32[16,1,32]{2,0,1:T(8,128)S(1)}, u32[]{:S(2)}, u32[]{:S(2)}) collective-permute-start(f32[16,1,32]{2,0,1:T(8,128)S(1)} %get-tuple-element.108), channel_id=1, source_target_pairs={{0,8},{8,16},{16,24},{24,32},{32,40},{40,48},{48,56},{56,64},{64,7... | collective-permute-start | bytes 6152 | tf_op jit(solution)/shard_map/ppermute | solution.py:21
  195.1 7.8 %collective-permute-start.33 = (f32[16,1,32]{2,0,1:T(8,128)S(1)}, f32[16,1,32]{2,0,1:T(8,128)S(1)}, u32[]{:S(2)}, u32[]{:S(2)}) collective-permute-start(f32[16,1,32]{2,0,1:T(8,128)S(1)} %get-tuple-element.109), channel_id=1, source_target_pairs={{8,0},{16,8},{24,16},{32,24},{40,32},{48,40},{56,48},{64,56},{72,6... | collective-permute-start | bytes 6152 | tf_op jit(solution)/shard_map/ppermute | solution.py:22
  196.5 12.1 %collective-permute-start.38 = (f32[8,3,1]{2,0,1:T(8,128)S(1)}, f32[8,3,1]{2,0,1:T(8,128)S(1)}, u32[]{:S(2)}, u32[]{:S(2)}) collective-permute-start(f32[8,3,1]{2,0,1:T(8,128)S(1)} %get-tuple-element.128), channel_id=1, source_target_pairs={{0,1},{1,2},{2,3},{3,4},{4,5},{5,6},{6,7},{8,9},{9,10},{10,11},{11... | collective-permute-start | bytes 296 | tf_op jit(solution)/shard_map/ppermute | solution.py:21
  201.0 7.6 %collective-permute-start.39 = (f32[8,3,1]{2,0,1:T(8,128)S(1)}, f32[8,3,1]{2,0,1:T(8,128)S(1)}, u32[]{:S(2)}, u32[]{:S(2)}) collective-permute-start(f32[8,3,1]{2,0,1:T(8,128)S(1)} %get-tuple-element.129), channel_id=1, source_target_pairs={{1,0},{2,1},{3,2},{4,3},{5,4},{6,5},{7,6},{9,8},{10,9},{11,10},{12... | collective-permute-start | bytes 296 | tf_op jit(solution)/shard_map/ppermute | solution.py:22
  212.2 7.4 %collective-permute-start.41 = (f32[8,1,16]{2,0,1:T(8,128)S(1)}, f32[8,1,16]{2,0,1:T(8,128)S(1)}, u32[]{:S(2)}, u32[]{:S(2)}) collective-permute-start(f32[8,1,16]{2,0,1:T(8,128)S(1)} %get-tuple-element.28), channel_id=1, source_target_pairs={{8,0},{16,8},{24,16},{32,24},{40,32},{48,40},{56,48},{64,56},{72,6... | collective-permute-start | bytes 1544 | tf_op jit(solution)/shard_map/ppermute | solution.py:22
  273.9 7.1 %collective-permute-start.57 = (f32[8,1,16]{2,0,1:T(8,128)S(1)}, f32[8,1,16]{2,0,1:T(8,128)S(1)}, u32[]{:S(2)}, u32[]{:S(2)}) collective-permute-start(f32[8,1,16]{2,0,1:T(8,128)S(1)} %get-tuple-element.20), channel_id=1, source_target_pairs={{8,0},{16,8},{24,16},{32,24},{40,32},{48,40},{56,48},{64,56},{72,6... | collective-permute-start | bytes 1544 | tf_op jit(solution)/shard_map/ppermute | solution.py:22
  281.8 7.2 %collective-permute-start.59 = (f32[8,3,1]{2,0,1:T(8,128)S(1)}, f32[8,3,1]{2,0,1:T(8,128)S(1)}, u32[]{:S(2)}, u32[]{:S(2)}) collective-permute-start(f32[8,3,1]{2,0,1:T(8,128)S(1)} %get-tuple-element.118), channel_id=1, source_target_pairs={{1,0},{2,1},{3,2},{4,3},{5,4},{6,5},{7,6},{9,8},{10,9},{11,10},{12... | collective-permute-start | bytes 296 | tf_op jit(solution)/shard_map/ppermute | solution.py:22
  290.0 7.1 %collective-permute-start.61 = (f32[8,1,16]{2,0,1:T(8,128)S(1)}, f32[8,1,16]{2,0,1:T(8,128)S(1)}, u32[]{:S(2)}, u32[]{:S(2)}) collective-permute-start(f32[8,1,16]{2,0,1:T(8,128)S(1)} %get-tuple-element.18), channel_id=1, source_target_pairs={{8,0},{16,8},{24,16},{32,24},{40,32},{48,40},{56,48},{64,56},{72,6... | collective-permute-start | bytes 1544 | tf_op jit(solution)/shard_map/ppermute | solution.py:22
  305.8 7.1 %collective-permute-start.65 = (f32[8,1,16]{2,0,1:T(8,128)S(1)}, f32[8,1,16]{2,0,1:T(8,128)S(1)}, u32[]{:S(2)}, u32[]{:S(2)}) collective-permute-start(f32[8,1,16]{2,0,1:T(8,128)S(1)} %get-tuple-element.16), channel_id=1, source_target_pairs={{8,0},{16,8},{24,16},{32,24},{40,32},{48,40},{56,48},{64,56},{72,6... | collective-permute-start | bytes 1544 | tf_op jit(solution)/shard_map/ppermute | solution.py:22
  333.2 7.3 %collective-permute-start.71 = (f32[16,4,1]{2,0,1:T(8,128)S(1)}, f32[16,4,1]{2,0,1:T(8,128)S(1)}, u32[]{:S(2)}, u32[]{:S(2)}) collective-permute-start(f32[16,4,1]{2,0,1:T(8,128)S(1)} %get-tuple-element.95), channel_id=1, source_target_pairs={{1,0},{2,1},{3,2},{4,3},{5,4},{6,5},{7,6},{9,8},{10,9},{11,10},{12... | collective-permute-start | bytes 776 | tf_op jit(solution)/shard_map/ppermute | solution.py:22
  353.1 7.3 %collective-permute-start.75 = (f32[16,4,1]{2,0,1:T(8,128)S(1)}, f32[16,4,1]{2,0,1:T(8,128)S(1)}, u32[]{:S(2)}, u32[]{:S(2)}) collective-permute-start(f32[16,4,1]{2,0,1:T(8,128)S(1)} %get-tuple-element.93), channel_id=1, source_target_pairs={{1,0},{2,1},{3,2},{4,3},{5,4},{6,5},{7,6},{9,8},{10,9},{11,10},{12... | collective-permute-start | bytes 776 | tf_op jit(solution)/shard_map/ppermute | solution.py:22
  361.9 7.3 %collective-permute-start.76 = (f32[32,1,64]{2,1,0:T(1,128)S(1)}, f32[32,1,64]{2,1,0:T(1,128)S(1)}, u32[]{:S(2)}, u32[]{:S(2)}) collective-permute-start(f32[32,1,64]{2,1,0:T(1,128)S(1)} %get-tuple-element.85), channel_id=1, source_target_pairs={{0,8},{8,16},{16,24},{24,32},{32,40},{40,48},{48,56},{56,64},{64,7... | collective-permute-start | bytes 24584 | tf_op jit(solution)/shard_map/ppermute | solution.py:21
  367.9 7.1 %collective-permute-start.77 = (f32[32,1,64]{2,1,0:T(1,128)S(1)}, f32[32,1,64]{2,1,0:T(1,128)S(1)}, u32[]{:S(2)}, u32[]{:S(2)}) collective-permute-start(f32[32,1,64]{2,1,0:T(1,128)S(1)} %get-tuple-element.86), channel_id=1, source_target_pairs={{8,0},{16,8},{24,16},{32,24},{40,32},{48,40},{56,48},{64,56},{72,6... | collective-permute-start | bytes 24584 | tf_op jit(solution)/shard_map/ppermute | solution.py:22
  375.2 8.0 %collective-permute-start.79 = (f32[32,6,1]{2,1,0:T(8,128)S(1)}, f32[32,6,1]{2,1,0:T(8,128)S(1)}, u32[]{:S(2)}, u32[]{:S(2)}) collective-permute-start(f32[32,6,1]{2,1,0:T(8,128)S(1)} %get-tuple-element.75), channel_id=1, source_target_pairs={{1,0},{2,1},{3,2},{4,3},{5,4},{6,5},{7,6},{9,8},{10,9},{11,10},{12... | collective-permute-start | bytes 2312 | tf_op jit(solution)/shard_map/ppermute | solution.py:22
  377.1 7.3 %collective-permute-start.78 = (f32[32,6,1]{2,1,0:T(8,128)S(1)}, f32[32,6,1]{2,1,0:T(8,128)S(1)}, u32[]{:S(2)}, u32[]{:S(2)}) collective-permute-start(f32[32,6,1]{2,1,0:T(8,128)S(1)} %get-tuple-element.76), channel_id=1, source_target_pairs={{0,1},{1,2},{2,3},{3,4},{4,5},{5,6},{6,7},{8,9},{9,10},{10,11},{11... | collective-permute-start | bytes 2312 | tf_op jit(solution)/shard_map/ppermute | solution.py:21
  385.1 7.3 %collective-permute-start.80 = (f32[32,1,64]{2,1,0:T(1,128)S(1)}, f32[32,1,64]{2,1,0:T(1,128)S(1)}, u32[]{:S(2)}, u32[]{:S(2)}) collective-permute-start(f32[32,1,64]{2,1,0:T(1,128)S(1)} %get-tuple-element.83), channel_id=1, source_target_pairs={{0,8},{8,16},{16,24},{24,32},{32,40},{40,48},{48,56},{56,64},{64,7... | collective-permute-start | bytes 24584 | tf_op jit(solution)/shard_map/ppermute | solution.py:21
  391.1 7.1 %collective-permute-start.81 = (f32[32,1,64]{2,1,0:T(1,128)S(1)}, f32[32,1,64]{2,1,0:T(1,128)S(1)}, u32[]{:S(2)}, u32[]{:S(2)}) collective-permute-start(f32[32,1,64]{2,1,0:T(1,128)S(1)} %get-tuple-element.84), channel_id=1, source_target_pairs={{8,0},{16,8},{24,16},{32,24},{40,32},{48,40},{56,48},{64,56},{72,6... | collective-permute-start | bytes 24584 | tf_op jit(solution)/shard_map/ppermute | solution.py:22
  398.4 8.1 %collective-permute-start.83 = (f32[32,6,1]{2,1,0:T(8,128)S(1)}, f32[32,6,1]{2,1,0:T(8,128)S(1)}, u32[]{:S(2)}, u32[]{:S(2)}) collective-permute-start(f32[32,6,1]{2,1,0:T(8,128)S(1)} %get-tuple-element.73), channel_id=1, source_target_pairs={{1,0},{2,1},{3,2},{4,3},{5,4},{6,5},{7,6},{9,8},{10,9},{11,10},{12... | collective-permute-start | bytes 2312 | tf_op jit(solution)/shard_map/ppermute | solution.py:22
  400.4 7.4 %collective-permute-start.82 = (f32[32,6,1]{2,1,0:T(8,128)S(1)}, f32[32,6,1]{2,1,0:T(8,128)S(1)}, u32[]{:S(2)}, u32[]{:S(2)}) collective-permute-start(f32[32,6,1]{2,1,0:T(8,128)S(1)} %get-tuple-element.74), channel_id=1, source_target_pairs={{0,1},{1,2},{2,3},{3,4},{4,5},{5,6},{6,7},{8,9},{9,10},{10,11},{11... | collective-permute-start | bytes 2312 | tf_op jit(solution)/shard_map/ppermute | solution.py:21
  408.9 7.1 %collective-permute-start.84 = (f32[64,1,128]{0,1,2:T(1,128)S(1)}, f32[64,1,128]{0,1,2:T(1,128)S(1)}, u32[]{:S(2)}, u32[]{:S(2)}) collective-permute-start(f32[64,1,128]{0,1,2:T(1,128)S(1)} %get-tuple-element.65), channel_id=1, source_target_pairs={{0,8},{8,16},{16,24},{24,32},{32,40},{40,48},{48,56},{56,64},{64,7... | collective-permute-start | bytes 98312 | tf_op jit(solution)/shard_map/ppermute | solution.py:21
  420.0 7.4 %collective-permute-start.87 = (f32[64,10,1]{0,1,2:T(8,128)S(1)}, f32[64,10,1]{0,1,2:T(8,128)S(1)}, u32[]{:S(2)}, u32[]{:S(2)}) collective-permute-start(f32[64,10,1]{0,1,2:T(8,128)S(1)} %get-tuple-element.53), channel_id=1, source_target_pairs={{1,0},{2,1},{3,2},{4,3},{5,4},{6,5},{7,6},{9,8},{10,9},{11,10},{12... | collective-permute-start | bytes 7688 | tf_op jit(solution)/shard_map/ppermute | solution.py:22
  440.3 7.3 %collective-permute-start.91 = (f32[64,10,1]{0,1,2:T(8,128)S(1)}, f32[64,10,1]{0,1,2:T(8,128)S(1)}, u32[]{:S(2)}, u32[]{:S(2)}) collective-permute-start(f32[64,10,1]{0,1,2:T(8,128)S(1)} %get-tuple-element.51), channel_id=1, source_target_pairs={{1,0},{2,1},{3,2},{4,3},{5,4},{6,5},{7,6},{9,8},{10,9},{11,10},{12... | collective-permute-start | bytes 7688 | tf_op jit(solution)/shard_map/ppermute | solution.py:22
  459.3 8.2 %collective-permute-start.95 = (f32[64,10,1]{0,1,2:T(8,128)S(1)}, f32[64,10,1]{0,1,2:T(8,128)S(1)}, u32[]{:S(2)}, u32[]{:S(2)}) collective-permute-start(f32[64,10,1]{0,1,2:T(8,128)S(1)} %get-tuple-element.49), channel_id=1, source_target_pairs={{1,0},{2,1},{3,2},{4,3},{5,4},{6,5},{7,6},{9,8},{10,9},{11,10},{12... | collective-permute-start | bytes 7688 | tf_op jit(solution)/shard_map/ppermute | solution.py:22
  (64 other events, 432.8 us)
where the time goes:
time: 476 us; the launch traced here: 470 us
  starting transfers between devices  316 us (66%)
  waiting for transfers between devices  61.4 us (13%)
  local copies, waits for them, and re-layouts  51.7 us (11%)
  other arithmetic  38.6 us (8%)
    ppermute x48, starting transfers between devices, extended(): before = lax.ppermute(last, axis, up)  239 us
    ppermute x48, starting transfers between devices, extended(): after = lax.ppermute(initial, axis, down)  77.2 us
    ppermute x48, waiting for transfers between devices, extended(): after = lax.ppermute(initial, axis, down)  40.5 us
    reshape x3, local copies, waits for them, and re-layouts, coarsen(): blocks = field.reshape(shape[0] // 2, 2, shape[1] // 2, 2, shape[2] // 2, 2)  40.4 us
    ppermute x48, waiting for transfers between devices, extended(): before = lax.ppermute(last, axis, up)  20.9 us
    reduce_sum x7, other arithmetic, coarsen(): return jnp.mean(blocks, axis=(1, 3, 5))  16.9 us
  transfers between devices with their start and end apart: 96, of which 36 were waited for; matrix products, arithmetic and copies ran while one was open for 7% of the time, Pallas kernels for 0%

commit v1 on v0

v1 whole, which is shorter than its diff:
```python
import functools

import jax
import jax.numpy as jnp
from jax import lax
from jax.experimental import pallas as pl
from jax.experimental.pallas import tpu as pltpu
from jax.sharding import PartitionSpec as P

F32 = jnp.float32
COARSE = 8
LOW_BOUND = 0.3
HIGH_BOUND = 2.0
COARSE_LOW = 0.02
VMEM_LIMIT = 48 * 1024 * 1024

KX, BX, KY, BY = 5, 4, 13, 12


def pairs(size, offset):
    found = []
    for i in range(offset, size - 1, 2):
        found += [(i, i + 1), (i + 1, i)]
    return found


def swap(value, axis, offset):
    return lax.ppermute(value, axis, pairs(lax.axis_size(axis), offset))


def chebyshev(sweeps, lower):
    middle = (HIGH_BOUND + lower) / 2
    half_width = (HIGH_BOUND - lower) / 2
    ratio = middle / half_width
    rho = 1 / ratio
    steps = []
    for _ in range(sweeps - 1):
        rho_next = 1 / (2 * ratio - rho)
        steps.append((rho_next * rho, 2 * rho_next / half_width))
        rho = rho_next
    return middle, steps


def iota(shape, axis):
    return lax.broadcasted_iota(jnp.int32, shape, axis)


def dot(a, b):
    return jnp.dot(a, b, preferred_element_type=F32, precision=lax.Precision.HIGHEST)


def coarsen_matrix(fine, coarse, right, left, scale):
    f, c = iota((fine, coarse), 0), iota((fine, coarse), 1)
    ahead = (f < right) & (c == lax.shift_right_logical(f, 1))
    behind = (f >= fine - left) & (coarse - c == lax.shift_right_logical(fine - f + 1, 1))
    return jnp.where(ahead | behind, scale, 0.0).astype(F32)


def refine_matrix(coarse, fine, right, left):
    c, f = iota((coarse, fine), 0), iota((coarse, fine), 1)
    ahead = (f < right) & (c == lax.shift_right_logical(f, 1))
    behind = (f >= fine - left) & (coarse - c == lax.shift_right_logical(fine - f + 1, 1))
    return jnp.where(ahead | behind, 1.0, 0.0).astype(F32)


def turn(value, shift, axis):
    shift = shift % value.shape[axis]
    return value if shift == 0 else pltpu.roll(value, shift, axis=axis)


def weights_row(kc, km, kp, factor):
    half = 0.5 * factor
    axis = kc.ndim - 2
    depth = kc.shape[axis]
    z = iota(kc.shape, axis)
    low, top = z == 0, z == depth - 1
    up = half * (kc + jnp.where(top, 0.0, turn(kc, -1, axis)))
    down = half * (kc + jnp.where(low, 0.0, turn(kc, 1, axis)))
    ahead = half * (kc + turn(kc, -1, axis + 1))
    behind = half * (kc + turn(kc, 1, axis + 1))
    right = half * (kc + kp)
    left = half * (kc + km)
    diagonal = up + down + ahead + behind + right + left
    inverse = jnp.where(kc > 0, 1.0 / diagonal, 0.0)
    up = jnp.where(top, 0.0, up)
    down = jnp.where(low, 0.0, down)
    weights = [w * inverse for w in (left, right, behind, ahead, down, up)]
    return weights, inverse, diagonal


def neighbour_sum(weights, below, centre, above):
    axis = centre.ndim - 2
    left, right, behind, ahead, down, up = weights
    total = left * below + right * above
    total = total + behind * turn(centre, 1, axis + 1) + ahead * turn(centre, -1, axis + 1)
    return total + down * turn(centre, 1, axis) + up * turn(centre, -1, axis)


class Level:
    def __init__(self, k, weights, bh, x, p, factor):
        self.k, self.weights, self.bh, self.x, self.p, self.factor = k, weights, bh, x, p, factor

    def rows(self, low, high, body):
        def step(q, carry):
            body(q)
            return carry

        lax.fori_loop(low, high, step, 0)

    def set_up(self, low, high, b, diagonal=None):
        def body(q):
            weights, inverse, diag = weights_row(self.k[q], self.k[q - 1], self.k[q + 1], self.factor)
            for n in range(6):
                self.weights[n, q] = weights[n]
            self.bh[q] = b[q] * inverse
            if diagonal is not None:
                diagonal[q] = diag

        self.rows(low, high, body)

    def total(self, x, q):
        return neighbour_sum([self.weights[n, q] for n in range(6)], x[q - 1], x[q], x[q + 1])

    def pre(self, low, high):
        middle, ((c1, c2),) = chebyshev(2, LOW_BOUND)

        def body(q):
            first = self.bh[q]
            self.x[q] = (1 / middle) * (1 + c1 - c2 + c2 * middle) * first + (c2 / middle) * self.total(self.bh, q)

        self.rows(low, high, body)

    def post(self, low, high, out):
        middle, ((c1, c2),) = chebyshev(2, LOW_BOUND)

        def first(q):
            update = (self.bh[q] - self.x[q] + self.total(self.x, q)) * (1 / middle)
            self.p[q] = update
            out[q] = self.x[q] + update

        def second(q):
            residue = self.bh[q] - out[q] + self.total(out, q)
            self.x[q] = out[q] + c1 * self.p[q] + c2 * residue

        self.rows(low - 1, high + 1, first)
        self.rows(low, high, second)


def spec(n):
    return [pl.BlockSpec(memory_space=pltpu.VMEM)] * n


def call(body, outs, scratch, *args):
    return pl.pallas_call(
        body,
        out_shape=[jax.ShapeDtypeStruct(s, F32) for s in outs],
        in_specs=spec(len(args)),
        out_specs=spec(len(outs)),
        scratch_shapes=[pltpu.VMEM(s, F32) for s in scratch],
        compiler_params=pltpu.CompilerParams(vmem_limit_bytes=VMEM_LIMIT),
    )(*args)


def odd(axis):
    return lax.rem(lax.axis_index(axis), 2) == 1


def pack_kernel(b_ref, k_ref, ya, yb, xa, xb):
    odd_x, odd_y = odd("gx"), odd("gy")
    lane = iota((64, 128), 1)
    for n, (ref, width) in enumerate(((k_ref, KY), (b_ref, BY))):
        first, last = jnp.zeros((64, 128), F32), jnp.zeros((64, 128), F32)
        for i in range(8):
            plane = ref[pl.ds(i, 64, stride=8), :]
            here = (lane >= 16 * i) & (lane < 16 * i + width)
            first = jnp.where(here, turn(plane, 16 * i, 1), first)
            last = jnp.where(here, turn(plane, 16 * i + width, 1), last)
        ya[n] = jnp.where(odd_y, first, last)
        yb[n] = jnp.where(odd_y, last, first)
    at = 0
    for ref, width in ((k_ref, KX), (b_ref, BX)):
        for i in range(width):
            first = ref[pl.ds(i, 64, stride=8), :]
            last = ref[pl.ds(8 - width + i, 64, stride=8), :]
            xa[at] = jnp.where(odd_x, first, last)
            xb[at] = jnp.where(odd_x, last, first)
            at += 1


def assemble(strips, n, width, i, lane):
    left, right = strips
    right_part = turn(right[n], -16 * i, 1)
    left_part = turn(left[n], 128 - width - 16 * i, 1)
    return jnp.where(lane < width, right_part, jnp.where(lane >= 128 - width, left_part, 0.0))


def first_kernel(b_ref, k_ref, xa, xb, ya, yb, k_out, b_out, x_out, k1_out, b1_out, sa, sb, weights, bh, diagonal, wide, thin):
    odd_x, odd_y = odd("gx"), odd("gy")
    lane = iota((64, 128), 1)

    def by_y(a, b):
        return jnp.where(odd_y, a, b), jnp.where(odd_y, b, a)

    def fill(out, n, q, plane, strips, i, width):
        out[q, :, 0:128] = plane
        out[q, :, 128:256] = assemble(strips, n, width, i, lane)

    own = [by_y(ya[n], yb[n]) for n in range(2)]
    own = ([own[0][0], own[1][0]], [own[0][1], own[1][1]])
    for i in range(8):
        fill(k_out, 0, i + 5, k_ref[pl.ds(i, 64, stride=8), :], own, i, KY)
        fill(b_out, 1, i + 5, b_ref[pl.ds(i, 64, stride=8), :], own, i, BY)
    for side in range(2):

        def pick(n):
            a, b = xa[n], xb[n]
            return jnp.where(odd_x, a, b) if side == 0 else jnp.where(odd_x, b, a)

        strips = [by_y(pick(9 + n), pick(11 + n)) for n in range(2)]
        strips = ([strips[0][0], strips[1][0]], [strips[0][1], strips[1][1]])
        for j in range(KX):
            fill(k_out, 0, j if side == 0 else 13 + j, pick(j), strips, 3 + j if side == 0 else j, KY)
        for j in range(BX):
            fill(b_out, 1, 1 + j if side == 0 else 13 + j, pick(KX + j), strips, 4 + j if side == 0 else j, BY)

    level = Level(k_out, weights, bh, x_out, None, 1.0)
    level.set_up(1, 17, b_out, diagonal)
    level.pre(2, 16)

    def residue(q):
        return diagonal[q] * (bh[q] - x_out[q] + level.total(x_out, q))

    def pair(m, carry):
        wide[m] = residue(2 * m + 3) + residue(2 * m + 4)
        return carry

    lax.fori_loop(0, 6, pair, 0)
    for m in range(8):
        wide[6 + m] = k_out[2 * m + 1] + k_out[2 * m + 2]
    matrix = coarsen_matrix(256, 128, 140, 12, 0.125)
    flat = dot(wide[...].reshape(14 * 64, 256), matrix)
    thin[...] = flat
    done = []
    for m in range(14):
        done.append(thin[pl.ds(64 * m, 32, stride=2), :] + thin[pl.ds(64 * m + 1, 32, stride=2), :])
    for m in range(6):
        b1_out[m] = done[m]
    for m in range(8):
        k1_out[m] = done[6 + m]
    for m in range(5):
        sa[m] = jnp.where(odd_x, done[m + 1], done[m])
        sb[m] = jnp.where(odd_x, done[m], done[m + 1])
    for m in range(6):
        sa[5 + m] = jnp.where(odd_x, done[8 + m], done[6 + m])
        sb[5 + m] = jnp.where(odd_x, done[6 + m], done[8 + m])


def second_kernel(count, b1, k1, ra, rb, k_out, b_out, x_out, g_out, weights, bh, diagonal, thin):
    odd_x = odd("gx")
    for side in range(2):

        def pick(n):
            a, b = ra[n], rb[n]
            return jnp.where(odd_x, a, b) if side == 0 else jnp.where(odd_x, b, a)

        for j in range(6):
            k_out[j if side == 0 else 10 + j] = pick(5 + j)
        for j in range(5):
            b_out[1 + j if side == 0 else 10 + j] = pick(j)
    for j in range(4):
        k_out[6 + j] = k1[2 + j]
        b_out[6 + j] = b1[1 + j]

    level = Level(k_out, weights, bh, x_out, None, 0.25)
    level.set_up(1, 15, b_out, diagonal)
    level.pre(2, 14)

    def residue(q):
        return diagonal[q] * (bh[q] - x_out[q] + level.total(x_out, q))

    parts = [residue(6) + residue(7), residue(8) + residue(9), k_out[6] + k_out[7], k_out[8] + k_out[9]]
    matrix = coarsen_matrix(128, 128, 64, 0, 0.125)
    thin[...] = dot(jnp.concatenate(parts, axis=0), matrix)
    payload = jnp.zeros((16, 128), F32)
    for n in range(4):
        part = thin[pl.ds(32 * n, 16, stride=2), :] + thin[pl.ds(32 * n + 1, 16, stride=2), :]
        payload = payload + turn(part, 32 * n, 1)
    for n in range(count):
        g_out[n] = payload


def last_kernel(
    count, g, ga, gb, k1, b1, x1_in, k0, b0, x0_in, pressure, residual,
    k2, b2, w2, bh2, x2, y2, p2, fine2, coarse2, w1, bh1, x1, y1, p1, stack1, w0, bh0, d0, x0, y0, p0, stack0,
):
    odd_y = odd("gy")
    me = lax.axis_index("gx")
    lane = iota((16, 128), 1)

    def window(j, carry):
        device = me - 11 + j
        inside = (device >= 0) & (device < count)
        at = jnp.clip(device, 0, count - 1)
        own, a, b = g[at], ga[at], gb[at]
        left, right = jnp.where(odd_y, a, b), jnp.where(odd_y, b, a)
        for n, out in ((0, b2), (2, k2)):
            for m in range(2):
                s = -32 * (n + m)
                value = jnp.where(lane < 32, turn(own, s, 1), jnp.where(lane < 64, turn(right, s + 32, 1), jnp.where(lane >= 96, turn(left, s + 96, 1), 0.0)))
                out[2 * j + m] = jnp.where(inside, value, 0.0)
        return carry

    lax.fori_loop(0, 23, window, 0)
    level = Level(k2, w2, bh2, x2, p2, 0.0625)
    level.set_up(1, 45, b2, y2)
    level.pre(2, 44)

    def residue(q):
        return y2[q] * (bh2[q] - x2[q] + level.total(x2, q))

    def pair(m, carry):
        fine2[m] = residue(2 * m) + residue(2 * m + 1)
        return carry

    lax.fori_loop(2, 21, pair, 0)
    zero = jnp.zeros((16, 128), F32)
    for m in (0, 1, 21, 22):
        fine2[m] = zero
    for m in range(23):
        fine2[23 + m] = k2[2 * m] + k2[2 * m + 1]
    coarse2[...] = dot(fine2[...].reshape(46 * 16, 128), coarsen_matrix(128, 128, 64, 32, 0.125))
    both = coarse2[pl.ds(0, 46 * 8, stride=2), :] + coarse2[pl.ds(1, 46 * 8, stride=2), :]
    both = both.reshape(46, 8, 128)
    b3, k3 = both[:23], both[23:]
    none = jnp.zeros((1, 8, 128), F32)

    def after(value):
        return jnp.concatenate([value[1:], none], axis=0)

    def before(value):
        return jnp.concatenate([none, value[:-1]], axis=0)

    w3, inverse, _ = weights_row(k3, before(k3), after(k3), 0.015625)
    middle, steps = chebyshev(COARSE, COARSE_LOW)
    source = b3 * inverse
    update = source * (1 / middle)
    e3 = update
    for c1, c2 in steps:
        update = c1 * update + c2 * (source - e3 + neighbour_sum(w3, before(e3), e3, after(e3)))
        e3 = e3 + update

    tall = coarse2
    for m in range(5):
        for half in range(2):
            tall[pl.ds(16 * m + half, 8, stride=2), :] = e3[9 + m]
    fine = dot(tall[0 : 5 * 16, :], refine_matrix(128, 128, 64, 32))
    for m in range(10):
        part = fine[16 * (m // 2) : 16 * (m // 2) + 16]
        x2[18 + m] = x2[18 + m] + part
    level.post(20, 26, y2)

    for m in range(6):
        for half in range(2):
            stack1[pl.ds(32 * m + half, 16, stride=2), :] = x2[20 + m]
    fine = dot(stack1[...], refine_matrix(128, 128, 70, 6))
    for m in range(12):
        x1[2 + m] = x1_in[2 + m] + fine[32 * (m // 2) : 32 * (m // 2) + 32]
    level = Level(k1, w1, bh1, x1, p1, 0.25)
    level.set_up(3, 13, b1)
    level.post(4, 12, y1)

    for m in range(8):
        for half in range(2):
            stack0[pl.ds(64 * m + half, 32, stride=2), :] = x1[4 + m]
    matrix = refine_matrix(128, 256, 140, 12)
    fine = dot(stack0[...], matrix)
    for m in range(14):
        row = (m + 1) // 2
        x0[2 + m] = x0_in[2 + m] + fine[64 * row : 64 * row + 64]
    level = Level(k0, w0, bh0, x0, p0, 1.0)
    level.set_up(3, 15, b0, d0)
    level.post(4, 14, y0)
    for i in range(8):
        q = 5 + i
        value = x0[q]
        left = d0[q] * (bh0[q] - value + level.total(x0, q))
        pressure[pl.ds(i, 64, stride=8), :] = value[:, 0:128]
        residual[pl.ds(i, 64, stride=8), :] = left[:, 0:128]


def on_device(right_side, conductivity):
    count = lax.axis_size("gx")
    b, k = right_side.reshape(512, 128), conductivity.reshape(512, 128)
    ya, yb, xa, xb = call(pack_kernel, [(2, 64, 128)] * 2 + [(13, 64, 128)] * 2, [], b, k)
    ya, yb = swap(ya, "gy", 0), swap(yb, "gy", 1)

    def with_y(strip):
        strip = lax.dynamic_update_slice(strip, ya, (9, 0, 0))
        return lax.dynamic_update_slice(strip, yb, (11, 0, 0))

    xa, xb = swap(with_y(xa), "gx", 0), swap(with_y(xb), "gx", 1)
    rows0, rows1 = (18, 64, 256), (16, 32, 128)
    k0, b0, x0, k1, b1, sa, sb = call(
        first_kernel,
        [rows0, rows0, rows0, (8, 32, 128), (6, 32, 128), (11, 32, 128), (11, 32, 128)],
        [(6,) + rows0, rows0, rows0, (14, 64, 256), (14 * 64, 128)],
        b, k, xa, xb, ya, yb,
    )
    ra, rb = swap(sa, "gx", 0), swap(sb, "gx", 1)
    k1, b1, x1, g = call(
        functools.partial(second_kernel, count),
        [rows1, rows1, rows1, (count, 16, 128)],
        [(6,) + rows1, rows1, rows1, (128, 128)],
        b1, k1, ra, rb,
    )
    g = lax.all_to_all(g, "gx", 0, 0, tiled=True)
    ga, gb = swap(g, "gy", 0), swap(g, "gy", 1)
    rows2 = (46, 16, 128)
    pressure, residual = call(
        functools.partial(last_kernel, count),
        [(512, 128)] * 2,
        [rows2, rows2, (6,) + rows2, rows2, rows2, rows2, rows2, (46, 16, 128), (46 * 16, 128)]
        + [(6,) + rows1, rows1, rows1, rows1, rows1, (6 * 32, 128)]
        + [(6,) + rows0, rows0, rows0, rows0, rows0, rows0, (8 * 64, 128)],
        g, ga, gb, k1, b1, x1, k0, b0, x0,
    )
    return pressure.reshape(64, 8, 128), residual.reshape(64, 8, 128)


def solution(mesh):
    place = P(None, "gx", "gy")
    return jax.shard_map(
        on_device, mesh=mesh, in_specs=(place, place), out_specs=(place, place), check_vma=False
    )
```

time: 476 us -> 97 us (0.20); the launches traced: 470 us -> 96.8 us
  starting transfers between devices: 316 us -> 20.9 us
  local copies, waits for them, and re-layouts: 51.7 us -> 1.91 us
  waiting for transfers between devices: 61.4 us -> 16 us
  other arithmetic: 38.6 us -> 0 us
  Pallas kernels: 0 us -> 32.2 us
  blocking collectives: 0 us -> 25 us
    ppermute x96 -> x8, starting transfers between devices: 316 us -> 20.9 us  [swap(): return lax.ppermute(value, axis, pairs(lax.axis_size(axis), offset))]
    ppermute x96 -> x8, waiting for transfers between devices: 61.4 us -> 16 us  [swap(): return lax.ppermute(value, axis, pairs(lax.axis_size(axis), offset))]
    reshape x6 -> x0, local copies, waits for them, and re-layouts: 40.7 us -> none  [the longest x3 40.4 us: coarsen(): blocks = field.reshape(shape[0] // 2, 2, shape[1] // 2, 2, shape[2] // 2, 2)]
    pallas_call x0 -> x4, Pallas kernels: none -> 32.2 us  [call(): pl.pallas_call(body, out_shape=[jax.ShapeDtypeStruct(s, F32) for s in out...]
    all_to_all x0 -> x1, blocking collectives: none -> 25 us  [on_device(): g = lax.all_to_all(g, 'gx', 0, 0, tiled=True)]
    reduce_sum x7 -> x0, other arithmetic: 16.9 us -> none  [coarsen(): return jnp.mean(blocks, axis=(1, 3, 5))]
    concatenate x47 -> x0, other arithmetic: 8.17 us -> none  [extended(): value = jnp.concatenate([before, value, after], axis=dim)]
    add x19 -> x0, other arithmetic: 6.84 us -> none  [the longest x13 4.98 us: smooth(): iterate = iterate + update]
  transfers between devices with their start and end apart: 96 -> 8, of which waited for: 36 -> 4; matrix products, arithmetic and copies ran while one was open for 7% -> 0% of each run, Pallas kernels for 0% -> 0%
where the time goes in v1:
time: 97 us; the launch traced here: 96.8 us
  Pallas kernels  32.2 us (33%)
  blocking collectives  25 us (26%)
  starting transfers between devices  20.9 us (22%)
  waiting for transfers between devices  16 us (16%)
  local copies, waits for them, and re-layouts  1.91 us (2%)
    pallas_call x4, Pallas kernels, call(): pl.pallas_call(body, out_shape=[jax.ShapeDtypeStruct(s, F32) for s in out...  32.2 us
    all_to_all x1, blocking collectives, on_device(): g = lax.all_to_all(g, 'gx', 0, 0, tiled=True)  25 us
    ppermute x8, starting transfers between devices, swap(): return lax.ppermute(value, axis, pairs(lax.axis_size(axis), offset))  20.9 us
    ppermute x8, waiting for transfers between devices, swap(): return lax.ppermute(value, axis, pairs(lax.axis_size(axis), offset))  16 us
  transfers between devices with their start and end apart: 8, of which 4 were waited for; matrix products, arithmetic and copies ran while one was open for 0% of the time, Pallas kernels for 0%

profile of v1, /device:TPU:1, one launch (start us, length us, event | category | flops | bytes accessed | tf_op | source)
XLA Modules:
  0.0 96.8 jit_solution(6540636202850783588)
XLA Ops:
  0.6 0.0 copy-start
  0.6 0.9 copy-done
  1.6 0.0 copy-start.1
  1.6 0.9 copy-done.1
  2.5 0.4 shard_map.41
  2.9 3.3 %collective-permute-start = (f32[2,64,128]{2,1,0:T(8,128)S(1)}, f32[2,64,128]{2,1,0:T(8,128)S(1)}, u32[]{:S(2)}, u32[]{:S(2)}) collective-permute-start(f32[2,64,128]{2,1,0:T(8,128)S(1)} %get-tuple-element.20), channel_id=1, source_target_pairs={{0,1},{1,0},{2,3},{3,2},{4,5},{5,4},{6,7},{7,6},{8,9},{9,8},{10,11... | collective-permute-start | bytes 196616 | tf_op jit(solution)/shard_map/ppermute | solution.py:28
  6.2 1.9 %collective-permute-start.1 = (f32[2,64,128]{2,1,0:T(8,128)S(1)}, f32[2,64,128]{2,1,0:T(8,128)S(1)}, u32[]{:S(2)}, u32[]{:S(2)}) collective-permute-start(f32[2,64,128]{2,1,0:T(8,128)S(1)} %get-tuple-element.21), channel_id=1, source_target_pairs={{1,2},{2,1},{3,4},{4,3},{5,6},{6,5},{9,10},{10,9},{11,12},{12,11},... | collective-permute-start | bytes 196616 | tf_op jit(solution)/shard_map/ppermute | solution.py:28
  8.2 0.0 collective-permute-done.ya
  8.2 3.6 %collective-permute-done.1.yb = f32[2,64,128]{2,1,0:T(8,128)S(1)} collective-permute-done((f32[2,64,128]{2,1,0:T(8,128)S(1)}, f32[2,64,128]{2,1,0:T(8,128)S(1)}, u32[]{:S(2)}, u32[]{:S(2)}) %collective-permute-start.1) | collective-permute-done | bytes 65568 | tf_op jit(solution)/shard_map/ppermute | solution.py:28
  11.8 0.7 collective-permute-start.3
  12.5 2.8 %collective-permute-start.2 = (f32[13,64,128]{2,1,0:T(8,128)S(1)}, f32[13,64,128]{2,1,0:T(8,128)S(1)}, u32[]{:S(2)}, u32[]{:S(2)}) collective-permute-start(f32[13,64,128]{2,1,0:T(8,128)S(1)} %get-tuple-element.37), channel_id=1, source_target_pairs={{0,8},{8,0},{16,24},{24,16},{32,40},{40,32},{48,56},{56,48},{64,72... | collective-permute-start | bytes 1277960 | tf_op jit(solution)/shard_map/ppermute | solution.py:28
  15.4 0.0 collective-permute-done.3.xb
  15.4 6.3 %collective-permute-done.2.xa = f32[13,64,128]{2,1,0:T(8,128)S(1)} collective-permute-done((f32[13,64,128]{2,1,0:T(8,128)S(1)}, f32[13,64,128]{2,1,0:T(8,128)S(1)}, u32[]{:S(2)}, u32[]{:S(2)}) %collective-permute-start.2) | collective-permute-done | bytes 426016 | tf_op jit(solution)/shard_map/ppermute | solution.py:28
  21.6 6.6 %shard_map.42 = (f32[18,64,256]{2,1,0:T(8,128)S(1)}, f32[18,64,256]{2,1,0:T(8,128)S(1)}, f32[18,64,256]{2,1,0:T(8,128)S(1)}, f32[8,32,128]{2,1,0:T(8,128)S(1)}, ...) custom-call(f32[512,128]{1,0:T(8,128)S(1)} %bitcast.5, f32[512,128]{1,0:T(8,128)S(1)} %bitcast.7, ...), custom_call_target="tpu_custom_call" | custom-call | tf_op jit(solution)/shard_map/pallas_call | solution.py:154
  28.2 1.8 %collective-permute-start.4 = (f32[11,32,128]{2,1,0:T(8,128)S(1)}, f32[11,32,128]{2,1,0:T(8,128)S(1)}, u32[]{:S(2)}, u32[]{:S(2)}) collective-permute-start(f32[11,32,128]{2,1,0:T(8,128)S(1)} %get-tuple-element.25), channel_id=1, source_target_pairs={{0,8},{8,0},{16,24},{24,16},{32,40},{40,32},{48,56},{56,48},{64,72... | collective-permute-start | bytes 540680 | tf_op jit(solution)/shard_map/ppermute | solution.py:28
  30.0 0.7 collective-permute-start.5
  30.7 2.2 %collective-permute-done.4.ra = f32[11,32,128]{2,1,0:T(8,128)S(1)} collective-permute-done((f32[11,32,128]{2,1,0:T(8,128)S(1)}, f32[11,32,128]{2,1,0:T(8,128)S(1)}, u32[]{:S(2)}, u32[]{:S(2)}) %collective-permute-start.4) | collective-permute-done | bytes 180256 | tf_op jit(solution)/shard_map/ppermute | solution.py:28
  32.9 0.0 collective-permute-done.5.rb
  32.9 2.7 %shard_map.43 = (f32[16,32,128]{2,1,0:T(8,128)S(1)}, f32[16,32,128]{2,1,0:T(8,128)S(1)}, f32[16,32,128]{2,1,0:T(8,128)S(1)}, f32[32,16,128]{2,1,0:T(8,128)S(1)}) custom-call(f32[6,32,128]{2,1,0:T(8,128)S(1)} %get-tuple-element.23.b1, f32[8,32,128]{2,1,0:T(8,128)S(1)} %get-tuple-element.24.k1, f32[11,32,128]{2,1,0:T(8,128)S(1)} %collective-permute-done.4.ra, ...), custom_call_target="tpu_custom_call" | custom-call | tf_op jit(solution)/shard_map/pallas_call | solution.py:154
  35.6 25.0 %all_to_all.5.g = f32[32,16,128]{2,1,0:T(8,128)S(1)} all-to-all(f32[32,16,128]{2,1,0:T(8,128)S(1)} %get-tuple-element.27), channel_id=1, replica_groups=mesh['gx'=32,'gy'=8] {'gx'}, dimensions={0} | all-to-all | bytes 524288 | tf_op jit(solution)/shard_map/all_to_all | solution.py:416
  60.6 9.6 %collective-permute-start.7 = (f32[32,16,128]{2,1,0:T(8,128)S(1)}, f32[32,16,128]{2,1,0:T(8,128)S(1)}, u32[]{:S(2)}, u32[]{:S(2)}) collective-permute-start(f32[32,16,128]{2,1,0:T(8,128)S(1)} %all_to_all.5.g), channel_id=1, source_target_pairs={{1,2},{2,1},{3,4},{4,3},{5,6},{6,5},{9,10},{10,9},{11,12},{12,11},... | collective-permute-start | bytes 786440 | tf_op jit(solution)/shard_map/ppermute | solution.py:28
  70.2 0.1 collective-permute-start.6
  70.3 3.9 %collective-permute-done.7.gb = f32[32,16,128]{2,1,0:T(8,128)S(1)} collective-permute-done((f32[32,16,128]{2,1,0:T(8,128)S(1)}, f32[32,16,128]{2,1,0:T(8,128)S(1)}, u32[]{:S(2)}, u32[]{:S(2)}) %collective-permute-start.7) | collective-permute-done | bytes 262176 | tf_op jit(solution)/shard_map/ppermute | solution.py:28
  74.2 0.0 collective-permute-done.6.ga
  74.2 22.6 %shard_map.44 = (f32[512,128]{1,0:T(8,128)}, f32[512,128]{1,0:T(8,128)}) custom-call(f32[32,16,128]{2,1,0:T(8,128)S(1)} %all_to_all.5.g, f32[32,16,128]{2,1,0:T(8,128)S(1)} %collective-permute-done.6.ga, f32[32,16,128]{2,1,0:T(8,128)S(1)} %collective-permute-done.7.gb, f32[16,32,128]{2,1,0:T(8,128)S(1)} %get-tuple-element.28.k1, ...), custom_call_target="tpu_custom_call" | custom-call | tf_op jit(solution)/shard_map/pallas_call | solution.py:154
  (2 shorter events, 0.0 us)
Async XLA Ops:
  0.6 1.0 copy-start
  1.6 0.9 copy-start.1
  2.9 5.2 %collective-permute-start = (f32[2,64,128]{2,1,0:T(8,128)S(1)}, f32[2,64,128]{2,1,0:T(8,128)S(1)}, u32[]{:S(2)}, u32[]{:S(2)}) collective-permute-start(f32[2,64,128]{2,1,0:T(8,128)S(1)} %get-tuple-element.20), channel_id=1, source_target_pairs={{0,1},{1,0},{2,3},{3,2},{4,5},{5,4},{6,7},{7,6},{8,9},{9,8},{10,11... | collective-permute-start | bytes 196616 | tf_op jit(solution)/shard_map/ppermute | solution.py:28
  6.2 5.6 %collective-permute-start.1 = (f32[2,64,128]{2,1,0:T(8,128)S(1)}, f32[2,64,128]{2,1,0:T(8,128)S(1)}, u32[]{:S(2)}, u32[]{:S(2)}) collective-permute-start(f32[2,64,128]{2,1,0:T(8,128)S(1)} %get-tuple-element.21), channel_id=1, source_target_pairs={{1,2},{2,1},{3,4},{4,3},{5,6},{6,5},{9,10},{10,9},{11,12},{12,11},... | collective-permute-start | bytes 196616 | tf_op jit(solution)/shard_map/ppermute | solution.py:28
  11.8 3.5 %collective-permute-start.3 = (f32[13,64,128]{2,1,0:T(8,128)S(1)}, f32[13,64,128]{2,1,0:T(8,128)S(1)}, u32[]{:S(2)}, u32[]{:S(2)}) collective-permute-start(f32[13,64,128]{2,1,0:T(8,128)S(1)} %get-tuple-element.36), channel_id=1, source_target_pairs={{8,16},{16,8},{24,32},{32,24},{40,48},{48,40},{56,64},{64,56},{72,... | collective-permute-start | bytes 1277960 | tf_op jit(solution)/shard_map/ppermute | solution.py:28
  12.5 9.1 %collective-permute-start.2 = (f32[13,64,128]{2,1,0:T(8,128)S(1)}, f32[13,64,128]{2,1,0:T(8,128)S(1)}, u32[]{:S(2)}, u32[]{:S(2)}) collective-permute-start(f32[13,64,128]{2,1,0:T(8,128)S(1)} %get-tuple-element.37), channel_id=1, source_target_pairs={{0,8},{8,0},{16,24},{24,16},{32,40},{40,32},{48,56},{56,48},{64,72... | collective-permute-start | bytes 1277960 | tf_op jit(solution)/shard_map/ppermute | solution.py:28
  28.2 4.7 %collective-permute-start.4 = (f32[11,32,128]{2,1,0:T(8,128)S(1)}, f32[11,32,128]{2,1,0:T(8,128)S(1)}, u32[]{:S(2)}, u32[]{:S(2)}) collective-permute-start(f32[11,32,128]{2,1,0:T(8,128)S(1)} %get-tuple-element.25), channel_id=1, source_target_pairs={{0,8},{8,0},{16,24},{24,16},{32,40},{40,32},{48,56},{56,48},{64,72... | collective-permute-start | bytes 540680 | tf_op jit(solution)/shard_map/ppermute | solution.py:28
  30.0 2.9 %collective-permute-start.5 = (f32[11,32,128]{2,1,0:T(8,128)S(1)}, f32[11,32,128]{2,1,0:T(8,128)S(1)}, u32[]{:S(2)}, u32[]{:S(2)}) collective-permute-start(f32[11,32,128]{2,1,0:T(8,128)S(1)} %get-tuple-element.26), channel_id=1, source_target_pairs={{8,16},{16,8},{24,32},{32,24},{40,48},{48,40},{56,64},{64,56},{72,... | collective-permute-start | bytes 540680 | tf_op jit(solution)/shard_map/ppermute | solution.py:28
  60.6 13.6 %collective-permute-start.7 = (f32[32,16,128]{2,1,0:T(8,128)S(1)}, f32[32,16,128]{2,1,0:T(8,128)S(1)}, u32[]{:S(2)}, u32[]{:S(2)}) collective-permute-start(f32[32,16,128]{2,1,0:T(8,128)S(1)} %all_to_all.5.g), channel_id=1, source_target_pairs={{1,2},{2,1},{3,4},{4,3},{5,6},{6,5},{9,10},{10,9},{11,12},{12,11},... | collective-permute-start | bytes 786440 | tf_op jit(solution)/shard_map/ppermute | solution.py:28
  70.2 4.0 %collective-permute-start.6 = (f32[32,16,128]{2,1,0:T(8,128)S(1)}, f32[32,16,128]{2,1,0:T(8,128)S(1)}, u32[]{:S(2)}, u32[]{:S(2)}) collective-permute-start(f32[32,16,128]{2,1,0:T(8,128)S(1)} %all_to_all.5.g), channel_id=1, source_target_pairs={{0,1},{1,0},{2,3},{3,2},{4,5},{5,4},{6,7},{7,6},{8,9},{9,8},{10,11... | collective-permute-start | bytes 786440 | tf_op jit(solution)/shard_map/ppermute | solution.py:28

commit v2 on v1

--- a/solution.py
+++ b/solution.py
@@ -12,7 +12,9 @@
 LOW_BOUND = 0.3
 HIGH_BOUND = 2.0
 COARSE_LOW = 0.02
-VMEM_LIMIT = 48 * 1024 * 1024
+VMEM_LIMIT = 28 * 1024 * 1024
+
+SHAPE0, SHAPE1, SHAPE2, WINDOW_UNROLL = (1,True), (4, True), (8, True), True
 
 KX, BX, KY, BY = 5, 4, 13, 12
 
@@ -46,7 +48,14 @@
 
 
 def dot(a, b):
-    return jnp.dot(a, b, preferred_element_type=F32, precision=lax.Precision.HIGHEST)
+    b = b.astype(jnp.bfloat16)
+    total = None
+    for _ in range(3):
+        piece = a.astype(jnp.bfloat16)
+        a = a - piece.astype(F32)
+        part = jnp.dot(piece, b, preferred_element_type=F32)
+        total = part if total is None else total + part
+    return total
 
 
 def coarsen_matrix(fine, coarse, right, left, scale):
@@ -96,50 +105,67 @@
     return total + down * turn(centre, 1, axis) + up * turn(centre, -1, axis)
 
 
+def rows(low, high, body, chunk, unroll):
+    full = (high - low) // chunk
+
+    def step(n, carry):
+        body(pl.ds(low + n * chunk, chunk), pl.ds(low + n * chunk - 1, chunk), pl.ds(low + n * chunk + 1, chunk))
+        return carry
+
+    lax.fori_loop(0, full, step, 0, unroll=unroll)
+    at = low + full * chunk
+    if at < high:
+        body(pl.ds(at, high - at), pl.ds(at - 1, high - at), pl.ds(at + 1, high - at))
+
+
 class Level:
-    def __init__(self, k, weights, bh, x, p, factor):
+    def __init__(self, k, weights, bh, x, p, factor, chunk, unroll):
         self.k, self.weights, self.bh, self.x, self.p, self.factor = k, weights, bh, x, p, factor
+        self.chunk, self.unroll = chunk, unroll
 
     def rows(self, low, high, body):
-        def step(q, carry):
-            body(q)
-            return carry
-
-        lax.fori_loop(low, high, step, 0)
-
-    def set_up(self, low, high, b, diagonal=None):
-        def body(q):
-            weights, inverse, diag = weights_row(self.k[q], self.k[q - 1], self.k[q + 1], self.factor)
+        rows(low, high, body, self.chunk, self.unroll)
+
+    def set_up(self, low, high, b, diagonal):
+        def body(q, below, above):
+            weights, inverse, diag = weights_row(self.k[q], self.k[below], self.k[above], self.factor)
             for n in range(6):
                 self.weights[n, q] = weights[n]
             self.bh[q] = b[q] * inverse
-            if diagonal is not None:
-                diagonal[q] = diag
+            diagonal[q] = diag
 
         self.rows(low, high, body)
 
-    def total(self, x, q):
-        return neighbour_sum([self.weights[n, q] for n in range(6)], x[q - 1], x[q], x[q + 1])
+    def total(self, x, q, below, above):
+        return neighbour_sum([self.weights[n, q] for n in range(6)], x[below], x[q], x[above])
 
     def pre(self, low, high):
         middle, ((c1, c2),) = chebyshev(2, LOW_BOUND)
 
-        def body(q):
+        def body(q, below, above):
             first = self.bh[q]
-            self.x[q] = (1 / middle) * (1 + c1 - c2 + c2 * middle) * first + (c2 / middle) * self.total(self.bh, q)
+            total = self.total(self.bh, q, below, above)
+            self.x[q] = (1 / middle) * (1 + c1 - c2 + c2 * middle) * first + (c2 / middle) * total
+
+        self.rows(low, high, body)
+
+    def residue(self, low, high, diagonal, out, at):
+        def body(q, below, above):
+            value = diagonal[q] * (self.bh[q] - self.x[q] + self.total(self.x, q, below, above))
+            out[pl.ds(q.start + (at - low), q.size)] = value
 
         self.rows(low, high, body)
 
     def post(self, low, high, out):
         middle, ((c1, c2),) = chebyshev(2, LOW_BOUND)
 
-        def first(q):
-            update = (self.bh[q] - self.x[q] + self.total(self.x, q)) * (1 / middle)
+        def first(q, below, above):
+            update = (self.bh[q] - self.x[q] + self.total(self.x, q, below, above)) * (1 / middle)
             self.p[q] = update
             out[q] = self.x[q] + update
 
-        def second(q):
-            residue = self.bh[q] - out[q] + self.total(out, q)
+        def second(q, below, above):
+            residue = self.bh[q] - out[q] + self.total(out, q, below, above)
             self.x[q] = out[q] + c1 * self.p[q] + c2 * residue
 
         self.rows(low - 1, high + 1, first)
@@ -194,7 +220,7 @@
     return jnp.where(lane < width, right_part, jnp.where(lane >= 128 - width, left_part, 0.0))
 
 
-def first_kernel(b_ref, k_ref, xa, xb, ya, yb, k_out, b_out, x_out, k1_out, b1_out, sa, sb, weights, bh, diagonal, wide, thin):
+def first_kernel(b_ref, k_ref, xa, xb, ya, yb, weights, bh, diagonal, x_out, k1_out, b1_out, sa, sb, k_out, b_out, fine, wide, thin):
     odd_x, odd_y = odd("gx"), odd("gy")
     lane = iota((64, 128), 1)
 
@@ -223,18 +249,12 @@
         for j in range(BX):
             fill(b_out, 1, 1 + j if side == 0 else 13 + j, pick(KX + j), strips, 4 + j if side == 0 else j, BY)
 
-    level = Level(k_out, weights, bh, x_out, None, 1.0)
+    level = Level(k_out, weights, bh, x_out, None, 1.0, *SHAPE0)
     level.set_up(1, 17, b_out, diagonal)
     level.pre(2, 16)
-
-    def residue(q):
-        return diagonal[q] * (bh[q] - x_out[q] + level.total(x_out, q))
-
-    def pair(m, carry):
-        wide[m] = residue(2 * m + 3) + residue(2 * m + 4)
-        return carry
-
-    lax.fori_loop(0, 6, pair, 0)
+    level.residue(3, 15, diagonal, fine, 0)
+    for m in range(6):
+        wide[m] = fine[2 * m] + fine[2 * m + 1]
     for m in range(8):
         wide[6 + m] = k_out[2 * m + 1] + k_out[2 * m + 2]
     matrix = coarsen_matrix(256, 128, 140, 12, 0.125)
@@ -255,7 +275,7 @@
         sb[5 + m] = jnp.where(odd_x, done[6 + m], done[8 + m])
 
 
-def second_kernel(count, b1, k1, ra, rb, k_out, b_out, x_out, g_out, weights, bh, diagonal, thin):
+def second_kernel(count, b1, k1, ra, rb, weights, bh, x_out, g_out, k_out, b_out, diagonal, fine, thin):
     odd_x = odd("gx")
     for side in range(2):
 
@@ -271,14 +291,11 @@
         k_out[6 + j] = k1[2 + j]
         b_out[6 + j] = b1[1 + j]
 
-    level = Level(k_out, weights, bh, x_out, None, 0.25)
+    level = Level(k_out, weights, bh, x_out, None, 0.25, *SHAPE1)
     level.set_up(1, 15, b_out, diagonal)
     level.pre(2, 14)
-
-    def residue(q):
-        return diagonal[q] * (bh[q] - x_out[q] + level.total(x_out, q))
-
-    parts = [residue(6) + residue(7), residue(8) + residue(9), k_out[6] + k_out[7], k_out[8] + k_out[9]]
+    level.residue(6, 10, diagonal, fine, 0)
+    parts = [fine[0] + fine[1], fine[2] + fine[3], k_out[6] + k_out[7], k_out[8] + k_out[9]]
     matrix = coarsen_matrix(128, 128, 64, 0, 0.125)
     thin[...] = dot(jnp.concatenate(parts, axis=0), matrix)
     payload = jnp.zeros((16, 128), F32)
@@ -290,8 +307,8 @@
 
 
 def last_kernel(
-    count, g, ga, gb, k1, b1, x1_in, k0, b0, x0_in, pressure, residual,
-    k2, b2, w2, bh2, x2, y2, p2, fine2, coarse2, w1, bh1, x1, y1, p1, stack1, w0, bh0, d0, x0, y0, p0, stack0,
+    count, g, ga, gb, w1, bh1, x1, w0, bh0, d0, x0, pressure, residual,
+    k2, b2, w2, bh2, x2, y2, p2, fine2, sums2, coarse2, t1, y1, p1, stack1, t0, y0, p0, stack0,
 ):
     odd_y = odd("gy")
     me = lax.axis_index("gx")
@@ -310,25 +327,19 @@
                 out[2 * j + m] = jnp.where(inside, value, 0.0)
         return carry
 
-    lax.fori_loop(0, 23, window, 0)
-    level = Level(k2, w2, bh2, x2, p2, 0.0625)
+    lax.fori_loop(0, 23, window, 0, unroll=WINDOW_UNROLL)
+    level = Level(k2, w2, bh2, x2, p2, 0.0625, *SHAPE2)
     level.set_up(1, 45, b2, y2)
     level.pre(2, 44)
-
-    def residue(q):
-        return y2[q] * (bh2[q] - x2[q] + level.total(x2, q))
-
-    def pair(m, carry):
-        fine2[m] = residue(2 * m) + residue(2 * m + 1)
-        return carry
-
-    lax.fori_loop(2, 21, pair, 0)
+    level.residue(4, 42, y2, fine2, 4)
     zero = jnp.zeros((16, 128), F32)
     for m in (0, 1, 21, 22):
-        fine2[m] = zero
+        sums2[m] = zero
+    for m in range(2, 21):
+        sums2[m] = fine2[2 * m] + fine2[2 * m + 1]
     for m in range(23):
-        fine2[23 + m] = k2[2 * m] + k2[2 * m + 1]
-    coarse2[...] = dot(fine2[...].reshape(46 * 16, 128), coarsen_matrix(128, 128, 64, 32, 0.125))
+        sums2[23 + m] = k2[2 * m] + k2[2 * m + 1]
+    coarse2[...] = dot(sums2[...].reshape(46 * 16, 128), coarsen_matrix(128, 128, 64, 32, 0.125))
     both = coarse2[pl.ds(0, 46 * 8, stride=2), :] + coarse2[pl.ds(1, 46 * 8, stride=2), :]
     both = both.reshape(46, 8, 128)
     b3, k3 = both[:23], both[23:]
@@ -364,26 +375,24 @@
             stack1[pl.ds(32 * m + half, 16, stride=2), :] = x2[20 + m]
     fine = dot(stack1[...], refine_matrix(128, 128, 70, 6))
     for m in range(12):
-        x1[2 + m] = x1_in[2 + m] + fine[32 * (m // 2) : 32 * (m // 2) + 32]
-    level = Level(k1, w1, bh1, x1, p1, 0.25)
-    level.set_up(3, 13, b1)
+        t1[2 + m] = x1[2 + m] + fine[32 * (m // 2) : 32 * (m // 2) + 32]
+    level = Level(None, w1, bh1, t1, p1, 0.25, *SHAPE1)
     level.post(4, 12, y1)
 
     for m in range(8):
         for half in range(2):
-            stack0[pl.ds(64 * m + half, 32, stride=2), :] = x1[4 + m]
+            stack0[pl.ds(64 * m + half, 32, stride=2), :] = t1[4 + m]
     matrix = refine_matrix(128, 256, 140, 12)
     fine = dot(stack0[...], matrix)
     for m in range(14):
         row = (m + 1) // 2
-        x0[2 + m] = x0_in[2 + m] + fine[64 * row : 64 * row + 64]
-    level = Level(k0, w0, bh0, x0, p0, 1.0)
-    level.set_up(3, 15, b0, d0)
+        t0[2 + m] = x0[2 + m] + fine[64 * row : 64 * row + 64]
+    level = Level(None, w0, bh0, t0, p0, 1.0, *SHAPE0)
     level.post(4, 14, y0)
     for i in range(8):
         q = 5 + i
-        value = x0[q]
-        left = d0[q] * (bh0[q] - value + level.total(x0, q))
+        value = t0[q]
+        left = d0[q] * (bh0[q] - value + level.total(t0, q, q - 1, q + 1))
         pressure[pl.ds(i, 64, stride=8), :] = value[:, 0:128]
         residual[pl.ds(i, 64, stride=8), :] = left[:, 0:128]
 
@@ -400,17 +409,17 @@
 
     xa, xb = swap(with_y(xa), "gx", 0), swap(with_y(xb), "gx", 1)
     rows0, rows1 = (18, 64, 256), (16, 32, 128)
-    k0, b0, x0, k1, b1, sa, sb = call(
+    w0, bh0, d0, x0, k1, b1, sa, sb = call(
         first_kernel,
-        [rows0, rows0, rows0, (8, 32, 128), (6, 32, 128), (11, 32, 128), (11, 32, 128)],
-        [(6,) + rows0, rows0, rows0, (14, 64, 256), (14 * 64, 128)],
+        [(6,) + rows0, rows0, rows0, rows0, (8, 32, 128), (6, 32, 128), (11, 32, 128), (11, 32, 128)],
+        [rows0, rows0, (12, 64, 256), (14, 64, 256), (14 * 64, 128)],
         b, k, xa, xb, ya, yb,
     )
     ra, rb = swap(sa, "gx", 0), swap(sb, "gx", 1)
-    k1, b1, x1, g = call(
+    w1, bh1, x1, g = call(
         functools.partial(second_kernel, count),
-        [rows1, rows1, rows1, (count, 16, 128)],
-        [(6,) + rows1, rows1, rows1, (128, 128)],
+        [(6,) + rows1, rows1, rows1, (count, 16, 128)],
+        [rows1, rows1, rows1, (4, 32, 128), (128, 128)],
         b1, k1, ra, rb,
     )
     g = lax.all_to_all(g, "gx", 0, 0, tiled=True)
@@ -419,10 +428,10 @@
     pressure, residual = call(
         functools.partial(last_kernel, count),
         [(512, 128)] * 2,
-        [rows2, rows2, (6,) + rows2, rows2, rows2, rows2, rows2, (46, 16, 128), (46 * 16, 128)]
-        + [(6,) + rows1, rows1, rows1, rows1, rows1, (6 * 32, 128)]
-        + [(6,) + rows0, rows0, rows0, rows0, rows0, rows0, (8 * 64, 128)],
-        g, ga, gb, k1, b1, x1, k0, b0, x0,
+        [rows2, rows2, (6,) + rows2, rows2, rows2, rows2, rows2, rows2, rows2, (46 * 16, 128)]
+        + [rows1, rows1, rows1, (6 * 32, 128)]
+        + [rows0, rows0, rows0, (8 * 64, 128)],
+        g, ga, gb, w1, bh1, x1, w0, bh0, d0, x0,
     )
     return pressure.reshape(64, 8, 128), residual.reshape(64, 8, 128)
 

time: 97 us -> 75.2 us (0.78)
  Pallas kernels: 32.2 us -> 10.4 us
    pallas_call x4, Pallas kernels: 32.2 us -> 10.4 us  [call(): pl.pallas_call(body, out_shape=[jax.ShapeDtypeStruct(s, F32) for s in out...]
where the time goes in v2:
time: 75.2 us; the launch traced here: 75 us
  blocking collectives  25 us (33%)
  starting transfers between devices  20.9 us (28%)
  waiting for transfers between devices  16 us (21%)
  Pallas kernels  10.4 us (14%)
  local copies, waits for them, and re-layouts  1.91 us (3%)
    all_to_all x1, blocking collectives, on_device(): g = lax.all_to_all(g, 'gx', 0, 0, tiled=True)  25 us
    ppermute x8, starting transfers between devices, swap(): return lax.ppermute(value, axis, pairs(lax.axis_size(axis), offset))  20.9 us
    ppermute x8, waiting for transfers between devices, swap(): return lax.ppermute(value, axis, pairs(lax.axis_size(axis), offset))  16 us
    pallas_call x4, Pallas kernels, call(): pl.pallas_call(body, out_shape=[jax.ShapeDtypeStruct(s, F32) for s in out...  10.4 us
    unnamed x4, local copies, waits for them, and re-layouts  1.89 us
  transfers between devices with their start and end apart: 8, of which 4 were waited for; matrix products, arithmetic and copies ran while one was open for 0% of the time, Pallas kernels for 0%

profile of v2, /device:TPU:1, one launch (start us, length us, event | category | flops | bytes accessed | tf_op | source)
XLA Modules:
  0.0 75.0 jit_solution(14881562391807175419)
XLA Ops:
  0.6 0.0 copy-start
  0.6 0.9 %copy-done = f32[64,8,128]{2,1,0:T(8,128)S(1)} copy-done((f32[64,8,128]{2,1,0:T(8,128)S(1)}, f32[64,8,128]{2,1,0:T(8,128)}, u32[]{:S(2)}) %copy-start) | copy-done | bytes 262168
  1.6 0.0 copy-start.1
  1.6 0.9 %copy-done.1 = f32[64,8,128]{2,1,0:T(8,128)S(1)} copy-done((f32[64,8,128]{2,1,0:T(8,128)S(1)}, f32[64,8,128]{2,1,0:T(8,128)}, u32[]{:S(2)}) %copy-start.1) | copy-done | bytes 262168
  2.5 0.4 shard_map.41
  2.9 3.3 %collective-permute-start = (f32[2,64,128]{2,1,0:T(8,128)S(1)}, f32[2,64,128]{2,1,0:T(8,128)S(1)}, u32[]{:S(2)}, u32[]{:S(2)}) collective-permute-start(f32[2,64,128]{2,1,0:T(8,128)S(1)} %get-tuple-element.21), channel_id=1, source_target_pairs={{0,1},{1,0},{2,3},{3,2},{4,5},{5,4},{6,7},{7,6},{8,9},{9,8},{10,11... | collective-permute-start | bytes 196616 | tf_op jit(solution)/shard_map/ppermute | solution.py:30
  6.2 1.9 %collective-permute-start.1 = (f32[2,64,128]{2,1,0:T(8,128)S(1)}, f32[2,64,128]{2,1,0:T(8,128)S(1)}, u32[]{:S(2)}, u32[]{:S(2)}) collective-permute-start(f32[2,64,128]{2,1,0:T(8,128)S(1)} %get-tuple-element.22), channel_id=1, source_target_pairs={{1,2},{2,1},{3,4},{4,3},{5,6},{6,5},{9,10},{10,9},{11,12},{12,11},... | collective-permute-start | bytes 196616 | tf_op jit(solution)/shard_map/ppermute | solution.py:30
  8.2 0.0 collective-permute-done.ya
  8.2 3.6 %collective-permute-done.1.yb = f32[2,64,128]{2,1,0:T(8,128)S(1)} collective-permute-done((f32[2,64,128]{2,1,0:T(8,128)S(1)}, f32[2,64,128]{2,1,0:T(8,128)S(1)}, u32[]{:S(2)}, u32[]{:S(2)}) %collective-permute-start.1) | collective-permute-done | bytes 65568 | tf_op jit(solution)/shard_map/ppermute | solution.py:30
  11.8 0.7 collective-permute-start.3
  12.5 2.8 %collective-permute-start.2 = (f32[13,64,128]{2,1,0:T(8,128)S(1)}, f32[13,64,128]{2,1,0:T(8,128)S(1)}, u32[]{:S(2)}, u32[]{:S(2)}) collective-permute-start(f32[13,64,128]{2,1,0:T(8,128)S(1)} %get-tuple-element.39), channel_id=1, source_target_pairs={{0,8},{8,0},{16,24},{24,16},{32,40},{40,32},{48,56},{56,48},{64,72... | collective-permute-start | bytes 1277960 | tf_op jit(solution)/shard_map/ppermute | solution.py:30
  15.4 0.0 collective-permute-done.3.xb
  15.4 6.3 %collective-permute-done.2.xa = f32[13,64,128]{2,1,0:T(8,128)S(1)} collective-permute-done((f32[13,64,128]{2,1,0:T(8,128)S(1)}, f32[13,64,128]{2,1,0:T(8,128)S(1)}, u32[]{:S(2)}, u32[]{:S(2)}) %collective-permute-start.2) | collective-permute-done | bytes 426016 | tf_op jit(solution)/shard_map/ppermute | solution.py:30
  21.6 3.9 %shard_map.42 = (f32[6,18,64,256]{3,2,1,0:T(8,128)S(1)}, f32[18,64,256]{2,1,0:T(8,128)S(1)}, f32[18,64,256]{2,1,0:T(8,128)S(1)}, f32[18,64,256]{2,1,0:T(8,128)S(...) custom-call(f32[512,128]{1,0:T(8,128)S(1)} %bitcast.5, ...), custom_call_target="tpu_custom_call" | custom-call | tf_op jit(solution)/shard_map/pallas_call | solution.py:180
  25.5 1.8 %collective-permute-start.4 = (f32[11,32,128]{2,1,0:T(8,128)S(1)}, f32[11,32,128]{2,1,0:T(8,128)S(1)}, u32[]{:S(2)}, u32[]{:S(2)}) collective-permute-start(f32[11,32,128]{2,1,0:T(8,128)S(1)} %get-tuple-element.26), channel_id=1, source_target_pairs={{0,8},{8,0},{16,24},{24,16},{32,40},{40,32},{48,56},{56,48},{64,72... | collective-permute-start | bytes 540680 | tf_op jit(solution)/shard_map/ppermute | solution.py:30
  27.3 0.7 collective-permute-start.5
  28.0 2.2 %collective-permute-done.4.ra = f32[11,32,128]{2,1,0:T(8,128)S(1)} collective-permute-done((f32[11,32,128]{2,1,0:T(8,128)S(1)}, f32[11,32,128]{2,1,0:T(8,128)S(1)}, u32[]{:S(2)}, u32[]{:S(2)}) %collective-permute-start.4) | collective-permute-done | bytes 180256 | tf_op jit(solution)/shard_map/ppermute | solution.py:30
  30.2 0.0 collective-permute-done.5.rb
  30.2 0.6 shard_map.43
  30.8 25.0 %all_to_all.5.g = f32[32,16,128]{2,1,0:T(8,128)S(1)} all-to-all(f32[32,16,128]{2,1,0:T(8,128)S(1)} %get-tuple-element.28), channel_id=1, replica_groups=mesh['gx'=32,'gy'=8] {'gx'}, dimensions={0} | all-to-all | bytes 524288 | tf_op jit(solution)/shard_map/all_to_all | solution.py:425
  55.8 9.6 %collective-permute-start.7 = (f32[32,16,128]{2,1,0:T(8,128)S(1)}, f32[32,16,128]{2,1,0:T(8,128)S(1)}, u32[]{:S(2)}, u32[]{:S(2)}) collective-permute-start(f32[32,16,128]{2,1,0:T(8,128)S(1)} %all_to_all.5.g), channel_id=1, source_target_pairs={{1,2},{2,1},{3,4},{4,3},{5,6},{6,5},{9,10},{10,9},{11,12},{12,11},... | collective-permute-start | bytes 786440 | tf_op jit(solution)/shard_map/ppermute | solution.py:30
  65.4 0.1 collective-permute-start.6
  65.5 3.9 %collective-permute-done.7.gb = f32[32,16,128]{2,1,0:T(8,128)S(1)} collective-permute-done((f32[32,16,128]{2,1,0:T(8,128)S(1)}, f32[32,16,128]{2,1,0:T(8,128)S(1)}, u32[]{:S(2)}, u32[]{:S(2)}) %collective-permute-start.7) | collective-permute-done | bytes 262176 | tf_op jit(solution)/shard_map/ppermute | solution.py:30
  69.4 0.0 collective-permute-done.6.ga
  69.4 5.5 %shard_map.44 = (f32[512,128]{1,0:T(8,128)}, f32[512,128]{1,0:T(8,128)}) custom-call(f32[32,16,128]{2,1,0:T(8,128)S(1)} %all_to_all.5.g, f32[32,16,128]{2,1,0:T(8,128)S(1)} %collective-permute-done.6.ga, f32[32,16,128]{2,1,0:T(8,128)S(1)} %collective-permute-done.7.gb, f32[6,16,32,128]{3,2,1,0:T(8,128)S(1)} %get-tuple-element.29.w1, ...), custom_call_target="tpu_custom_call" | custom-call | tf_op jit(solution)/shard_map/pallas_call | solution.py:180
  (2 shorter events, 0.0 us)
Async XLA Ops:
  0.6 1.0 %copy-start = (f32[64,8,128]{2,1,0:T(8,128)S(1)}, f32[64,8,128]{2,1,0:T(8,128)}, u32[]{:S(2)}) copy-start(f32[64,8,128]{2,1,0:T(8,128)} %param.2) | copy-start | bytes 786436
  1.6 0.9 %copy-start.1 = (f32[64,8,128]{2,1,0:T(8,128)S(1)}, f32[64,8,128]{2,1,0:T(8,128)}, u32[]{:S(2)}) copy-start(f32[64,8,128]{2,1,0:T(8,128)} %param.3) | copy-start | bytes 786436
  2.9 5.2 %collective-permute-start = (f32[2,64,128]{2,1,0:T(8,128)S(1)}, f32[2,64,128]{2,1,0:T(8,128)S(1)}, u32[]{:S(2)}, u32[]{:S(2)}) collective-permute-start(f32[2,64,128]{2,1,0:T(8,128)S(1)} %get-tuple-element.21), channel_id=1, source_target_pairs={{0,1},{1,0},{2,3},{3,2},{4,5},{5,4},{6,7},{7,6},{8,9},{9,8},{10,11... | collective-permute-start | bytes 196616 | tf_op jit(solution)/shard_map/ppermute | solution.py:30
  6.2 5.6 %collective-permute-start.1 = (f32[2,64,128]{2,1,0:T(8,128)S(1)}, f32[2,64,128]{2,1,0:T(8,128)S(1)}, u32[]{:S(2)}, u32[]{:S(2)}) collective-permute-start(f32[2,64,128]{2,1,0:T(8,128)S(1)} %get-tuple-element.22), channel_id=1, source_target_pairs={{1,2},{2,1},{3,4},{4,3},{5,6},{6,5},{9,10},{10,9},{11,12},{12,11},... | collective-permute-start | bytes 196616 | tf_op jit(solution)/shard_map/ppermute | solution.py:30
  11.8 3.5 %collective-permute-start.3 = (f32[13,64,128]{2,1,0:T(8,128)S(1)}, f32[13,64,128]{2,1,0:T(8,128)S(1)}, u32[]{:S(2)}, u32[]{:S(2)}) collective-permute-start(f32[13,64,128]{2,1,0:T(8,128)S(1)} %get-tuple-element.38), channel_id=1, source_target_pairs={{8,16},{16,8},{24,32},{32,24},{40,48},{48,40},{56,64},{64,56},{72,... | collective-permute-start | bytes 1277960 | tf_op jit(solution)/shard_map/ppermute | solution.py:30
  12.5 9.1 %collective-permute-start.2 = (f32[13,64,128]{2,1,0:T(8,128)S(1)}, f32[13,64,128]{2,1,0:T(8,128)S(1)}, u32[]{:S(2)}, u32[]{:S(2)}) collective-permute-start(f32[13,64,128]{2,1,0:T(8,128)S(1)} %get-tuple-element.39), channel_id=1, source_target_pairs={{0,8},{8,0},{16,24},{24,16},{32,40},{40,32},{48,56},{56,48},{64,72... | collective-permute-start | bytes 1277960 | tf_op jit(solution)/shard_map/ppermute | solution.py:30
  25.5 4.7 %collective-permute-start.4 = (f32[11,32,128]{2,1,0:T(8,128)S(1)}, f32[11,32,128]{2,1,0:T(8,128)S(1)}, u32[]{:S(2)}, u32[]{:S(2)}) collective-permute-start(f32[11,32,128]{2,1,0:T(8,128)S(1)} %get-tuple-element.26), channel_id=1, source_target_pairs={{0,8},{8,0},{16,24},{24,16},{32,40},{40,32},{48,56},{56,48},{64,72... | collective-permute-start | bytes 540680 | tf_op jit(solution)/shard_map/ppermute | solution.py:30
  27.3 2.9 %collective-permute-start.5 = (f32[11,32,128]{2,1,0:T(8,128)S(1)}, f32[11,32,128]{2,1,0:T(8,128)S(1)}, u32[]{:S(2)}, u32[]{:S(2)}) collective-permute-start(f32[11,32,128]{2,1,0:T(8,128)S(1)} %get-tuple-element.27), channel_id=1, source_target_pairs={{8,16},{16,8},{24,32},{32,24},{40,48},{48,40},{56,64},{64,56},{72,... | collective-permute-start | bytes 540680 | tf_op jit(solution)/shard_map/ppermute | solution.py:30
  55.8 13.6 %collective-permute-start.7 = (f32[32,16,128]{2,1,0:T(8,128)S(1)}, f32[32,16,128]{2,1,0:T(8,128)S(1)}, u32[]{:S(2)}, u32[]{:S(2)}) collective-permute-start(f32[32,16,128]{2,1,0:T(8,128)S(1)} %all_to_all.5.g), channel_id=1, source_target_pairs={{1,2},{2,1},{3,4},{4,3},{5,6},{6,5},{9,10},{10,9},{11,12},{12,11},... | collective-permute-start | bytes 786440 | tf_op jit(solution)/shard_map/ppermute | solution.py:30
  65.4 4.0 %collective-permute-start.6 = (f32[32,16,128]{2,1,0:T(8,128)S(1)}, f32[32,16,128]{2,1,0:T(8,128)S(1)}, u32[]{:S(2)}, u32[]{:S(2)}) collective-permute-start(f32[32,16,128]{2,1,0:T(8,128)S(1)} %all_to_all.5.g), channel_id=1, source_target_pairs={{0,1},{1,0},{2,3},{3,2},{4,5},{5,4},{6,7},{7,6},{8,9},{9,8},{10,11... | collective-permute-start | bytes 786440 | tf_op jit(solution)/shard_map/ppermute | solution.py:30

commit v3 on v2

--- a/solution.py
+++ b/solution.py
@@ -16,7 +16,10 @@
 
 SHAPE0, SHAPE1, SHAPE2, WINDOW_UNROLL = (1,True), (4, True), (8, True), True
 
-KX, BX, KY, BY = 5, 4, 13, 12
+PIECES = 4
+
+KX, BX, KY, BY = 7, 6, 13, 12
+PACKED = ((0, 0, 9, 14), (0, 9, 9, 14), (0, 18, 4, 14), (1, 0, 10, 12), (1, 10, 10, 12))
 
 
 def pairs(size, offset):
@@ -176,140 +179,181 @@
     return [pl.BlockSpec(memory_space=pltpu.VMEM)] * n
 
 
-def call(body, outs, scratch, *args):
+def call(body, outs, scratch, *args, hbm_in=0, hbm_out=0, sems=(), cost=None):
+    args = [pltpu.with_memory_space_constraint(x, pltpu.HBM) if n < hbm_in else x for n, x in enumerate(args)]
     return pl.pallas_call(
         body,
-        out_shape=[jax.ShapeDtypeStruct(s, F32) for s in outs],
-        in_specs=spec(len(args)),
-        out_specs=spec(len(outs)),
-        scratch_shapes=[pltpu.VMEM(s, F32) for s in scratch],
+        out_shape=[pltpu.HBM(s, F32) if n < hbm_out else jax.ShapeDtypeStruct(s, F32) for n, s in enumerate(outs)],
+        in_specs=[pl.BlockSpec(memory_space=pltpu.HBM)] * hbm_in + spec(len(args) - hbm_in),
+        out_specs=[pl.BlockSpec(memory_space=pltpu.HBM)] * hbm_out + spec(len(outs) - hbm_out),
+        scratch_shapes=[pltpu.VMEM(s, F32) for s in scratch] + [pltpu.SemaphoreType.DMA(s) for s in sems],
         compiler_params=pltpu.CompilerParams(vmem_limit_bytes=VMEM_LIMIT),
+        cost_estimate=cost,
     )(*args)
+
+
+class Copies:
+    def __init__(self, sems):
+        self.sems, self.used = sems, 0
+
+    def start(self, source, target):
+        copy = pltpu.make_async_copy(source, target, self.sems.at[self.used])
+        copy.start()
+        self.used += 1
+        return copy
 
 
 def odd(axis):
     return lax.rem(lax.axis_index(axis), 2) == 1
 
 
-def pack_kernel(b_ref, k_ref, ya, yb, xa, xb):
-    odd_x, odd_y = odd("gx"), odd("gy")
-    lane = iota((64, 128), 1)
-    for n, (ref, width) in enumerate(((k_ref, KY), (b_ref, BY))):
-        first, last = jnp.zeros((64, 128), F32), jnp.zeros((64, 128), F32)
+def pieces(n, source, target, copies):
+    size = source.shape[0] // n
+    return [copies.start(source.at[pl.ds(i * size, size)], target.at[pl.ds(i * size, size)]) for i in range(n)]
+
+
+def strip_kernel(b_any, k_any, own, xa, xb, b_ref, k_ref, sems):
+    odd_x = odd("gx")
+    arrays = ((k_ref, KX), (b_ref, BX))
+    copies = Copies(sems)
+    waits = [pieces(PIECES, k_any, k_ref, copies), pieces(PIECES, b_any, b_ref, copies)]
+    at = 0
+    for n, (ref, width) in enumerate(arrays):
+        for copy in waits[n]:
+            copy.wait()
+        planes = [ref[pl.ds(i, 64, stride=8), :] for i in range(8)]
         for i in range(8):
-            plane = ref[pl.ds(i, 64, stride=8), :]
-            here = (lane >= 16 * i) & (lane < 16 * i + width)
-            first = jnp.where(here, turn(plane, 16 * i, 1), first)
-            last = jnp.where(here, turn(plane, 16 * i + width, 1), last)
-        ya[n] = jnp.where(odd_y, first, last)
-        yb[n] = jnp.where(odd_y, last, first)
-    at = 0
-    for ref, width in ((k_ref, KX), (b_ref, BX)):
+            own[n, i] = planes[i]
         for i in range(width):
-            first = ref[pl.ds(i, 64, stride=8), :]
-            last = ref[pl.ds(8 - width + i, 64, stride=8), :]
+            first, last = planes[i], planes[8 - width + i]
             xa[at] = jnp.where(odd_x, first, last)
             xb[at] = jnp.where(odd_x, last, first)
             at += 1
 
 
-def assemble(strips, n, width, i, lane):
-    left, right = strips
-    right_part = turn(right[n], -16 * i, 1)
-    left_part = turn(left[n], 128 - width - 16 * i, 1)
-    return jnp.where(lane < width, right_part, jnp.where(lane >= 128 - width, left_part, 0.0))
-
-
-def first_kernel(b_ref, k_ref, xa, xb, ya, yb, weights, bh, diagonal, x_out, k1_out, b1_out, sa, sb, k_out, b_out, fine, wide, thin):
+def pack_kernel(own, xa, xb, k_out, b_out, ya, yb):
     odd_x, odd_y = odd("gx"), odd("gy")
     lane = iota((64, 128), 1)
-
-    def by_y(a, b):
-        return jnp.where(odd_y, a, b), jnp.where(odd_y, b, a)
-
-    def fill(out, n, q, plane, strips, i, width):
-        out[q, :, 0:128] = plane
-        out[q, :, 128:256] = assemble(strips, n, width, i, lane)
-
-    own = [by_y(ya[n], yb[n]) for n in range(2)]
-    own = ([own[0][0], own[1][0]], [own[0][1], own[1][1]])
+    for n in range(KX + BX):
+        a, b = xa[n], xb[n]
+        left, right = jnp.where(odd_x, a, b), jnp.where(odd_x, b, a)
+        if n < KX:
+            k_out[n], k_out[8 + KX + n] = left, right
+        else:
+            b_out[n - KX], b_out[8 + BX + n - KX] = left, right
     for i in range(8):
-        fill(k_out, 0, i + 5, k_ref[pl.ds(i, 64, stride=8), :], own, i, KY)
-        fill(b_out, 1, i + 5, b_ref[pl.ds(i, 64, stride=8), :], own, i, BY)
-    for side in range(2):
-
-        def pick(n):
-            a, b = xa[n], xb[n]
-            return jnp.where(odd_x, a, b) if side == 0 else jnp.where(odd_x, b, a)
-
-        strips = [by_y(pick(9 + n), pick(11 + n)) for n in range(2)]
-        strips = ([strips[0][0], strips[1][0]], [strips[0][1], strips[1][1]])
-        for j in range(KX):
-            fill(k_out, 0, j if side == 0 else 13 + j, pick(j), strips, 3 + j if side == 0 else j, KY)
-        for j in range(BX):
-            fill(b_out, 1, 1 + j if side == 0 else 13 + j, pick(KX + j), strips, 4 + j if side == 0 else j, BY)
-
+        k_out[KX + i] = own[0, i]
+        b_out[BX + i] = own[1, i]
+    for n, (array, start, count, room) in enumerate(PACKED):
+        ref, width = ((k_out, KY), (b_out, BY))[array]
+        first, last = jnp.zeros((64, 128), F32), jnp.zeros((64, 128), F32)
+        for i in range(count):
+            plane = ref[start + i]
+            here = (lane >= room * i) & (lane < room * i + width)
+            first = jnp.where(here, turn(plane, room * i, 1), first)
+            last = jnp.where(here, turn(plane, room * i + width, 1), last)
+        ya[n] = jnp.where(odd_y, first, last)
+        yb[n] = jnp.where(odd_y, last, first)
+
+
+def first_kernel(
+    count, k_rows, b_rows, ya, yb, k_hbm, b_hbm, x_hbm, k1_hbm, b1_hbm, x1_hbm, sa_hbm, sb_hbm, g_hbm,
+    weights, bh, diagonal, x_out, k1, b1, x1, sa, sb, k_out, b_out, fine, wide, thin, w1, bh1, diagonal1, fine1, thin1, g_out, sems,
+):
+    copies = Copies(sems)
+    flying = []
+    odd_x, odd_y = odd("gx"), odd("gy")
+    lane = iota((64, 128), 1)
+    for n, (array, start, some, room) in enumerate(PACKED):
+        a, b = ya[n], yb[n]
+        left, right = jnp.where(odd_y, a, b), jnp.where(odd_y, b, a)
+        rows_in, out, width, shift = ((k_rows, k_out, KY, 0), (b_rows, b_out, BY, 1))[array]
+        for i in range(some):
+            ahead, behind = turn(right, -room * i, 1), turn(left, 128 - width - room * i, 1)
+            out[shift + start + i, :, 0:128] = rows_in[start + i]
+            out[shift + start + i, :, 128:256] = jnp.where(lane < width, ahead, jnp.where(lane >= 128 - width, behind, 0.0))
+
+    flying.append(copies.start(k_out.at[pl.ds(4, 14)], k_hbm))
+    flying.append(copies.start(b_out.at[pl.ds(5, 12)], b_hbm))
     level = Level(k_out, weights, bh, x_out, None, 1.0, *SHAPE0)
-    level.set_up(1, 17, b_out, diagonal)
-    level.pre(2, 16)
-    level.residue(3, 15, diagonal, fine, 0)
-    for m in range(6):
+    level.set_up(1, 21, b_out, diagonal)
+    level.pre(2, 20)
+    flying.append(copies.start(x_out.at[pl.ds(4, 14)], x_hbm))
+    level.residue(3, 19, diagonal, fine, 0)
+    for m in range(8):
         wide[m] = fine[2 * m] + fine[2 * m + 1]
-    for m in range(8):
-        wide[6 + m] = k_out[2 * m + 1] + k_out[2 * m + 2]
-    matrix = coarsen_matrix(256, 128, 140, 12, 0.125)
-    flat = dot(wide[...].reshape(14 * 64, 256), matrix)
-    thin[...] = flat
-    done = []
-    for m in range(14):
-        done.append(thin[pl.ds(64 * m, 32, stride=2), :] + thin[pl.ds(64 * m + 1, 32, stride=2), :])
-    for m in range(6):
-        b1_out[m] = done[m]
-    for m in range(8):
-        k1_out[m] = done[6 + m]
-    for m in range(5):
-        sa[m] = jnp.where(odd_x, done[m + 1], done[m])
-        sb[m] = jnp.where(odd_x, done[m], done[m + 1])
-    for m in range(6):
-        sa[5 + m] = jnp.where(odd_x, done[8 + m], done[6 + m])
-        sb[5 + m] = jnp.where(odd_x, done[6 + m], done[8 + m])
-
-
-def second_kernel(count, b1, k1, ra, rb, weights, bh, x_out, g_out, k_out, b_out, diagonal, fine, thin):
+    for m in range(10):
+        wide[8 + m] = k_out[2 * m + 1] + k_out[2 * m + 2]
+    thin[...] = dot(wide[...].reshape(18 * 64, 256), coarsen_matrix(256, 128, 140, 12, 0.125))
+    for m in range(18):
+        plane = thin[pl.ds(64 * m, 32, stride=2), :] + thin[pl.ds(64 * m + 1, 32, stride=2), :]
+        if m < 8:
+            b1[1 + m] = plane
+        else:
+            k1[m - 8] = plane
+
+    level = Level(k1, w1, bh1, x1, None, 0.25, *SHAPE1)
+    flying.append(copies.start(k1, k1_hbm))
+    flying.append(copies.start(b1, b1_hbm))
+    level.set_up(1, 9, b1, diagonal1)
+    level.pre(2, 8)
+    flying.append(copies.start(x1, x1_hbm))
+    for n, (ref, to_right, to_left) in enumerate(((x1, 3, 4), (x1, 4, 5), (x1, 5, 6), (b1, 4, 5), (k1, 3, 6))):
+        sa[n] = jnp.where(odd_x, ref[to_left], ref[to_right])
+        sb[n] = jnp.where(odd_x, ref[to_right], ref[to_left])
+    flying.append(copies.start(sa, sa_hbm))
+    flying.append(copies.start(sb, sb_hbm))
+    level.residue(3, 7, diagonal1, fine1, 0)
+    parts = [fine1[0] + fine1[1], fine1[2] + fine1[3], k1[3] + k1[4], k1[5] + k1[6]]
+    thin1[...] = dot(jnp.concatenate(parts, axis=0), coarsen_matrix(128, 128, 64, 0, 0.125))
+    payload = jnp.zeros((16, 128), F32)
+    for n in range(4):
+        part = thin1[pl.ds(32 * n, 16, stride=2), :] + thin1[pl.ds(32 * n + 1, 16, stride=2), :]
+        payload = payload + turn(part, 32 * n, 1)
+    for n in range(count):
+        g_out[n] = payload
+    flying += pieces(PIECES, g_out, g_hbm, copies)
+    for copy in flying:
+        copy.wait()
+
+
+def prepare_kernel(
+    ra_hbm, rb_hbm, k1_hbm, b1_hbm, x1_hbm, k_hbm, b_hbm, x_hbm, w0, bh0, d0, x0, w1, bh1, x1,
+    ra, rb, k1_in, b1_in, x1_in, k0, b0, k1, b1, d1, sems,
+):
     odd_x = odd("gx")
+    copies = Copies(sems)
+    for_level0 = [copies.start(k_hbm, k0), copies.start(b_hbm, b0.at[pl.ds(1, 12)]), copies.start(x_hbm, x0)]
+    for_level1 = [copies.start(*pair) for pair in ((ra_hbm, ra), (rb_hbm, rb), (k1_hbm, k1_in), (b1_hbm, b1_in), (x1_hbm, x1_in))]
+    for copy in for_level1:
+        copy.wait()
     for side in range(2):
 
         def pick(n):
             a, b = ra[n], rb[n]
             return jnp.where(odd_x, a, b) if side == 0 else jnp.where(odd_x, b, a)
 
-        for j in range(6):
-            k_out[j if side == 0 else 10 + j] = pick(5 + j)
-        for j in range(5):
-            b_out[1 + j if side == 0 else 10 + j] = pick(j)
-    for j in range(4):
-        k_out[6 + j] = k1[2 + j]
-        b_out[6 + j] = b1[1 + j]
-
-    level = Level(k_out, weights, bh, x_out, None, 0.25, *SHAPE1)
-    level.set_up(1, 15, b_out, diagonal)
-    level.pre(2, 14)
-    level.residue(6, 10, diagonal, fine, 0)
-    parts = [fine[0] + fine[1], fine[2] + fine[3], k_out[6] + k_out[7], k_out[8] + k_out[9]]
-    matrix = coarsen_matrix(128, 128, 64, 0, 0.125)
-    thin[...] = dot(jnp.concatenate(parts, axis=0), matrix)
-    payload = jnp.zeros((16, 128), F32)
-    for n in range(4):
-        part = thin[pl.ds(32 * n, 16, stride=2), :] + thin[pl.ds(32 * n + 1, 16, stride=2), :]
-        payload = payload + turn(part, 32 * n, 1)
-    for n in range(count):
-        g_out[n] = payload
+        for n in range(3):
+            x1[n if side == 0 else 9 + n] = pick(n)
+        b1[1 if side == 0 else 10] = pick(3)
+        k1[0 if side == 0 else 11] = pick(4)
+    for n in range(6):
+        x1[3 + n] = x1_in[2 + n]
+    for n in range(8):
+        b1[2 + n] = b1_in[1 + n]
+    for n in range(10):
+        k1[1 + n] = k1_in[n]
+    Level(k1, w1, bh1, None, None, 0.25, *SHAPE1).set_up(1, 11, b1, d1)
+    for copy in for_level0:
+        copy.wait()
+    Level(k0, w0, bh0, None, None, 1.0, *SHAPE0).set_up(1, 13, b0, d0)
 
 
 def last_kernel(
-    count, g, ga, gb, w1, bh1, x1, w0, bh0, d0, x0, pressure, residual,
-    k2, b2, w2, bh2, x2, y2, p2, fine2, sums2, coarse2, t1, y1, p1, stack1, t0, y0, p0, stack0,
+    count, w0, bh0, d0, x0, w1, bh1, x1, g, ga, gb, pressure, residual,
+    k2, b2, w2, bh2, x2, y2, p2, fine2, sums2, coarse2, t1, y1, p1, stack1, t0, y0, p0, stack0, pressure_rows, residual_rows, sems,
 ):
+    copies = Copies(sems)
     odd_y = odd("gy")
     me = lax.axis_index("gx")
     lane = iota((16, 128), 1)
@@ -375,63 +419,77 @@
             stack1[pl.ds(32 * m + half, 16, stride=2), :] = x2[20 + m]
     fine = dot(stack1[...], refine_matrix(128, 128, 70, 6))
     for m in range(12):
-        t1[2 + m] = x1[2 + m] + fine[32 * (m // 2) : 32 * (m // 2) + 32]
+        t1[m] = x1[m] + fine[32 * (m // 2) : 32 * (m // 2) + 32]
     level = Level(None, w1, bh1, t1, p1, 0.25, *SHAPE1)
-    level.post(4, 12, y1)
+    level.post(2, 10, y1)
 
     for m in range(8):
         for half in range(2):
-            stack0[pl.ds(64 * m + half, 32, stride=2), :] = t1[4 + m]
+            stack0[pl.ds(64 * m + half, 32, stride=2), :] = t1[2 + m]
     matrix = refine_matrix(128, 256, 140, 12)
     fine = dot(stack0[...], matrix)
     for m in range(14):
         row = (m + 1) // 2
-        t0[2 + m] = x0[2 + m] + fine[64 * row : 64 * row + 64]
+        t0[m] = x0[m] + fine[64 * row : 64 * row + 64]
     level = Level(None, w0, bh0, t0, p0, 1.0, *SHAPE0)
-    level.post(4, 14, y0)
+    level.post(2, 12, y0)
     for i in range(8):
-        q = 5 + i
-        value = t0[q]
-        left = d0[q] * (bh0[q] - value + level.total(t0, q, q - 1, q + 1))
-        pressure[pl.ds(i, 64, stride=8), :] = value[:, 0:128]
-        residual[pl.ds(i, 64, stride=8), :] = left[:, 0:128]
+        pressure_rows[pl.ds(i, 64, stride=8), :] = t0[3 + i, :, 0:128]
+    waits = pieces(PIECES, pressure_rows, pressure, copies)
+    for i in range(8):
+        q = 3 + i
+        value = bh0[q] - t0[q] + level.total(t0, q, q - 1, q + 1)
+        residual_rows[pl.ds(i, 64, stride=8), :] = (d0[q] * value)[:, 0:128]
+    waits += pieces(PIECES, residual_rows, residual, copies)
+    for copy in waits:
+        copy.wait()
 
 
 def on_device(right_side, conductivity):
     count = lax.axis_size("gx")
     b, k = right_side.reshape(512, 128), conductivity.reshape(512, 128)
-    ya, yb, xa, xb = call(pack_kernel, [(2, 64, 128)] * 2 + [(13, 64, 128)] * 2, [], b, k)
+    own, xa, xb = call(
+        strip_kernel, [(2, 8, 64, 128)] + [(KX + BX, 64, 128)] * 2, [(512, 128)] * 2, b, k, hbm_in=2, sems=[(2 * PIECES,)]
+    )
+    xa, xb = swap(xa, "gx", 0), swap(xb, "gx", 1)
+    k_rows, b_rows, ya, yb = call(
+        pack_kernel, [(8 + 2 * KX, 64, 128), (8 + 2 * BX, 64, 128)] + [(len(PACKED), 64, 128)] * 2, [], own, xa, xb
+    )
     ya, yb = swap(ya, "gy", 0), swap(yb, "gy", 1)
-
-    def with_y(strip):
-        strip = lax.dynamic_update_slice(strip, ya, (9, 0, 0))
-        return lax.dynamic_update_slice(strip, yb, (11, 0, 0))
-
-    xa, xb = swap(with_y(xa), "gx", 0), swap(with_y(xb), "gx", 1)
-    rows0, rows1 = (18, 64, 256), (16, 32, 128)
-    w0, bh0, d0, x0, k1, b1, sa, sb = call(
-        first_kernel,
-        [(6,) + rows0, rows0, rows0, rows0, (8, 32, 128), (6, 32, 128), (11, 32, 128), (11, 32, 128)],
-        [rows0, rows0, (12, 64, 256), (14, 64, 256), (14 * 64, 128)],
-        b, k, xa, xb, ya, yb,
+    rows0, rows1, rows2, rows3 = (22, 64, 256), (10, 32, 128), (46, 16, 128), (12, 32, 128)
+    wide0 = (14, 64, 256)
+    k0, b0, x0, k1, b1, x1, sa, sb, g = call(
+        functools.partial(first_kernel, count),
+        [wide0, (12, 64, 256), wide0, rows1, rows1, rows1, (5, 32, 128), (5, 32, 128), (count, 16, 128)],
+        [(6,) + rows0, rows0, rows0, rows0, rows1, rows1, rows1, (5, 32, 128), (5, 32, 128)]
+        + [rows0, rows0, (16, 64, 256), (18, 64, 256), (18 * 64, 128)]
+        + [(6,) + rows1, rows1, rows1, (4, 32, 128), (128, 128), (count, 16, 128)],
+        k_rows, b_rows, ya, yb,
+        hbm_out=9,
+        sems=[(8 + PIECES,)],
     )
     ra, rb = swap(sa, "gx", 0), swap(sb, "gx", 1)
-    w1, bh1, x1, g = call(
-        functools.partial(second_kernel, count),
-        [(6,) + rows1, rows1, rows1, (count, 16, 128)],
-        [rows1, rows1, rows1, (4, 32, 128), (128, 128)],
-        b1, k1, ra, rb,
+    g = lax.all_to_all(g, "gx", 0, 0, tiled=True)
+    g, ra, rb, k0, b0, x0, k1, b1, x1 = lax.optimization_barrier((g, ra, rb, k0, b0, x0, k1, b1, x1))
+    ga, gb = swap(g, "gy", 0), swap(g, "gy", 1)
+    kept = call(
+        prepare_kernel,
+        [(6,) + wide0, wide0, wide0, wide0, (6,) + rows3, rows3, rows3],
+        [(5, 32, 128), (5, 32, 128), rows1, rows1, rows1, wide0, wide0, rows3, rows3, rows3],
+        ra, rb, k1, b1, x1, k0, b0, x0,
+        hbm_in=8,
+        sems=[(8,)],
+        cost=pl.CostEstimate(flops=20_000_000, bytes_accessed=8_000_000, transcendentals=200_000),
     )
-    g = lax.all_to_all(g, "gx", 0, 0, tiled=True)
-    ga, gb = swap(g, "gy", 0), swap(g, "gy", 1)
-    rows2 = (46, 16, 128)
     pressure, residual = call(
         functools.partial(last_kernel, count),
         [(512, 128)] * 2,
         [rows2, rows2, (6,) + rows2, rows2, rows2, rows2, rows2, rows2, rows2, (46 * 16, 128)]
-        + [rows1, rows1, rows1, (6 * 32, 128)]
-        + [rows0, rows0, rows0, (8 * 64, 128)],
-        g, ga, gb, w1, bh1, x1, w0, bh0, d0, x0,
+        + [rows3, rows3, rows3, (6 * 32, 128)]
+        + [wide0, wide0, wide0, (8 * 64, 128), (512, 128), (512, 128)],
+        *kept, g, ga, gb,
+        hbm_out=2,
+        sems=[(2 * PIECES,)],
     )
     return pressure.reshape(64, 8, 128), residual.reshape(64, 8, 128)
 

time: 75.2 us -> 70.4 us (0.936)
  blocking collectives: 25 us -> 0 us
  starting transfers between devices: 20.9 us -> 31.9 us
  Pallas kernels: 10.4 us -> 17.3 us
  waiting for transfers between devices: 16 us -> 19.8 us
  local copies, waits for them, and re-layouts: 1.91 us -> 0.01 us
    all_to_all x1 -> x0, blocking collectives: 25 us -> none  [on_device(): g = lax.all_to_all(g, 'gx', 0, 0, tiled=True)]
    all_to_all x0 -> x1, starting transfers between devices: none -> 14.9 us  [on_device(): g = lax.all_to_all(g, 'gx', 0, 0, tiled=True)]
    pallas_call x4 -> x5, Pallas kernels: 10.4 us -> 17.3 us  [call(): pl.pallas_call(body, out_shape=[pltpu.HBM(s, F32) if n < hbm_out else jax...]
    ppermute x8, starting transfers between devices: 20.9 us -> 17 us  [swap(): return lax.ppermute(value, axis, pairs(lax.axis_size(axis), offset))]
    all_to_all x0 -> x1, waiting for transfers between devices: none -> 3.82 us  [on_device(): g = lax.all_to_all(g, 'gx', 0, 0, tiled=True)]
    unnamed x4, local copies, waits for them, and re-layouts: 1.89 us -> 0.01 us
  transfers between devices with their start and end apart: 8 -> 9, of which waited for: 4 -> 5; matrix products, arithmetic and copies ran while one was open for 0% -> 0% of each run, Pallas kernels for 0% -> 5%
where the time goes in v3:
time: 70.4 us; the launch traced here: 69.9 us
  starting transfers between devices  31.9 us (45%)
  waiting for transfers between devices  19.8 us (28%)
  Pallas kernels  17.3 us (25%)
  between operations  0.9 us (1%)
    pallas_call x5, Pallas kernels, call(): pl.pallas_call(body, out_shape=[pltpu.HBM(s, F32) if n < hbm_out else jax...  17.3 us
    ppermute x8, starting transfers between devices, swap(): return lax.ppermute(value, axis, pairs(lax.axis_size(axis), offset))  17 us
    ppermute x8, waiting for transfers between devices, swap(): return lax.ppermute(value, axis, pairs(lax.axis_size(axis), offset))  15.9 us
    all_to_all x1, starting transfers between devices, on_device(): g = lax.all_to_all(g, 'gx', 0, 0, tiled=True)  14.9 us
    all_to_all x1, waiting for transfers between devices, on_device(): g = lax.all_to_all(g, 'gx', 0, 0, tiled=True)  3.82 us
  transfers between devices with their start and end apart: 9, of which 5 were waited for; matrix products, arithmetic and copies ran while one was open for 0% of the time, Pallas kernels for 5%

profile of v3, /device:TPU:1, one launch (start us, length us, event | category | flops | bytes accessed | tf_op | source)
XLA Modules:
  0.0 69.9 jit_solution(10878096411552587973)
XLA Ops:
  0.6 1.2 %shard_map.41 = (f32[2,8,64,128]{3,2,1,0:T(8,128)S(1)}, f32[13,64,128]{2,1,0:T(8,128)S(1)}, f32[13,64,128]{2,1,0:T(8,128)S(1)}) custom-call(f32[512,128]{1,0:T(8,128)} %bitcast.4, f32[512,128]{1,0:T(8,128)} %bitcast.5), custom_call_target="tpu_custom_call" | custom-call | tf_op jit(solution)/shard_map/pallas_call | solution.py:184
  1.8 2.6 %collective-permute-start = (f32[13,64,128]{2,1,0:T(8,128)S(1)}, f32[13,64,128]{2,1,0:T(8,128)S(1)}, u32[]{:S(2)}, u32[]{:S(2)}) collective-permute-start(f32[13,64,128]{2,1,0:T(8,128)S(1)} %get-tuple-element.37), channel_id=1, source_target_pairs={{0,8},{8,0},{16,24},{24,16},{32,40},{40,32},{48,56},{56,48},{64,72... | collective-permute-start | bytes 1277960 | tf_op jit(solution)/shard_map/ppermute | solution.py:33
  4.4 0.7 collective-permute-start.1
  5.1 7.8 %collective-permute-done.xa = f32[13,64,128]{2,1,0:T(8,128)S(1)} collective-permute-done((f32[13,64,128]{2,1,0:T(8,128)S(1)}, f32[13,64,128]{2,1,0:T(8,128)S(1)}, u32[]{:S(2)}, u32[]{:S(2)}) %collective-permute-start) | collective-permute-done | bytes 426016 | tf_op jit(solution)/shard_map/ppermute | solution.py:33
  12.9 0.0 collective-permute-done.1.xb
  12.9 0.8 %shard_map.42 = (f32[22,64,128]{2,1,0:T(8,128)S(1)}, f32[20,64,128]{2,1,0:T(8,128)S(1)}, f32[5,64,128]{2,1,0:T(8,128)S(1)}, f32[5,64,128]{2,1,0:T(8,128)S(1)}) custom-call(f32[2,8,64,128]{3,2,1,0:T(8,128)S(1)} %get-tuple-element.36.own, f32[13,64,128]{2,1,0:T(8,128)S(1)} %collective-permute-done.xa, f32[13,64,128]{2,1,0:T(8,128)S(1)} %collective-permute-done.1.xb), custom_call_target="tpu_custom_call" | custom-call | tf_op jit(solution)/shard_map/pallas_call | solution.py:184
  13.6 2.4 %collective-permute-start.2 = (f32[5,64,128]{2,1,0:T(8,128)S(1)}, f32[5,64,128]{2,1,0:T(8,128)S(1)}, u32[]{:S(2)}, u32[]{:S(2)}) collective-permute-start(f32[5,64,128]{2,1,0:T(8,128)S(1)} %get-tuple-element.41), channel_id=1, source_target_pairs={{0,1},{1,0},{2,3},{3,2},{4,5},{5,4},{6,7},{7,6},{8,9},{9,8},{10,11... | collective-permute-start | bytes 491528 | tf_op jit(solution)/shard_map/ppermute | solution.py:33
  16.0 3.0 %collective-permute-start.3 = (f32[5,64,128]{2,1,0:T(8,128)S(1)}, f32[5,64,128]{2,1,0:T(8,128)S(1)}, u32[]{:S(2)}, u32[]{:S(2)}) collective-permute-start(f32[5,64,128]{2,1,0:T(8,128)S(1)} %get-tuple-element.42), channel_id=1, source_target_pairs={{1,2},{2,1},{3,4},{4,3},{5,6},{6,5},{9,10},{10,9},{11,12},{12,11},... | collective-permute-start | bytes 491528 | tf_op jit(solution)/shard_map/ppermute | solution.py:33
  19.0 0.0 collective-permute-done.2.ya
  19.0 3.6 %collective-permute-done.3.yb = f32[5,64,128]{2,1,0:T(8,128)S(1)} collective-permute-done((f32[5,64,128]{2,1,0:T(8,128)S(1)}, f32[5,64,128]{2,1,0:T(8,128)S(1)}, u32[]{:S(2)}, u32[]{:S(2)}) %collective-permute-start.3) | collective-permute-done | bytes 163872 | tf_op jit(solution)/shard_map/ppermute | solution.py:33
  22.6 6.5 %shard_map.43 = (f32[14,64,256]{2,1,0:T(8,128)}, f32[12,64,256]{2,1,0:T(8,128)}, f32[14,64,256]{2,1,0:T(8,128)}, f32[10,32,128]{2,1,0:T(8,128)}, f32[10,32,128]{...) custom-call(f32[22,64,128]{2,1,0:T(8,128)S(1)} %get-tuple-element.39, ...), custom_call_target="tpu_custom_call" | custom-call | tf_op jit(solution)/shard_map/pallas_call | solution.py:184
  29.2 14.9 %all-to-all-start = ((f32[32,16,128]{2,1,0:T(8,128)}), f32[32,16,128]{2,1,0:T(8,128)S(1)}, u32[]{:S(2)}, u32[]{:S(2)}) async-start(f32[32,16,128]{2,1,0:T(8,128)} %get-tuple-element.43), calls=%async_computation | async-start | bytes 524288 | tf_op jit(solution)/shard_map/all_to_all | solution.py:472
  44.1 1.3 %collective-permute-start.4 = (f32[5,32,128]{2,1,0:T(8,128)}, f32[5,32,128]{2,1,0:T(8,128)S(1)}, u32[]{:S(2)}, u32[]{:S(2)}) collective-permute-start(f32[5,32,128]{2,1,0:T(8,128)} %get-tuple-element.44), channel_id=1, source_target_pairs={{0,8},{8,0},{16,24},{24,16},{32,40},{40,32},{48,56},{56,48},{64,72... | collective-permute-start | bytes 245768 | tf_op jit(solution)/shard_map/ppermute | solution.py:33
  45.4 0.7 collective-permute-start.5
  46.0 4.0 %collective-permute-done.4.ra_hbm = f32[5,32,128]{2,1,0:T(8,128)S(1)} collective-permute-done((f32[5,32,128]{2,1,0:T(8,128)}, f32[5,32,128]{2,1,0:T(8,128)S(1)}, u32[]{:S(2)}, u32[]{:S(2)}) %collective-permute-start.4) | collective-permute-done | bytes 81952 | tf_op jit(solution)/shard_map/ppermute | solution.py:33
  50.0 0.0 copy-start
  50.0 0.0 collective-permute-done.5.rb_hbm
  50.0 0.0 copy-start.1
  50.0 3.8 %all-to-all-done.g = f32[32,16,128]{2,1,0:T(8,128)S(1)} async-done(((f32[32,16,128]{2,1,0:T(8,128)}), f32[32,16,128]{2,1,0:T(8,128)S(1)}, u32[]{:S(2)}, u32[]{:S(2)}) %all-to-all-start) | async-done | bytes 262176 | tf_op jit(solution)/shard_map/all_to_all | solution.py:472
  53.9 0.0 collective-permute-start.6
  53.9 6.4 %collective-permute-start.7 = (f32[32,16,128]{2,1,0:T(8,128)S(1)}, f32[32,16,128]{2,1,0:T(8,128)S(1)}, u32[]{:S(2)}, u32[]{:S(2)}) collective-permute-start(f32[32,16,128]{2,1,0:T(8,128)S(1)} %all-to-all-done.g), channel_id=1, source_target_pairs={{1,2},{2,1},{3,4},{4,3},{5,6},{6,5},{9,10},{10,9},{11,12},{12,11},... | collective-permute-start | bytes 786440 | tf_op jit(solution)/shard_map/ppermute | solution.py:33
  60.3 0.0 copy-done
  60.3 0.0 copy-done.1
  60.3 3.3 %shard_map.44 = (f32[6,14,64,256]{3,2,1,0:T(8,128)S(1)}, f32[14,64,256]{2,1,0:T(8,128)S(1)}, f32[14,64,256]{2,1,0:T(8,128)S(1)}, f32[14,64,256]{2,1,0:T(8,128)S(...) custom-call(f32[5,32,128]{2,1,0:T(8,128)} %copy-done, ...), custom_call_target="tpu_custom_call" | custom-call | flops 20000000 | bytes 8000000 | tf_op jit(solution)/shard_map/pallas_call | solution.py:184
  63.6 0.0 collective-permute-done.6.ga
  63.6 0.6 collective-permute-done.7.gb
  64.2 5.6 %shard_map.45 = (f32[512,128]{1,0:T(8,128)}, f32[512,128]{1,0:T(8,128)}) custom-call(f32[6,14,64,256]{3,2,1,0:T(8,128)S(1)} %get-tuple-element.60.w0, f32[14,64,256]{2,1,0:T(8,128)S(1)} %get-tuple-element.61.bh0, f32[14,64,256]{2,1,0:T(8,128)S(1)} %get-tuple-element.62.d0, f32[14,64,256]{2,1,0:T(8,128)S(1)} %get-tuple-element.63.x0, ...), custom_call_target="tpu_custom_call" | custom-call | tf_op jit(solution)/shard_map/pallas_call | solution.py:184
Async XLA Ops:
  1.8 11.0 %collective-permute-start = (f32[13,64,128]{2,1,0:T(8,128)S(1)}, f32[13,64,128]{2,1,0:T(8,128)S(1)}, u32[]{:S(2)}, u32[]{:S(2)}) collective-permute-start(f32[13,64,128]{2,1,0:T(8,128)S(1)} %get-tuple-element.37), channel_id=1, source_target_pairs={{0,8},{8,0},{16,24},{24,16},{32,40},{40,32},{48,56},{56,48},{64,72... | collective-permute-start | bytes 1277960 | tf_op jit(solution)/shard_map/ppermute | solution.py:33
  4.4 8.5 %collective-permute-start.1 = (f32[13,64,128]{2,1,0:T(8,128)S(1)}, f32[13,64,128]{2,1,0:T(8,128)S(1)}, u32[]{:S(2)}, u32[]{:S(2)}) collective-permute-start(f32[13,64,128]{2,1,0:T(8,128)S(1)} %get-tuple-element.38), channel_id=1, source_target_pairs={{8,16},{16,8},{24,32},{32,24},{40,48},{48,40},{56,64},{64,56},{72,... | collective-permute-start | bytes 1277960 | tf_op jit(solution)/shard_map/ppermute | solution.py:33
  13.6 5.4 %collective-permute-start.2 = (f32[5,64,128]{2,1,0:T(8,128)S(1)}, f32[5,64,128]{2,1,0:T(8,128)S(1)}, u32[]{:S(2)}, u32[]{:S(2)}) collective-permute-start(f32[5,64,128]{2,1,0:T(8,128)S(1)} %get-tuple-element.41), channel_id=1, source_target_pairs={{0,1},{1,0},{2,3},{3,2},{4,5},{5,4},{6,7},{7,6},{8,9},{9,8},{10,11... | collective-permute-start | bytes 491528 | tf_op jit(solution)/shard_map/ppermute | solution.py:33
  16.0 6.6 %collective-permute-start.3 = (f32[5,64,128]{2,1,0:T(8,128)S(1)}, f32[5,64,128]{2,1,0:T(8,128)S(1)}, u32[]{:S(2)}, u32[]{:S(2)}) collective-permute-start(f32[5,64,128]{2,1,0:T(8,128)S(1)} %get-tuple-element.42), channel_id=1, source_target_pairs={{1,2},{2,1},{3,4},{4,3},{5,6},{6,5},{9,10},{10,9},{11,12},{12,11},... | collective-permute-start | bytes 491528 | tf_op jit(solution)/shard_map/ppermute | solution.py:33
  29.2 24.7 %all-to-all-start = ((f32[32,16,128]{2,1,0:T(8,128)}), f32[32,16,128]{2,1,0:T(8,128)S(1)}, u32[]{:S(2)}, u32[]{:S(2)}) async-start(f32[32,16,128]{2,1,0:T(8,128)} %get-tuple-element.43), calls=%async_computation | async-start | bytes 524288 | tf_op jit(solution)/shard_map/all_to_all | solution.py:472
  44.1 6.0 %collective-permute-start.4 = (f32[5,32,128]{2,1,0:T(8,128)}, f32[5,32,128]{2,1,0:T(8,128)S(1)}, u32[]{:S(2)}, u32[]{:S(2)}) collective-permute-start(f32[5,32,128]{2,1,0:T(8,128)} %get-tuple-element.44), channel_id=1, source_target_pairs={{0,8},{8,0},{16,24},{24,16},{32,40},{40,32},{48,56},{56,48},{64,72... | collective-permute-start | bytes 245768 | tf_op jit(solution)/shard_map/ppermute | solution.py:33
  45.4 4.6 %collective-permute-start.5 = (f32[5,32,128]{2,1,0:T(8,128)}, f32[5,32,128]{2,1,0:T(8,128)S(1)}, u32[]{:S(2)}, u32[]{:S(2)}) collective-permute-start(f32[5,32,128]{2,1,0:T(8,128)} %get-tuple-element.45), channel_id=1, source_target_pairs={{8,16},{16,8},{24,32},{32,24},{40,48},{48,40},{56,64},{64,56},{72,... | collective-permute-start | bytes 245768 | tf_op jit(solution)/shard_map/ppermute | solution.py:33
  50.0 10.3 %copy-start = (f32[5,32,128]{2,1,0:T(8,128)}, f32[5,32,128]{2,1,0:T(8,128)S(1)}, u32[]{:S(2)}) copy-start(f32[5,32,128]{2,1,0:T(8,128)S(1)} %collective-permute-done.4.ra_hbm) | copy-start | bytes 245764
  50.0 10.3 %copy-start.1 = (f32[5,32,128]{2,1,0:T(8,128)}, f32[5,32,128]{2,1,0:T(8,128)S(1)}, u32[]{:S(2)}) copy-start(f32[5,32,128]{2,1,0:T(8,128)S(1)} %collective-permute-done.5.rb_hbm) | copy-start | bytes 245764
  53.9 9.7 %collective-permute-start.6 = (f32[32,16,128]{2,1,0:T(8,128)S(1)}, f32[32,16,128]{2,1,0:T(8,128)S(1)}, u32[]{:S(2)}, u32[]{:S(2)}) collective-permute-start(f32[32,16,128]{2,1,0:T(8,128)S(1)} %all-to-all-done.g), channel_id=1, source_target_pairs={{0,1},{1,0},{2,3},{3,2},{4,5},{5,4},{6,7},{7,6},{8,9},{9,8},{10,11... | collective-permute-start | bytes 786440 | tf_op jit(solution)/shard_map/ppermute | solution.py:33
  53.9 10.3 %collective-permute-start.7 = (f32[32,16,128]{2,1,0:T(8,128)S(1)}, f32[32,16,128]{2,1,0:T(8,128)S(1)}, u32[]{:S(2)}, u32[]{:S(2)}) collective-permute-start(f32[32,16,128]{2,1,0:T(8,128)S(1)} %all-to-all-done.g), channel_id=1, source_target_pairs={{1,2},{2,1},{3,4},{4,3},{5,6},{6,5},{9,10},{10,9},{11,12},{12,11},... | collective-permute-start | bytes 786440 | tf_op jit(solution)/shard_map/ppermute | solution.py:33

commit v4 on v3

--- a/solution.py
+++ b/solution.py
@@ -19,7 +19,8 @@
 PIECES = 4
 
 KX, BX, KY, BY = 7, 6, 13, 12
-PACKED = ((0, 0, 9, 14), (0, 9, 9, 14), (0, 18, 4, 14), (1, 0, 10, 12), (1, 10, 10, 12))
+PACKED_K = ((0, 9, 14), (9, 9, 14), (18, 4, 14))
+PACKED_B = ((0, 10, 12), (10, 10, 12))
 
 
 def pairs(size, offset):
@@ -80,24 +81,29 @@
     return value if shift == 0 else pltpu.roll(value, shift, axis=axis)
 
 
+def edged(value, axis, top):
+    depth = value.shape[axis]
+    cut = functools.partial(lax.slice_in_dim, value, axis=axis)
+    index = iota(value.shape[:axis] + (8,) + value.shape[axis + 1 :], axis)
+    if top:
+        edge = jnp.where(index == 7, 0.0, cut(depth - 8, depth))
+        return edge if depth == 8 else jnp.concatenate([cut(0, depth - 8), edge], axis=axis)
+    edge = jnp.where(index == 0, 0.0, cut(0, 8))
+    return edge if depth == 8 else jnp.concatenate([edge, cut(8, depth)], axis=axis)
+
+
 def weights_row(kc, km, kp, factor):
-    half = 0.5 * factor
     axis = kc.ndim - 2
-    depth = kc.shape[axis]
-    z = iota(kc.shape, axis)
-    low, top = z == 0, z == depth - 1
-    up = half * (kc + jnp.where(top, 0.0, turn(kc, -1, axis)))
-    down = half * (kc + jnp.where(low, 0.0, turn(kc, 1, axis)))
-    ahead = half * (kc + turn(kc, -1, axis + 1))
-    behind = half * (kc + turn(kc, 1, axis + 1))
-    right = half * (kc + kp)
-    left = half * (kc + km)
-    diagonal = up + down + ahead + behind + right + left
+    up = kc + edged(turn(kc, -1, axis), axis, True)
+    down = kc + edged(turn(kc, 1, axis), axis, False)
+    ahead = kc + turn(kc, -1, axis + 1)
+    behind = kc + turn(kc, 1, axis + 1)
+    right = kc + kp
+    left = kc + km
+    diagonal = (up + down) + (ahead + behind) + (right + left)
     inverse = jnp.where(kc > 0, 1.0 / diagonal, 0.0)
-    up = jnp.where(top, 0.0, up)
-    down = jnp.where(low, 0.0, down)
-    weights = [w * inverse for w in (left, right, behind, ahead, down, up)]
-    return weights, inverse, diagonal
+    weights = [w * inverse for w in (left, right, behind, ahead, edged(down, axis, False), edged(up, axis, True))]
+    return weights, inverse * (2.0 / factor), diagonal * (0.5 * factor)
 
 
 def neighbour_sum(weights, below, centre, above):
@@ -129,13 +135,17 @@
     def rows(self, low, high, body):
         rows(low, high, body, self.chunk, self.unroll)
 
-    def set_up(self, low, high, b, diagonal):
+    def set_up(self, low, high, b=None, diagonal=None, inverses=None):
         def body(q, below, above):
             weights, inverse, diag = weights_row(self.k[q], self.k[below], self.k[above], self.factor)
             for n in range(6):
                 self.weights[n, q] = weights[n]
-            self.bh[q] = b[q] * inverse
-            diagonal[q] = diag
+            if b is not None:
+                self.bh[q] = b[q] * inverse
+            if inverses is not None:
+                inverses[q] = inverse
+            if diagonal is not None:
+                diagonal[q] = diag
 
         self.rows(low, high, body)
 
@@ -212,43 +222,38 @@
     return [copies.start(source.at[pl.ds(i * size, size)], target.at[pl.ds(i * size, size)]) for i in range(n)]
 
 
-def strip_kernel(b_any, k_any, own, xa, xb, b_ref, k_ref, sems):
+def strip_kernel(k_any, b_any, own_k, own_b, xka, xkb, xba, xbb, k_ref, b_ref, sems):
     odd_x = odd("gx")
-    arrays = ((k_ref, KX), (b_ref, BX))
     copies = Copies(sems)
     waits = [pieces(PIECES, k_any, k_ref, copies), pieces(PIECES, b_any, b_ref, copies)]
-    at = 0
-    for n, (ref, width) in enumerate(arrays):
+    for n, (ref, own, xa, xb, width) in enumerate(((k_ref, own_k, xka, xkb, KX), (b_ref, own_b, xba, xbb, BX))):
         for copy in waits[n]:
             copy.wait()
         planes = [ref[pl.ds(i, 64, stride=8), :] for i in range(8)]
         for i in range(8):
-            own[n, i] = planes[i]
+            own[i] = planes[i]
         for i in range(width):
             first, last = planes[i], planes[8 - width + i]
-            xa[at] = jnp.where(odd_x, first, last)
-            xb[at] = jnp.where(odd_x, last, first)
-            at += 1
-
-
-def pack_kernel(own, xa, xb, k_out, b_out, ya, yb):
+            xa[i] = jnp.where(odd_x, first, last)
+            xb[i] = jnp.where(odd_x, last, first)
+
+
+def pack_kernel(packed, width, own, xa, xb, rows_out, ya, yb):
     odd_x, odd_y = odd("gx"), odd("gy")
     lane = iota((64, 128), 1)
-    for n in range(KX + BX):
+    halo = xa.shape[0]
+    planes = [None] * (8 + 2 * halo)
+    for n in range(halo):
         a, b = xa[n], xb[n]
-        left, right = jnp.where(odd_x, a, b), jnp.where(odd_x, b, a)
-        if n < KX:
-            k_out[n], k_out[8 + KX + n] = left, right
-        else:
-            b_out[n - KX], b_out[8 + BX + n - KX] = left, right
+        planes[n], planes[8 + halo + n] = jnp.where(odd_x, a, b), jnp.where(odd_x, b, a)
     for i in range(8):
-        k_out[KX + i] = own[0, i]
-        b_out[BX + i] = own[1, i]
-    for n, (array, start, count, room) in enumerate(PACKED):
-        ref, width = ((k_out, KY), (b_out, BY))[array]
+        planes[halo + i] = own[i]
+    for n, plane in enumerate(planes):
+        rows_out[n] = plane
+    for n, (start, count, room) in enumerate(packed):
         first, last = jnp.zeros((64, 128), F32), jnp.zeros((64, 128), F32)
         for i in range(count):
-            plane = ref[start + i]
+            plane = planes[start + i]
             here = (lane >= room * i) & (lane < room * i + width)
             first = jnp.where(here, turn(plane, room * i, 1), first)
             last = jnp.where(here, turn(plane, room * i + width, 1), last)
@@ -256,46 +261,62 @@
         yb[n] = jnp.where(odd_y, last, first)
 
 
-def first_kernel(
-    count, k_rows, b_rows, ya, yb, k_hbm, b_hbm, x_hbm, k1_hbm, b1_hbm, x1_hbm, sa_hbm, sb_hbm, g_hbm,
-    weights, bh, diagonal, x_out, k1, b1, x1, sa, sb, k_out, b_out, fine, wide, thin, w1, bh1, diagonal1, fine1, thin1, g_out, sems,
+def outer_columns(packed, width, ya, yb):
+    odd_y = odd("gy")
+    lane = iota((64, 128), 1)
+    for n, (start, count, room) in enumerate(packed):
+        a, b = ya[n], yb[n]
+        left, right = jnp.where(odd_y, a, b), jnp.where(odd_y, b, a)
+        for i in range(count):
+            ahead, behind = turn(right, -room * i, 1), turn(left, 128 - width - room * i, 1)
+            yield start + i, jnp.where(lane < width, ahead, jnp.where(lane >= 128 - width, behind, 0.0))
+
+
+def weights_kernel(
+    k_rows, ya, yb, k_hbm, k1_hbm, weights, inverse, diagonal, k1, w1, inverse1, diagonal1, k_out, wide, thin, sems,
 ):
     copies = Copies(sems)
-    flying = []
-    odd_x, odd_y = odd("gx"), odd("gy")
-    lane = iota((64, 128), 1)
-    for n, (array, start, some, room) in enumerate(PACKED):
-        a, b = ya[n], yb[n]
-        left, right = jnp.where(odd_y, a, b), jnp.where(odd_y, b, a)
-        rows_in, out, width, shift = ((k_rows, k_out, KY, 0), (b_rows, b_out, BY, 1))[array]
-        for i in range(some):
-            ahead, behind = turn(right, -room * i, 1), turn(left, 128 - width - room * i, 1)
-            out[shift + start + i, :, 0:128] = rows_in[start + i]
-            out[shift + start + i, :, 128:256] = jnp.where(lane < width, ahead, jnp.where(lane >= 128 - width, behind, 0.0))
-
-    flying.append(copies.start(k_out.at[pl.ds(4, 14)], k_hbm))
-    flying.append(copies.start(b_out.at[pl.ds(5, 12)], b_hbm))
-    level = Level(k_out, weights, bh, x_out, None, 1.0, *SHAPE0)
-    level.set_up(1, 21, b_out, diagonal)
+    for q, outer in outer_columns(PACKED_K, KY, ya, yb):
+        k_out[q, :, 0:128] = k_rows[q]
+        k_out[q, :, 128:256] = outer
+    flying = [copies.start(k_out.at[pl.ds(4, 14)], k_hbm)]
+    for m in range(10):
+        wide[m] = k_out[2 * m + 1] + k_out[2 * m + 2]
+    thin[...] = dot(wide[...].reshape(10 * 64, 256), coarsen_matrix(256, 128, 140, 12, 0.125))
+    for m in range(10):
+        k1[m] = thin[pl.ds(64 * m, 32, stride=2), :] + thin[pl.ds(64 * m + 1, 32, stride=2), :]
+    flying.append(copies.start(k1, k1_hbm))
+    Level(k_out, weights, None, None, None, 1.0, *SHAPE0).set_up(1, 21, None, diagonal, inverse)
+    Level(k1, w1, None, None, None, 0.25, *SHAPE1).set_up(1, 9, None, diagonal1, inverse1)
+    for copy in flying:
+        copy.wait()
+
+
+def first_kernel(
+    count, b_rows, ya, yb, weights, inverse, diagonal, k1, w1, inverse1, diagonal1,
+    bh_hbm, x_hbm, b1_hbm, x1_hbm, sa_hbm, sb_hbm, g_hbm,
+    bh, x_out, b1, bh1, x1, sa, sb, fine, wide, thin, fine1, thin1, g_out, sems,
+):
+    odd_x = odd("gx")
+    copies = Copies(sems)
+    for n, outer in outer_columns(PACKED_B, BY, ya, yb):
+        q = n + 1
+        bh[q, :, 0:128] = b_rows[n] * inverse[q, :, 0:128]
+        bh[q, :, 128:256] = outer * inverse[q, :, 128:256]
+    flying = [copies.start(bh.at[pl.ds(5, 12)], bh_hbm)]
+    level = Level(None, weights, bh, x_out, None, 1.0, *SHAPE0)
     level.pre(2, 20)
     flying.append(copies.start(x_out.at[pl.ds(4, 14)], x_hbm))
     level.residue(3, 19, diagonal, fine, 0)
     for m in range(8):
         wide[m] = fine[2 * m] + fine[2 * m + 1]
-    for m in range(10):
-        wide[8 + m] = k_out[2 * m + 1] + k_out[2 * m + 2]
-    thin[...] = dot(wide[...].reshape(18 * 64, 256), coarsen_matrix(256, 128, 140, 12, 0.125))
-    for m in range(18):
-        plane = thin[pl.ds(64 * m, 32, stride=2), :] + thin[pl.ds(64 * m + 1, 32, stride=2), :]
-        if m < 8:
-            b1[1 + m] = plane
-        else:
-            k1[m - 8] = plane
-
-    level = Level(k1, w1, bh1, x1, None, 0.25, *SHAPE1)
-    flying.append(copies.start(k1, k1_hbm))
+    thin[...] = dot(wide[...].reshape(8 * 64, 256), coarsen_matrix(256, 128, 140, 12, 0.125))
+    for m in range(8):
+        b1[1 + m] = thin[pl.ds(64 * m, 32, stride=2), :] + thin[pl.ds(64 * m + 1, 32, stride=2), :]
+        bh1[1 + m] = b1[1 + m] * inverse1[1 + m]
     flying.append(copies.start(b1, b1_hbm))
-    level.set_up(1, 9, b1, diagonal1)
+
+    level = Level(None, w1, bh1, x1, None, 0.25, *SHAPE1)
     level.pre(2, 8)
     flying.append(copies.start(x1, x1_hbm))
     for n, (ref, to_right, to_left) in enumerate(((x1, 3, 4), (x1, 4, 5), (x1, 5, 6), (b1, 4, 5), (k1, 3, 6))):
@@ -318,12 +339,12 @@
 
 
 def prepare_kernel(
-    ra_hbm, rb_hbm, k1_hbm, b1_hbm, x1_hbm, k_hbm, b_hbm, x_hbm, w0, bh0, d0, x0, w1, bh1, x1,
-    ra, rb, k1_in, b1_in, x1_in, k0, b0, k1, b1, d1, sems,
+    ra_hbm, rb_hbm, k1_hbm, b1_hbm, x1_hbm, k_hbm, bh_hbm, x_hbm, w0, bh0, d0, x0, w1, bh1, x1,
+    ra, rb, k1_in, b1_in, x1_in, k0, k1, b1, sems,
 ):
     odd_x = odd("gx")
     copies = Copies(sems)
-    for_level0 = [copies.start(k_hbm, k0), copies.start(b_hbm, b0.at[pl.ds(1, 12)]), copies.start(x_hbm, x0)]
+    for_level0 = [copies.start(k_hbm, k0), copies.start(bh_hbm, bh0.at[pl.ds(1, 12)]), copies.start(x_hbm, x0)]
     for_level1 = [copies.start(*pair) for pair in ((ra_hbm, ra), (rb_hbm, rb), (k1_hbm, k1_in), (b1_hbm, b1_in), (x1_hbm, x1_in))]
     for copy in for_level1:
         copy.wait()
@@ -343,10 +364,10 @@
         b1[2 + n] = b1_in[1 + n]
     for n in range(10):
         k1[1 + n] = k1_in[n]
-    Level(k1, w1, bh1, None, None, 0.25, *SHAPE1).set_up(1, 11, b1, d1)
+    Level(k1, w1, bh1, None, None, 0.25, *SHAPE1).set_up(1, 11, b1)
     for copy in for_level0:
         copy.wait()
-    Level(k0, w0, bh0, None, None, 1.0, *SHAPE0).set_up(1, 13, b0, d0)
+    Level(k0, w0, None, None, None, 1.0, *SHAPE0).set_up(1, 13, None, d0)
 
 
 def last_kernel(
@@ -448,35 +469,57 @@
 def on_device(right_side, conductivity):
     count = lax.axis_size("gx")
     b, k = right_side.reshape(512, 128), conductivity.reshape(512, 128)
-    own, xa, xb = call(
-        strip_kernel, [(2, 8, 64, 128)] + [(KX + BX, 64, 128)] * 2, [(512, 128)] * 2, b, k, hbm_in=2, sems=[(2 * PIECES,)]
+    plane = (64, 128)
+    own_k, own_b, xka, xkb, xba, xbb = call(
+        strip_kernel,
+        [(8,) + plane] * 2 + [(KX,) + plane] * 2 + [(BX,) + plane] * 2,
+        [(512, 128)] * 2,
+        k, b,
+        hbm_in=2,
+        sems=[(2 * PIECES,)],
     )
-    xa, xb = swap(xa, "gx", 0), swap(xb, "gx", 1)
-    k_rows, b_rows, ya, yb = call(
-        pack_kernel, [(8 + 2 * KX, 64, 128), (8 + 2 * BX, 64, 128)] + [(len(PACKED), 64, 128)] * 2, [], own, xa, xb
-    )
-    ya, yb = swap(ya, "gy", 0), swap(yb, "gy", 1)
+    xka, xkb = swap(xka, "gx", 0), swap(xkb, "gx", 1)
+    xba, xbb = swap(xba, "gx", 0), swap(xbb, "gx", 1)
+
+    def packed(own, xa, xb, pack, width):
+        rows_out, ya, yb = call(
+            functools.partial(pack_kernel, pack, width),
+            [(8 + 2 * xa.shape[0],) + plane] + [(len(pack),) + plane] * 2,
+            [],
+            own, xa, xb,
+            cost=pl.CostEstimate(flops=1_000_000, bytes_accessed=2_000_000, transcendentals=0),
+        )
+        return rows_out, swap(ya, "gy", 0), swap(yb, "gy", 1)
+
     rows0, rows1, rows2, rows3 = (22, 64, 256), (10, 32, 128), (46, 16, 128), (12, 32, 128)
     wide0 = (14, 64, 256)
-    k0, b0, x0, k1, b1, x1, sa, sb, g = call(
+    k0, k1, *about_k = call(
+        weights_kernel,
+        [wide0, rows1, (6,) + rows0, rows0, rows0, rows1, (6,) + rows1, rows1, rows1],
+        [rows0, (10, 64, 256), (10 * 64, 128)],
+        *packed(own_k, xka, xkb, PACKED_K, KY),
+        hbm_out=2,
+        sems=[(2,)],
+        cost=pl.CostEstimate(flops=20_000_000, bytes_accessed=8_000_000, transcendentals=300_000),
+    )
+    bh0, x0, b1, x1, sa, sb, g = call(
         functools.partial(first_kernel, count),
-        [wide0, (12, 64, 256), wide0, rows1, rows1, rows1, (5, 32, 128), (5, 32, 128), (count, 16, 128)],
-        [(6,) + rows0, rows0, rows0, rows0, rows1, rows1, rows1, (5, 32, 128), (5, 32, 128)]
-        + [rows0, rows0, (16, 64, 256), (18, 64, 256), (18 * 64, 128)]
-        + [(6,) + rows1, rows1, rows1, (4, 32, 128), (128, 128), (count, 16, 128)],
-        k_rows, b_rows, ya, yb,
-        hbm_out=9,
-        sems=[(8 + PIECES,)],
+        [(12, 64, 256), wide0, rows1, rows1, (5, 32, 128), (5, 32, 128), (count, 16, 128)],
+        [rows0, rows0, rows1, rows1, rows1, (5, 32, 128), (5, 32, 128)]
+        + [(16, 64, 256), (8, 64, 256), (8 * 64, 128), (4, 32, 128), (128, 128), (count, 16, 128)],
+        *packed(own_b, xba, xbb, PACKED_B, BY), *about_k,
+        hbm_out=7,
+        sems=[(6 + PIECES,)],
     )
     ra, rb = swap(sa, "gx", 0), swap(sb, "gx", 1)
     g = lax.all_to_all(g, "gx", 0, 0, tiled=True)
-    g, ra, rb, k0, b0, x0, k1, b1, x1 = lax.optimization_barrier((g, ra, rb, k0, b0, x0, k1, b1, x1))
+    g, ra, rb, k0, bh0, x0, k1, b1, x1 = lax.optimization_barrier((g, ra, rb, k0, bh0, x0, k1, b1, x1))
     ga, gb = swap(g, "gy", 0), swap(g, "gy", 1)
     kept = call(
         prepare_kernel,
         [(6,) + wide0, wide0, wide0, wide0, (6,) + rows3, rows3, rows3],
-        [(5, 32, 128), (5, 32, 128), rows1, rows1, rows1, wide0, wide0, rows3, rows3, rows3],
-        ra, rb, k1, b1, x1, k0, b0, x0,
+        [(5, 32, 128), (5, 32, 128), rows1, rows1, rows1, wide0, rows3, rows3],
+        ra, rb, k1, b1, x1, k0, bh0, x0,
         hbm_in=8,
         sems=[(8,)],
         cost=pl.CostEstimate(flops=20_000_000, bytes_accessed=8_000_000, transcendentals=200_000),

time: 70.4 us -> 67 us (0.952)
  waiting for transfers between devices: 19.8 us -> 10.8 us
  starting transfers between devices: 31.9 us -> 37.9 us
    ppermute x8 -> x12, waiting for transfers between devices: 15.9 us -> 7.16 us  [swap(): return lax.ppermute(value, axis, pairs(lax.axis_size(axis), offset))]
    ppermute x8 -> x12, starting transfers between devices: 17 us -> 22.5 us  [swap(): return lax.ppermute(value, axis, pairs(lax.axis_size(axis), offset))]
    pallas_call x5 -> x7, Pallas kernels: 17.3 us -> 16.9 us  [call(): pl.pallas_call(body, out_shape=[pltpu.HBM(s, F32) if n < hbm_out else jax...]
  transfers between devices with their start and end apart: 9 -> 13, of which waited for: 5 -> 3; matrix products, arithmetic and copies ran while one was open for 0% -> 0% of each run, Pallas kernels for 5% -> 10%
where the time goes in v4:
time: 67 us; the launch traced here: 66.6 us
  starting transfers between devices  37.9 us (57%)
  Pallas kernels  16.9 us (25%)
  waiting for transfers between devices  10.8 us (16%)
  between operations  0.99 us (1%)
    ppermute x12, starting transfers between devices, swap(): return lax.ppermute(value, axis, pairs(lax.axis_size(axis), offset))  22.5 us
    pallas_call x7, Pallas kernels, call(): pl.pallas_call(body, out_shape=[pltpu.HBM(s, F32) if n < hbm_out else jax...  16.9 us
    all_to_all x1, starting transfers between devices, on_device(): g = lax.all_to_all(g, 'gx', 0, 0, tiled=True)  15.3 us
    ppermute x12, waiting for transfers between devices, swap(): return lax.ppermute(value, axis, pairs(lax.axis_size(axis), offset))  7.16 us
    all_to_all x1, waiting for transfers between devices, on_device(): g = lax.all_to_all(g, 'gx', 0, 0, tiled=True)  3.68 us
  transfers between devices with their start and end apart: 13, of which 3 were waited for; matrix products, arithmetic and copies ran while one was open for 0% of the time, Pallas kernels for 10%

profile of v4, /device:TPU:1, one launch (start us, length us, event | category | flops | bytes accessed | tf_op | source)
XLA Modules:
  0.0 66.6 jit_solution(15960499574059626180)
XLA Ops:
  0.6 1.2 %shard_map.41 = (f32[8,64,128]{2,1,0:T(8,128)S(1)}, f32[8,64,128]{2,1,0:T(8,128)S(1)}, f32[7,64,128]{2,1,0:T(8,128)S(1)}, f32[7,64,128]{2,1,0:T(8,128)S(1)}, f32...) custom-call(f32[512,128]{1,0:T(8,128)} %bitcast.4, f32[512,128]{1,0:T(8,128)} %bitcast.5), custom_call_target="tpu_custom_call" | custom-call | tf_op jit(solution)/shard_map/pallas_call | solution.py:194
  1.8 2.6 %collective-permute-start.4 = (f32[7,64,128]{2,1,0:T(8,128)S(1)}, f32[7,64,128]{2,1,0:T(8,128)S(1)}, u32[]{:S(2)}, u32[]{:S(2)}) collective-permute-start(f32[7,64,128]{2,1,0:T(8,128)S(1)} %get-tuple-element.55), channel_id=1, source_target_pairs={{0,8},{8,0},{16,24},{24,16},{32,40},{40,32},{48,56},{56,48},{64,72... | collective-permute-start | bytes 688136 | tf_op jit(solution)/shard_map/ppermute | solution.py:34
  4.4 0.7 collective-permute-start.5
  5.1 4.6 %collective-permute-start = (f32[6,64,128]{2,1,0:T(8,128)S(1)}, f32[6,64,128]{2,1,0:T(8,128)S(1)}, u32[]{:S(2)}, u32[]{:S(2)}) collective-permute-start(f32[6,64,128]{2,1,0:T(8,128)S(1)} %get-tuple-element.49), channel_id=1, source_target_pairs={{0,8},{8,0},{16,24},{24,16},{32,40},{40,32},{48,56},{56,48},{64,72... | collective-permute-start | bytes 589832 | tf_op jit(solution)/shard_map/ppermute | solution.py:34
  9.6 0.7 collective-permute-start.1
  10.3 0.0 collective-permute-done.4.xa
  10.3 0.0 collective-permute-done.5.xb
  10.3 0.4 shard_map.43
  10.8 1.6 %collective-permute-start.6 = (f32[3,64,128]{2,1,0:T(8,128)S(1)}, f32[3,64,128]{2,1,0:T(8,128)S(1)}, u32[]{:S(2)}, u32[]{:S(2)}) collective-permute-start(f32[3,64,128]{2,1,0:T(8,128)S(1)} %get-tuple-element.58), channel_id=1, source_target_pairs={{0,1},{1,0},{2,3},{3,2},{4,5},{5,4},{6,7},{7,6},{8,9},{9,8},{10,11... | collective-permute-start | bytes 294920 | tf_op jit(solution)/shard_map/ppermute | solution.py:34
  12.4 3.0 %collective-permute-start.7 = (f32[3,64,128]{2,1,0:T(8,128)S(1)}, f32[3,64,128]{2,1,0:T(8,128)S(1)}, u32[]{:S(2)}, u32[]{:S(2)}) collective-permute-start(f32[3,64,128]{2,1,0:T(8,128)S(1)} %get-tuple-element.59), channel_id=1, source_target_pairs={{1,2},{2,1},{3,4},{4,3},{5,6},{6,5},{9,10},{10,9},{11,12},{12,11},... | collective-permute-start | bytes 294920 | tf_op jit(solution)/shard_map/ppermute | solution.py:34
  15.4 0.0 collective-permute-done.xa
  15.4 0.0 collective-permute-done.1.xb
  15.4 0.4 shard_map.42
  15.8 0.2 collective-permute-start.2
  16.0 3.4 %collective-permute-start.3 = (f32[2,64,128]{2,1,0:T(8,128)S(1)}, f32[2,64,128]{2,1,0:T(8,128)S(1)}, u32[]{:S(2)}, u32[]{:S(2)}) collective-permute-start(f32[2,64,128]{2,1,0:T(8,128)S(1)} %get-tuple-element.53), channel_id=1, source_target_pairs={{1,2},{2,1},{3,4},{4,3},{5,6},{6,5},{9,10},{10,9},{11,12},{12,11},... | collective-permute-start | bytes 196616 | tf_op jit(solution)/shard_map/ppermute | solution.py:34
  19.4 0.0 collective-permute-done.6.ya
  19.5 0.0 collective-permute-done.7.yb
  19.5 2.8 %shard_map.44 = (f32[14,64,256]{2,1,0:T(8,128)}, f32[10,32,128]{2,1,0:T(8,128)}, f32[6,22,64,256]{3,2,1,0:T(8,128)S(1)}, f32[22,64,256]{2,1,0:T(8,128)S(1)}, f32...) custom-call(f32[22,64,128]{2,1,0:T(8,128)S(1)} %get-tuple-element.57, ...), custom_call_target="tpu_custom_call" | custom-call | flops 20000000 | bytes 8000000 | tf_op jit(solution)/shard_map/pallas_call | solution.py:194
  22.3 0.0 collective-permute-done.2.ya
  22.3 0.0 collective-permute-done.3.yb
  22.3 3.6 %shard_map.45 = (f32[12,64,256]{2,1,0:T(8,128)}, f32[14,64,256]{2,1,0:T(8,128)}, f32[10,32,128]{2,1,0:T(8,128)}, f32[10,32,128]{2,1,0:T(8,128)}, f32[5,32,128]{2...) custom-call(f32[20,64,128]{2,1,0:T(8,128)S(1)} %get-tuple-element.51.b_rows, ...), custom_call_target="tpu_custom_call" | custom-call | tf_op jit(solution)/shard_map/pallas_call | solution.py:194
  25.9 15.3 %all-to-all-start = ((f32[32,16,128]{2,1,0:T(8,128)}), f32[32,16,128]{2,1,0:T(8,128)S(1)}, u32[]{:S(2)}, u32[]{:S(2)}) async-start(f32[32,16,128]{2,1,0:T(8,128)} %get-tuple-element.67), calls=%async_computation | async-start | bytes 524288 | tf_op jit(solution)/shard_map/all_to_all | solution.py:515
  41.2 1.3 %collective-permute-start.8 = (f32[5,32,128]{2,1,0:T(8,128)}, f32[5,32,128]{2,1,0:T(8,128)S(1)}, u32[]{:S(2)}, u32[]{:S(2)}) collective-permute-start(f32[5,32,128]{2,1,0:T(8,128)} %get-tuple-element.68), channel_id=1, source_target_pairs={{0,8},{8,0},{16,24},{24,16},{32,40},{40,32},{48,56},{56,48},{64,72... | collective-permute-start | bytes 245768 | tf_op jit(solution)/shard_map/ppermute | solution.py:34
  42.5 0.7 collective-permute-start.9
  43.2 6.4 %collective-permute-done.8.ra_hbm = f32[5,32,128]{2,1,0:T(8,128)S(1)} collective-permute-done((f32[5,32,128]{2,1,0:T(8,128)}, f32[5,32,128]{2,1,0:T(8,128)S(1)}, u32[]{:S(2)}, u32[]{:S(2)}) %collective-permute-start.8) | collective-permute-done | bytes 81952 | tf_op jit(solution)/shard_map/ppermute | solution.py:34
  49.5 0.0 copy-start
  49.5 0.0 collective-permute-done.9.rb_hbm
  49.5 0.0 copy-start.1
  49.5 3.7 %all-to-all-done.g = f32[32,16,128]{2,1,0:T(8,128)S(1)} async-done(((f32[32,16,128]{2,1,0:T(8,128)}), f32[32,16,128]{2,1,0:T(8,128)S(1)}, u32[]{:S(2)}, u32[]{:S(2)}) %all-to-all-start) | async-done | bytes 262176 | tf_op jit(solution)/shard_map/all_to_all | solution.py:515
  53.2 3.6 %collective-permute-start.11 = (f32[32,16,128]{2,1,0:T(8,128)S(1)}, f32[32,16,128]{2,1,0:T(8,128)S(1)}, u32[]{:S(2)}, u32[]{:S(2)}) collective-permute-start(f32[32,16,128]{2,1,0:T(8,128)S(1)} %all-to-all-done.g), channel_id=1, source_target_pairs={{1,2},{2,1},{3,4},{4,3},{5,6},{6,5},{9,10},{10,9},{11,12},{12,11},... | collective-permute-start | bytes 786440 | tf_op jit(solution)/shard_map/ppermute | solution.py:34
  56.8 0.3 collective-permute-start.10
  57.1 0.0 copy-done
  57.1 0.0 copy-done.1
  57.1 3.0 %shard_map.46 = (f32[6,14,64,256]{3,2,1,0:T(8,128)S(1)}, f32[14,64,256]{2,1,0:T(8,128)S(1)}, f32[14,64,256]{2,1,0:T(8,128)S(1)}, f32[14,64,256]{2,1,0:T(8,128)S(...) custom-call(f32[5,32,128]{2,1,0:T(8,128)} %copy-done, ...), custom_call_target="tpu_custom_call" | custom-call | flops 20000000 | bytes 8000000 | tf_op jit(solution)/shard_map/pallas_call | solution.py:194
  60.1 0.8 %collective-permute-done.11.gb = f32[32,16,128]{2,1,0:T(8,128)S(1)} collective-permute-done((f32[32,16,128]{2,1,0:T(8,128)S(1)}, f32[32,16,128]{2,1,0:T(8,128)S(1)}, u32[]{:S(2)}, u32[]{:S(2)}) %collective-permute-start.11) | collective-permute-done | bytes 262176 | tf_op jit(solution)/shard_map/ppermute | solution.py:34
  60.9 0.0 collective-permute-done.10.ga
  60.9 5.5 %shard_map.47 = (f32[512,128]{1,0:T(8,128)}, f32[512,128]{1,0:T(8,128)}) custom-call(f32[6,14,64,256]{3,2,1,0:T(8,128)S(1)} %get-tuple-element.84.w0, f32[14,64,256]{2,1,0:T(8,128)S(1)} %get-tuple-element.85.bh0, f32[14,64,256]{2,1,0:T(8,128)S(1)} %get-tuple-element.86.d0, f32[14,64,256]{2,1,0:T(8,128)S(1)} %get-tuple-element.87.x0, ...), custom_call_target="tpu_custom_call" | custom-call | tf_op jit(solution)/shard_map/pallas_call | solution.py:194
Async XLA Ops:
  1.8 8.5 %collective-permute-start.4 = (f32[7,64,128]{2,1,0:T(8,128)S(1)}, f32[7,64,128]{2,1,0:T(8,128)S(1)}, u32[]{:S(2)}, u32[]{:S(2)}) collective-permute-start(f32[7,64,128]{2,1,0:T(8,128)S(1)} %get-tuple-element.55), channel_id=1, source_target_pairs={{0,8},{8,0},{16,24},{24,16},{32,40},{40,32},{48,56},{56,48},{64,72... | collective-permute-start | bytes 688136 | tf_op jit(solution)/shard_map/ppermute | solution.py:34
  4.4 5.9 %collective-permute-start.5 = (f32[7,64,128]{2,1,0:T(8,128)S(1)}, f32[7,64,128]{2,1,0:T(8,128)S(1)}, u32[]{:S(2)}, u32[]{:S(2)}) collective-permute-start(f32[7,64,128]{2,1,0:T(8,128)S(1)} %get-tuple-element.56), channel_id=1, source_target_pairs={{8,16},{16,8},{24,32},{32,24},{40,48},{48,40},{56,64},{64,56},{72,... | collective-permute-start | bytes 688136 | tf_op jit(solution)/shard_map/ppermute | solution.py:34
  5.1 10.4 %collective-permute-start = (f32[6,64,128]{2,1,0:T(8,128)S(1)}, f32[6,64,128]{2,1,0:T(8,128)S(1)}, u32[]{:S(2)}, u32[]{:S(2)}) collective-permute-start(f32[6,64,128]{2,1,0:T(8,128)S(1)} %get-tuple-element.49), channel_id=1, source_target_pairs={{0,8},{8,0},{16,24},{24,16},{32,40},{40,32},{48,56},{56,48},{64,72... | collective-permute-start | bytes 589832 | tf_op jit(solution)/shard_map/ppermute | solution.py:34
  9.6 5.8 %collective-permute-start.1 = (f32[6,64,128]{2,1,0:T(8,128)S(1)}, f32[6,64,128]{2,1,0:T(8,128)S(1)}, u32[]{:S(2)}, u32[]{:S(2)}) collective-permute-start(f32[6,64,128]{2,1,0:T(8,128)S(1)} %get-tuple-element.50), channel_id=1, source_target_pairs={{8,16},{16,8},{24,32},{32,24},{40,48},{48,40},{56,64},{64,56},{72,... | collective-permute-start | bytes 589832 | tf_op jit(solution)/shard_map/ppermute | solution.py:34
  10.8 8.7 %collective-permute-start.6 = (f32[3,64,128]{2,1,0:T(8,128)S(1)}, f32[3,64,128]{2,1,0:T(8,128)S(1)}, u32[]{:S(2)}, u32[]{:S(2)}) collective-permute-start(f32[3,64,128]{2,1,0:T(8,128)S(1)} %get-tuple-element.58), channel_id=1, source_target_pairs={{0,1},{1,0},{2,3},{3,2},{4,5},{5,4},{6,7},{7,6},{8,9},{9,8},{10,11... | collective-permute-start | bytes 294920 | tf_op jit(solution)/shard_map/ppermute | solution.py:34
  12.4 7.1 %collective-permute-start.7 = (f32[3,64,128]{2,1,0:T(8,128)S(1)}, f32[3,64,128]{2,1,0:T(8,128)S(1)}, u32[]{:S(2)}, u32[]{:S(2)}) collective-permute-start(f32[3,64,128]{2,1,0:T(8,128)S(1)} %get-tuple-element.59), channel_id=1, source_target_pairs={{1,2},{2,1},{3,4},{4,3},{5,6},{6,5},{9,10},{10,9},{11,12},{12,11},... | collective-permute-start | bytes 294920 | tf_op jit(solution)/shard_map/ppermute | solution.py:34
  15.8 6.4 %collective-permute-start.2 = (f32[2,64,128]{2,1,0:T(8,128)S(1)}, f32[2,64,128]{2,1,0:T(8,128)S(1)}, u32[]{:S(2)}, u32[]{:S(2)}) collective-permute-start(f32[2,64,128]{2,1,0:T(8,128)S(1)} %get-tuple-element.52), channel_id=1, source_target_pairs={{0,1},{1,0},{2,3},{3,2},{4,5},{5,4},{6,7},{7,6},{8,9},{9,8},{10,11... | collective-permute-start | bytes 196616 | tf_op jit(solution)/shard_map/ppermute | solution.py:34
  16.0 6.3 %collective-permute-start.3 = (f32[2,64,128]{2,1,0:T(8,128)S(1)}, f32[2,64,128]{2,1,0:T(8,128)S(1)}, u32[]{:S(2)}, u32[]{:S(2)}) collective-permute-start(f32[2,64,128]{2,1,0:T(8,128)S(1)} %get-tuple-element.53), channel_id=1, source_target_pairs={{1,2},{2,1},{3,4},{4,3},{5,6},{6,5},{9,10},{10,9},{11,12},{12,11},... | collective-permute-start | bytes 196616 | tf_op jit(solution)/shard_map/ppermute | solution.py:34
  25.9 27.4 %all-to-all-start = ((f32[32,16,128]{2,1,0:T(8,128)}), f32[32,16,128]{2,1,0:T(8,128)S(1)}, u32[]{:S(2)}, u32[]{:S(2)}) async-start(f32[32,16,128]{2,1,0:T(8,128)} %get-tuple-element.67), calls=%async_computation | async-start | bytes 524288 | tf_op jit(solution)/shard_map/all_to_all | solution.py:515
  41.2 8.3 %collective-permute-start.8 = (f32[5,32,128]{2,1,0:T(8,128)}, f32[5,32,128]{2,1,0:T(8,128)S(1)}, u32[]{:S(2)}, u32[]{:S(2)}) collective-permute-start(f32[5,32,128]{2,1,0:T(8,128)} %get-tuple-element.68), channel_id=1, source_target_pairs={{0,8},{8,0},{16,24},{24,16},{32,40},{40,32},{48,56},{56,48},{64,72... | collective-permute-start | bytes 245768 | tf_op jit(solution)/shard_map/ppermute | solution.py:34
  42.5 7.0 %collective-permute-start.9 = (f32[5,32,128]{2,1,0:T(8,128)}, f32[5,32,128]{2,1,0:T(8,128)S(1)}, u32[]{:S(2)}, u32[]{:S(2)}) collective-permute-start(f32[5,32,128]{2,1,0:T(8,128)} %get-tuple-element.69), channel_id=1, source_target_pairs={{8,16},{16,8},{24,32},{32,24},{40,48},{48,40},{56,64},{64,56},{72,... | collective-permute-start | bytes 245768 | tf_op jit(solution)/shard_map/ppermute | solution.py:34
  49.5 7.6 %copy-start = (f32[5,32,128]{2,1,0:T(8,128)}, f32[5,32,128]{2,1,0:T(8,128)S(1)}, u32[]{:S(2)}) copy-start(f32[5,32,128]{2,1,0:T(8,128)S(1)} %collective-permute-done.8.ra_hbm) | copy-start | bytes 245764
  49.5 7.6 %copy-start.1 = (f32[5,32,128]{2,1,0:T(8,128)}, f32[5,32,128]{2,1,0:T(8,128)S(1)}, u32[]{:S(2)}) copy-start(f32[5,32,128]{2,1,0:T(8,128)S(1)} %collective-permute-done.9.rb_hbm) | copy-start | bytes 245764
  53.2 7.7 %collective-permute-start.11 = (f32[32,16,128]{2,1,0:T(8,128)S(1)}, f32[32,16,128]{2,1,0:T(8,128)S(1)}, u32[]{:S(2)}, u32[]{:S(2)}) collective-permute-start(f32[32,16,128]{2,1,0:T(8,128)S(1)} %all-to-all-done.g), channel_id=1, source_target_pairs={{1,2},{2,1},{3,4},{4,3},{5,6},{6,5},{9,10},{10,9},{11,12},{12,11},... | collective-permute-start | bytes 786440 | tf_op jit(solution)/shard_map/ppermute | solution.py:34
  56.8 4.1 %collective-permute-start.10 = (f32[32,16,128]{2,1,0:T(8,128)S(1)}, f32[32,16,128]{2,1,0:T(8,128)S(1)}, u32[]{:S(2)}, u32[]{:S(2)}) collective-permute-start(f32[32,16,128]{2,1,0:T(8,128)S(1)} %all-to-all-done.g), channel_id=1, source_target_pairs={{0,1},{1,0},{2,3},{3,2},{4,5},{5,4},{6,7},{7,6},{8,9},{9,8},{10,11... | collective-permute-start | bytes 786440 | tf_op jit(solution)/shard_map/ppermute | solution.py:34

commit v5 on v4

--- a/solution.py
+++ b/solution.py
@@ -15,6 +15,8 @@
 VMEM_LIMIT = 28 * 1024 * 1024
 
 SHAPE0, SHAPE1, SHAPE2, WINDOW_UNROLL = (1,True), (4, True), (8, True), True
+
+WINDOW = 23
 
 PIECES = 4
 
@@ -222,20 +224,17 @@
     return [copies.start(source.at[pl.ds(i * size, size)], target.at[pl.ds(i * size, size)]) for i in range(n)]
 
 
-def strip_kernel(k_any, b_any, own_k, own_b, xka, xkb, xba, xbb, k_ref, b_ref, sems):
+def strip_kernel(width, source, own, xa, xb, ref, sems):
     odd_x = odd("gx")
-    copies = Copies(sems)
-    waits = [pieces(PIECES, k_any, k_ref, copies), pieces(PIECES, b_any, b_ref, copies)]
-    for n, (ref, own, xa, xb, width) in enumerate(((k_ref, own_k, xka, xkb, KX), (b_ref, own_b, xba, xbb, BX))):
-        for copy in waits[n]:
-            copy.wait()
-        planes = [ref[pl.ds(i, 64, stride=8), :] for i in range(8)]
-        for i in range(8):
-            own[i] = planes[i]
-        for i in range(width):
-            first, last = planes[i], planes[8 - width + i]
-            xa[i] = jnp.where(odd_x, first, last)
-            xb[i] = jnp.where(odd_x, last, first)
+    for copy in pieces(PIECES, source, ref, Copies(sems)):
+        copy.wait()
+    planes = [ref[pl.ds(i, 64, stride=8), :] for i in range(8)]
+    for i in range(8):
+        own[i] = planes[i]
+    for i in range(width):
+        first, last = planes[i], planes[8 - width + i]
+        xa[i] = jnp.where(odd_x, first, last)
+        xb[i] = jnp.where(odd_x, last, first)
 
 
 def pack_kernel(packed, width, own, xa, xb, rows_out, ya, yb):
@@ -303,10 +302,9 @@
         q = n + 1
         bh[q, :, 0:128] = b_rows[n] * inverse[q, :, 0:128]
         bh[q, :, 128:256] = outer * inverse[q, :, 128:256]
-    flying = [copies.start(bh.at[pl.ds(5, 12)], bh_hbm)]
+    flying = []
     level = Level(None, weights, bh, x_out, None, 1.0, *SHAPE0)
     level.pre(2, 20)
-    flying.append(copies.start(x_out.at[pl.ds(4, 14)], x_hbm))
     level.residue(3, 19, diagonal, fine, 0)
     for m in range(8):
         wide[m] = fine[2 * m] + fine[2 * m + 1]
@@ -314,16 +312,15 @@
     for m in range(8):
         b1[1 + m] = thin[pl.ds(64 * m, 32, stride=2), :] + thin[pl.ds(64 * m + 1, 32, stride=2), :]
         bh1[1 + m] = b1[1 + m] * inverse1[1 + m]
+    flying.append(copies.start(bh.at[pl.ds(5, 12)], bh_hbm))
+    flying.append(copies.start(x_out.at[pl.ds(4, 14)], x_hbm))
     flying.append(copies.start(b1, b1_hbm))
 
     level = Level(None, w1, bh1, x1, None, 0.25, *SHAPE1)
     level.pre(2, 8)
-    flying.append(copies.start(x1, x1_hbm))
-    for n, (ref, to_right, to_left) in enumerate(((x1, 3, 4), (x1, 4, 5), (x1, 5, 6), (b1, 4, 5), (k1, 3, 6))):
-        sa[n] = jnp.where(odd_x, ref[to_left], ref[to_right])
-        sb[n] = jnp.where(odd_x, ref[to_right], ref[to_left])
-    flying.append(copies.start(sa, sa_hbm))
-    flying.append(copies.start(sb, sb_hbm))
+    taken = ((x1, 3, 4), (x1, 4, 5), (x1, 5, 6), (b1, 4, 5), (k1, 3, 6))
+    pack_outer([jnp.where(odd_x, ref[to_left], ref[to_right]) for ref, to_right, to_left in taken], sa)
+    pack_outer([jnp.where(odd_x, ref[to_right], ref[to_left]) for ref, to_right, to_left in taken], sb)
     level.residue(3, 7, diagonal1, fine1, 0)
     parts = [fine1[0] + fine1[1], fine1[2] + fine1[3], k1[3] + k1[4], k1[5] + k1[6]]
     thin1[...] = dot(jnp.concatenate(parts, axis=0), coarsen_matrix(128, 128, 64, 0, 0.125))
@@ -334,8 +331,28 @@
     for n in range(count):
         g_out[n] = payload
     flying += pieces(PIECES, g_out, g_hbm, copies)
+    flying += [copies.start(*pair) for pair in ((x1, x1_hbm), (sa, sa_hbm), (sb, sb_hbm))]
     for copy in flying:
         copy.wait()
+
+
+def pack_outer(rows_in, out):
+    lane = iota((32, 128), 1)
+    out[0] = jnp.where(lane < 64, rows_in[0], turn(rows_in[1], 64, 1))
+    out[1] = jnp.where(lane < 64, rows_in[2], turn(rows_in[3], 64, 1))
+    last = rows_in[4]
+    for n, row in enumerate(rows_in):
+        at = 64 + 12 * n
+        last = jnp.where((lane >= at) & (lane < at + 6), turn(row, 12 * n, 1), last)
+        last = jnp.where((lane >= at + 6) & (lane < at + 12), turn(row, 12 * n - 52, 1), last)
+    out[2] = last
+
+
+def unpack_outer(tiles, n):
+    lane = iota((32, 128), 1)
+    own = turn(tiles[n // 2], 64 * (n % 2), 1)
+    right, left = turn(tiles[2], -12 * n, 1), turn(tiles[2], 52 - 12 * n, 1)
+    return jnp.where(lane < 64, own, jnp.where(lane < 70, right, jnp.where(lane >= 122, left, 0.0)))
 
 
 def prepare_kernel(
@@ -349,15 +366,11 @@
     for copy in for_level1:
         copy.wait()
     for side in range(2):
-
-        def pick(n):
-            a, b = ra[n], rb[n]
-            return jnp.where(odd_x, a, b) if side == 0 else jnp.where(odd_x, b, a)
-
+        tiles = [jnp.where(odd_x, ra[n], rb[n]) if side == 0 else jnp.where(odd_x, rb[n], ra[n]) for n in range(3)]
         for n in range(3):
-            x1[n if side == 0 else 9 + n] = pick(n)
-        b1[1 if side == 0 else 10] = pick(3)
-        k1[0 if side == 0 else 11] = pick(4)
+            x1[n if side == 0 else 9 + n] = unpack_outer(tiles, n)
+        b1[1 if side == 0 else 10] = unpack_outer(tiles, 3)
+        k1[0 if side == 0 else 11] = unpack_outer(tiles, 4)
     for n in range(6):
         x1[3 + n] = x1_in[2 + n]
     for n in range(8):
@@ -370,6 +383,10 @@
     Level(k0, w0, None, None, None, 1.0, *SHAPE0).set_up(1, 13, None, d0)
 
 
+def window_start(me, count, window):
+    return jnp.clip(me - WINDOW // 2, 0, count - window)
+
+
 def last_kernel(
     count, w0, bh0, d0, x0, w1, bh1, x1, g, ga, gb, pressure, residual,
     k2, b2, w2, bh2, x2, y2, p2, fine2, sums2, coarse2, t1, y1, p1, stack1, t0, y0, p0, stack0, pressure_rows, residual_rows, sems,
@@ -379,10 +396,12 @@
     me = lax.axis_index("gx")
     lane = iota((16, 128), 1)
 
+    start = window_start(me, count, g.shape[0])
+
     def window(j, carry):
-        device = me - 11 + j
+        device = me - WINDOW // 2 + j
         inside = (device >= 0) & (device < count)
-        at = jnp.clip(device, 0, count - 1)
+        at = jnp.clip(device - start, 0, g.shape[0] - 1)
         own, a, b = g[at], ga[at], gb[at]
         left, right = jnp.where(odd_y, a, b), jnp.where(odd_y, b, a)
         for n, out in ((0, b2), (2, k2)):
@@ -392,7 +411,7 @@
                 out[2 * j + m] = jnp.where(inside, value, 0.0)
         return carry
 
-    lax.fori_loop(0, 23, window, 0, unroll=WINDOW_UNROLL)
+    lax.fori_loop(0, WINDOW, window, 0, unroll=WINDOW_UNROLL)
     level = Level(k2, w2, bh2, x2, p2, 0.0625, *SHAPE2)
     level.set_up(1, 45, b2, y2)
     level.pre(2, 44)
@@ -459,8 +478,8 @@
     waits = pieces(PIECES, pressure_rows, pressure, copies)
     for i in range(8):
         q = 3 + i
-        value = bh0[q] - t0[q] + level.total(t0, q, q - 1, q + 1)
-        residual_rows[pl.ds(i, 64, stride=8), :] = (d0[q] * value)[:, 0:128]
+        value = d0[q] * (bh0[q] - t0[q] + level.total(t0, q, q - 1, q + 1))
+        residual_rows[pl.ds(i, 64, stride=8), :] = value[:, 0:128]
     waits += pieces(PIECES, residual_rows, residual, copies)
     for copy in waits:
         copy.wait()
@@ -470,16 +489,20 @@
     count = lax.axis_size("gx")
     b, k = right_side.reshape(512, 128), conductivity.reshape(512, 128)
     plane = (64, 128)
-    own_k, own_b, xka, xkb, xba, xbb = call(
-        strip_kernel,
-        [(8,) + plane] * 2 + [(KX,) + plane] * 2 + [(BX,) + plane] * 2,
-        [(512, 128)] * 2,
-        k, b,
-        hbm_in=2,
-        sems=[(2 * PIECES,)],
-    )
-    xka, xkb = swap(xka, "gx", 0), swap(xkb, "gx", 1)
-    xba, xbb = swap(xba, "gx", 0), swap(xbb, "gx", 1)
+
+    def strips(value, width):
+        own, xa, xb = call(
+            functools.partial(strip_kernel, width),
+            [(8,) + plane] + [(width,) + plane] * 2,
+            [(512, 128)],
+            value,
+            hbm_in=1,
+            sems=[(PIECES,)],
+        )
+        return own, swap(xa, "gx", 0), swap(xb, "gx", 1)
+
+    own_k, xka, xkb = strips(k, KX)
+    own_b, xba, xbb = strips(b, BX)
 
     def packed(own, xa, xb, pack, width):
         rows_out, ya, yb = call(
@@ -504,8 +527,8 @@
     )
     bh0, x0, b1, x1, sa, sb, g = call(
         functools.partial(first_kernel, count),
-        [(12, 64, 256), wide0, rows1, rows1, (5, 32, 128), (5, 32, 128), (count, 16, 128)],
-        [rows0, rows0, rows1, rows1, rows1, (5, 32, 128), (5, 32, 128)]
+        [(12, 64, 256), wide0, rows1, rows1, (3, 32, 128), (3, 32, 128), (count, 16, 128)],
+        [rows0, rows0, rows1, rows1, rows1, (3, 32, 128), (3, 32, 128)]
         + [(16, 64, 256), (8, 64, 256), (8 * 64, 128), (4, 32, 128), (128, 128), (count, 16, 128)],
         *packed(own_b, xba, xbb, PACKED_B, BY), *about_k,
         hbm_out=7,
@@ -514,11 +537,13 @@
     ra, rb = swap(sa, "gx", 0), swap(sb, "gx", 1)
     g = lax.all_to_all(g, "gx", 0, 0, tiled=True)
     g, ra, rb, k0, bh0, x0, k1, b1, x1 = lax.optimization_barrier((g, ra, rb, k0, bh0, x0, k1, b1, x1))
+    window = min(WINDOW, count)
+    g = lax.dynamic_slice_in_dim(g, window_start(lax.axis_index("gx"), count, window), window)
     ga, gb = swap(g, "gy", 0), swap(g, "gy", 1)
     kept = call(
         prepare_kernel,
         [(6,) + wide0, wide0, wide0, wide0, (6,) + rows3, rows3, rows3],
-        [(5, 32, 128), (5, 32, 128), rows1, rows1, rows1, wide0, rows3, rows3],
+        [(3, 32, 128), (3, 32, 128), rows1, rows1, rows1, wide0, rows3, rows3],
         ra, rb, k1, b1, x1, k0, bh0, x0,
         hbm_in=8,
         sems=[(8,)],

time: 67 us -> 66 us (0.985)
  starting transfers between devices: 37.9 us -> 35.8 us
  Pallas kernels: 16.9 us -> 18.3 us
  waiting for transfers between devices: 10.8 us -> 10 us
    all_to_all x1, starting transfers between devices: 15.3 us -> 13.3 us  [on_device(): g = lax.all_to_all(g, 'gx', 0, 0, tiled=True)]
    ppermute x12, waiting for transfers between devices: 7.16 us -> 5.68 us  [swap(): return lax.ppermute(value, axis, pairs(lax.axis_size(axis), offset))]
    pallas_call x7 -> x8, Pallas kernels: 16.9 us -> 18.3 us  [call(): pl.pallas_call(body, out_shape=[pltpu.HBM(s, F32) if n < hbm_out else jax...]
    all_to_all x1, waiting for transfers between devices: 3.68 us -> 4.36 us  [on_device(): g = lax.all_to_all(g, 'gx', 0, 0, tiled=True)]
  transfers between devices with their start and end apart: 13 -> 13, of which waited for: 3 -> 2; matrix products, arithmetic and copies ran while one was open for 0% -> 0% of each run, Pallas kernels for 10% -> 12%
where the time goes in v5:
time: 66 us; the launch traced here: 65.2 us
  starting transfers between devices  35.8 us (54%)
  Pallas kernels  18.3 us (28%)
  waiting for transfers between devices  10 us (15%)
  between operations  1.02 us (2%)
    ppermute x12, starting transfers between devices, swap(): return lax.ppermute(value, axis, pairs(lax.axis_size(axis), offset))  22.6 us
    pallas_call x8, Pallas kernels, call(): pl.pallas_call(body, out_shape=[pltpu.HBM(s, F32) if n < hbm_out else jax...  18.3 us
    all_to_all x1, starting transfers between devices, on_device(): g = lax.all_to_all(g, 'gx', 0, 0, tiled=True)  13.3 us
    ppermute x12, waiting for transfers between devices, swap(): return lax.ppermute(value, axis, pairs(lax.axis_size(axis), offset))  5.68 us
    all_to_all x1, waiting for transfers between devices, on_device(): g = lax.all_to_all(g, 'gx', 0, 0, tiled=True)  4.36 us
  transfers between devices with their start and end apart: 13, of which 2 were waited for; matrix products, arithmetic and copies ran while one was open for 0% of the time, Pallas kernels for 12%

profile of v5, /device:TPU:1, one launch (start us, length us, event | category | flops | bytes accessed | tf_op | source)
XLA Modules:
  0.0 65.2 jit_solution(6853726526483648420)
XLA Ops:
  0.6 1.0 %shard_map.43 = (f32[8,64,128]{2,1,0:T(8,128)S(1)}, f32[7,64,128]{2,1,0:T(8,128)S(1)}, f32[7,64,128]{2,1,0:T(8,128)S(1)}) custom-call(f32[512,128]{1,0:T(8,128)} %bitcast.4), custom_call_target="tpu_custom_call" | custom-call | tf_op jit(solution)/shard_map/pallas_call | solution.py:196
  1.7 2.6 %collective-permute-start.4 = (f32[7,64,128]{2,1,0:T(8,128)S(1)}, f32[7,64,128]{2,1,0:T(8,128)S(1)}, u32[]{:S(2)}, u32[]{:S(2)}) collective-permute-start(f32[7,64,128]{2,1,0:T(8,128)S(1)} %get-tuple-element.55), channel_id=1, source_target_pairs={{0,8},{8,0},{16,24},{24,16},{32,40},{40,32},{48,56},{56,48},{64,72... | collective-permute-start | bytes 688136 | tf_op jit(solution)/shard_map/ppermute | solution.py:36
  4.2 0.7 %collective-permute-start.5 = (f32[7,64,128]{2,1,0:T(8,128)S(1)}, f32[7,64,128]{2,1,0:T(8,128)S(1)}, u32[]{:S(2)}, u32[]{:S(2)}) collective-permute-start(f32[7,64,128]{2,1,0:T(8,128)S(1)} %get-tuple-element.56), channel_id=1, source_target_pairs={{8,16},{16,8},{24,32},{32,24},{40,48},{48,40},{56,64},{64,56},{72,... | collective-permute-start | bytes 688136 | tf_op jit(solution)/shard_map/ppermute | solution.py:36
  4.9 1.0 %shard_map.41 = (f32[8,64,128]{2,1,0:T(8,128)S(1)}, f32[6,64,128]{2,1,0:T(8,128)S(1)}, f32[6,64,128]{2,1,0:T(8,128)S(1)}) custom-call(f32[512,128]{1,0:T(8,128)} %bitcast.5), custom_call_target="tpu_custom_call" | custom-call | tf_op jit(solution)/shard_map/pallas_call | solution.py:196
  5.9 4.6 %collective-permute-start = (f32[6,64,128]{2,1,0:T(8,128)S(1)}, f32[6,64,128]{2,1,0:T(8,128)S(1)}, u32[]{:S(2)}, u32[]{:S(2)}) collective-permute-start(f32[6,64,128]{2,1,0:T(8,128)S(1)} %get-tuple-element.49), channel_id=1, source_target_pairs={{0,8},{8,0},{16,24},{24,16},{32,40},{40,32},{48,56},{56,48},{64,72... | collective-permute-start | bytes 589832 | tf_op jit(solution)/shard_map/ppermute | solution.py:36
  10.5 0.7 %collective-permute-start.1 = (f32[6,64,128]{2,1,0:T(8,128)S(1)}, f32[6,64,128]{2,1,0:T(8,128)S(1)}, u32[]{:S(2)}, u32[]{:S(2)}) collective-permute-start(f32[6,64,128]{2,1,0:T(8,128)S(1)} %get-tuple-element.50), channel_id=1, source_target_pairs={{8,16},{16,8},{24,32},{32,24},{40,48},{48,40},{56,64},{64,56},{72,... | collective-permute-start | bytes 589832 | tf_op jit(solution)/shard_map/ppermute | solution.py:36
  11.2 0.0 collective-permute-done.4.xa
  11.2 0.0 collective-permute-done.5.xb
  11.2 0.4 shard_map.44
  11.7 1.6 %collective-permute-start.6 = (f32[3,64,128]{2,1,0:T(8,128)S(1)}, f32[3,64,128]{2,1,0:T(8,128)S(1)}, u32[]{:S(2)}, u32[]{:S(2)}) collective-permute-start(f32[3,64,128]{2,1,0:T(8,128)S(1)} %get-tuple-element.58), channel_id=1, source_target_pairs={{0,1},{1,0},{2,3},{3,2},{4,5},{5,4},{6,7},{7,6},{8,9},{9,8},{10,11... | collective-permute-start | bytes 294920 | tf_op jit(solution)/shard_map/ppermute | solution.py:36
  13.3 3.0 %collective-permute-start.7 = (f32[3,64,128]{2,1,0:T(8,128)S(1)}, f32[3,64,128]{2,1,0:T(8,128)S(1)}, u32[]{:S(2)}, u32[]{:S(2)}) collective-permute-start(f32[3,64,128]{2,1,0:T(8,128)S(1)} %get-tuple-element.59), channel_id=1, source_target_pairs={{1,2},{2,1},{3,4},{4,3},{5,6},{6,5},{9,10},{10,9},{11,12},{12,11},... | collective-permute-start | bytes 294920 | tf_op jit(solution)/shard_map/ppermute | solution.py:36
  16.3 0.0 collective-permute-done.xa
  16.3 0.0 collective-permute-done.1.xb
  16.3 0.4 shard_map.42
  16.7 0.2 collective-permute-start.2
  16.9 3.4 %collective-permute-start.3 = (f32[2,64,128]{2,1,0:T(8,128)S(1)}, f32[2,64,128]{2,1,0:T(8,128)S(1)}, u32[]{:S(2)}, u32[]{:S(2)}) collective-permute-start(f32[2,64,128]{2,1,0:T(8,128)S(1)} %get-tuple-element.53), channel_id=1, source_target_pairs={{1,2},{2,1},{3,4},{4,3},{5,6},{6,5},{9,10},{10,9},{11,12},{12,11},... | collective-permute-start | bytes 196616 | tf_op jit(solution)/shard_map/ppermute | solution.py:36
  20.3 0.0 collective-permute-done.6.ya
  20.3 0.0 collective-permute-done.7.yb
  20.3 2.8 %shard_map.45 = (f32[14,64,256]{2,1,0:T(8,128)}, f32[10,32,128]{2,1,0:T(8,128)}, f32[6,22,64,256]{3,2,1,0:T(8,128)S(1)}, f32[22,64,256]{2,1,0:T(8,128)S(1)}, f32...) custom-call(f32[22,64,128]{2,1,0:T(8,128)S(1)} %get-tuple-element.57, ...), custom_call_target="tpu_custom_call" | custom-call | flops 20000000 | bytes 8000000 | tf_op jit(solution)/shard_map/pallas_call | solution.py:196
  23.2 0.0 collective-permute-done.2.ya
  23.2 0.0 collective-permute-done.3.yb
  23.2 3.7 %shard_map.46 = (f32[12,64,256]{2,1,0:T(8,128)}, f32[14,64,256]{2,1,0:T(8,128)}, f32[10,32,128]{2,1,0:T(8,128)}, f32[10,32,128]{2,1,0:T(8,128)}, f32[3,32,128]{2...) custom-call(f32[20,64,128]{2,1,0:T(8,128)S(1)} %get-tuple-element.51.b_rows, ...), custom_call_target="tpu_custom_call" | custom-call | tf_op jit(solution)/shard_map/pallas_call | solution.py:196
  26.9 13.3 %all-to-all-start = ((f32[32,16,128]{2,1,0:T(8,128)}), f32[32,16,128]{2,1,0:T(8,128)S(1)}, u32[]{:S(2)}, u32[]{:S(2)}) async-start(f32[32,16,128]{2,1,0:T(8,128)} %get-tuple-element.67), calls=%async_computation | async-start | bytes 524288 | tf_op jit(solution)/shard_map/all_to_all | solution.py:538
  40.2 1.3 %collective-permute-start.8 = (f32[3,32,128]{2,1,0:T(8,128)}, f32[3,32,128]{2,1,0:T(8,128)S(1)}, u32[]{:S(2)}, u32[]{:S(2)}) collective-permute-start(f32[3,32,128]{2,1,0:T(8,128)} %get-tuple-element.68), channel_id=1, source_target_pairs={{0,8},{8,0},{16,24},{24,16},{32,40},{40,32},{48,56},{56,48},{64,72... | collective-permute-start | bytes 147464 | tf_op jit(solution)/shard_map/ppermute | solution.py:36
  41.5 0.7 collective-permute-start.9
  42.2 5.7 %collective-permute-done.8.ra_hbm = f32[3,32,128]{2,1,0:T(8,128)S(1)} collective-permute-done((f32[3,32,128]{2,1,0:T(8,128)}, f32[3,32,128]{2,1,0:T(8,128)S(1)}, u32[]{:S(2)}, u32[]{:S(2)}) %collective-permute-start.8) | collective-permute-done | bytes 49184 | tf_op jit(solution)/shard_map/ppermute | solution.py:36
  47.8 0.0 copy-start
  47.8 0.0 collective-permute-done.9.rb_hbm
  47.8 0.0 copy-start.1
  47.8 4.4 %all-to-all-done = f32[32,16,128]{2,1,0:T(8,128)S(1)} async-done(((f32[32,16,128]{2,1,0:T(8,128)}), f32[32,16,128]{2,1,0:T(8,128)S(1)}, u32[]{:S(2)}, u32[]{:S(2)}) %all-to-all-start) | async-done | bytes 262176 | tf_op jit(solution)/shard_map/all_to_all | solution.py:538
  52.2 0.1 collective-permute-start.10
  52.3 3.8 %collective-permute-start.11 = (f32[23,16,128]{2,1,0:T(8,128)S(1)}, f32[23,16,128]{2,1,0:T(8,128)S(1)}, u32[]{:S(2)}, u32[]{:S(2)}) collective-permute-start(f32[23,16,128]{2,1,0:T(8,128)S(1)} %constant_dynamic-slice_fusion.g), channel_id=1, source_target_pairs={{1,2},{2,1},{3,4},{4,3},{5,6},{6,5},{9,10},{10,9},{11,12},{12,11},... | collective-permute-start | bytes 565256 | tf_op jit(solution)/shard_map/ppermute | solution.py:36
  56.1 0.0 copy-done
  56.1 0.0 copy-done.1
  56.1 3.1 %shard_map.47 = (f32[6,14,64,256]{3,2,1,0:T(8,128)S(1)}, f32[14,64,256]{2,1,0:T(8,128)S(1)}, f32[14,64,256]{2,1,0:T(8,128)S(1)}, f32[14,64,256]{2,1,0:T(8,128)S(...) custom-call(f32[3,32,128]{2,1,0:T(8,128)} %copy-done, ...), custom_call_target="tpu_custom_call" | custom-call | flops 20000000 | bytes 8000000 | tf_op jit(solution)/shard_map/pallas_call | solution.py:196
  59.2 0.0 collective-permute-done.10.ga
  59.2 0.0 collective-permute-done.11.gb
  59.2 5.8 %shard_map.48 = (f32[512,128]{1,0:T(8,128)}, f32[512,128]{1,0:T(8,128)}) custom-call(f32[6,14,64,256]{3,2,1,0:T(8,128)S(1)} %get-tuple-element.84.w0, f32[14,64,256]{2,1,0:T(8,128)S(1)} %get-tuple-element.85.bh0, f32[14,64,256]{2,1,0:T(8,128)S(1)} %get-tuple-element.86.d0, f32[14,64,256]{2,1,0:T(8,128)S(1)} %get-tuple-element.87.x0, ...), custom_call_target="tpu_custom_call" | custom-call | tf_op jit(solution)/shard_map/pallas_call | solution.py:196
  (1 shorter events, 0.0 us)
Async XLA Ops:
  1.7 9.5 %collective-permute-start.4 = (f32[7,64,128]{2,1,0:T(8,128)S(1)}, f32[7,64,128]{2,1,0:T(8,128)S(1)}, u32[]{:S(2)}, u32[]{:S(2)}) collective-permute-start(f32[7,64,128]{2,1,0:T(8,128)S(1)} %get-tuple-element.55), channel_id=1, source_target_pairs={{0,8},{8,0},{16,24},{24,16},{32,40},{40,32},{48,56},{56,48},{64,72... | collective-permute-start | bytes 688136 | tf_op jit(solution)/shard_map/ppermute | solution.py:36
  4.2 7.0 %collective-permute-start.5 = (f32[7,64,128]{2,1,0:T(8,128)S(1)}, f32[7,64,128]{2,1,0:T(8,128)S(1)}, u32[]{:S(2)}, u32[]{:S(2)}) collective-permute-start(f32[7,64,128]{2,1,0:T(8,128)S(1)} %get-tuple-element.56), channel_id=1, source_target_pairs={{8,16},{16,8},{24,32},{32,24},{40,48},{48,40},{56,64},{64,56},{72,... | collective-permute-start | bytes 688136 | tf_op jit(solution)/shard_map/ppermute | solution.py:36
  5.9 10.4 %collective-permute-start = (f32[6,64,128]{2,1,0:T(8,128)S(1)}, f32[6,64,128]{2,1,0:T(8,128)S(1)}, u32[]{:S(2)}, u32[]{:S(2)}) collective-permute-start(f32[6,64,128]{2,1,0:T(8,128)S(1)} %get-tuple-element.49), channel_id=1, source_target_pairs={{0,8},{8,0},{16,24},{24,16},{32,40},{40,32},{48,56},{56,48},{64,72... | collective-permute-start | bytes 589832 | tf_op jit(solution)/shard_map/ppermute | solution.py:36
  10.5 5.8 %collective-permute-start.1 = (f32[6,64,128]{2,1,0:T(8,128)S(1)}, f32[6,64,128]{2,1,0:T(8,128)S(1)}, u32[]{:S(2)}, u32[]{:S(2)}) collective-permute-start(f32[6,64,128]{2,1,0:T(8,128)S(1)} %get-tuple-element.50), channel_id=1, source_target_pairs={{8,16},{16,8},{24,32},{32,24},{40,48},{48,40},{56,64},{64,56},{72,... | collective-permute-start | bytes 589832 | tf_op jit(solution)/shard_map/ppermute | solution.py:36
  11.7 8.7 %collective-permute-start.6 = (f32[3,64,128]{2,1,0:T(8,128)S(1)}, f32[3,64,128]{2,1,0:T(8,128)S(1)}, u32[]{:S(2)}, u32[]{:S(2)}) collective-permute-start(f32[3,64,128]{2,1,0:T(8,128)S(1)} %get-tuple-element.58), channel_id=1, source_target_pairs={{0,1},{1,0},{2,3},{3,2},{4,5},{5,4},{6,7},{7,6},{8,9},{9,8},{10,11... | collective-permute-start | bytes 294920 | tf_op jit(solution)/shard_map/ppermute | solution.py:36
  13.3 7.1 %collective-permute-start.7 = (f32[3,64,128]{2,1,0:T(8,128)S(1)}, f32[3,64,128]{2,1,0:T(8,128)S(1)}, u32[]{:S(2)}, u32[]{:S(2)}) collective-permute-start(f32[3,64,128]{2,1,0:T(8,128)S(1)} %get-tuple-element.59), channel_id=1, source_target_pairs={{1,2},{2,1},{3,4},{4,3},{5,6},{6,5},{9,10},{10,9},{11,12},{12,11},... | collective-permute-start | bytes 294920 | tf_op jit(solution)/shard_map/ppermute | solution.py:36
  16.7 6.4 %collective-permute-start.2 = (f32[2,64,128]{2,1,0:T(8,128)S(1)}, f32[2,64,128]{2,1,0:T(8,128)S(1)}, u32[]{:S(2)}, u32[]{:S(2)}) collective-permute-start(f32[2,64,128]{2,1,0:T(8,128)S(1)} %get-tuple-element.52), channel_id=1, source_target_pairs={{0,1},{1,0},{2,3},{3,2},{4,5},{5,4},{6,7},{7,6},{8,9},{9,8},{10,11... | collective-permute-start | bytes 196616 | tf_op jit(solution)/shard_map/ppermute | solution.py:36
  16.9 6.3 %collective-permute-start.3 = (f32[2,64,128]{2,1,0:T(8,128)S(1)}, f32[2,64,128]{2,1,0:T(8,128)S(1)}, u32[]{:S(2)}, u32[]{:S(2)}) collective-permute-start(f32[2,64,128]{2,1,0:T(8,128)S(1)} %get-tuple-element.53), channel_id=1, source_target_pairs={{1,2},{2,1},{3,4},{4,3},{5,6},{6,5},{9,10},{10,9},{11,12},{12,11},... | collective-permute-start | bytes 196616 | tf_op jit(solution)/shard_map/ppermute | solution.py:36
  26.9 25.3 %all-to-all-start = ((f32[32,16,128]{2,1,0:T(8,128)}), f32[32,16,128]{2,1,0:T(8,128)S(1)}, u32[]{:S(2)}, u32[]{:S(2)}) async-start(f32[32,16,128]{2,1,0:T(8,128)} %get-tuple-element.67), calls=%async_computation | async-start | bytes 524288 | tf_op jit(solution)/shard_map/all_to_all | solution.py:538
  40.2 7.6 %collective-permute-start.8 = (f32[3,32,128]{2,1,0:T(8,128)}, f32[3,32,128]{2,1,0:T(8,128)S(1)}, u32[]{:S(2)}, u32[]{:S(2)}) collective-permute-start(f32[3,32,128]{2,1,0:T(8,128)} %get-tuple-element.68), channel_id=1, source_target_pairs={{0,8},{8,0},{16,24},{24,16},{32,40},{40,32},{48,56},{56,48},{64,72... | collective-permute-start | bytes 147464 | tf_op jit(solution)/shard_map/ppermute | solution.py:36
  41.5 6.3 %collective-permute-start.9 = (f32[3,32,128]{2,1,0:T(8,128)}, f32[3,32,128]{2,1,0:T(8,128)S(1)}, u32[]{:S(2)}, u32[]{:S(2)}) collective-permute-start(f32[3,32,128]{2,1,0:T(8,128)} %get-tuple-element.69), channel_id=1, source_target_pairs={{8,16},{16,8},{24,32},{32,24},{40,48},{48,40},{56,64},{64,56},{72,... | collective-permute-start | bytes 147464 | tf_op jit(solution)/shard_map/ppermute | solution.py:36
  47.8 8.3 %copy-start = (f32[3,32,128]{2,1,0:T(8,128)}, f32[3,32,128]{2,1,0:T(8,128)S(1)}, u32[]{:S(2)}) copy-start(f32[3,32,128]{2,1,0:T(8,128)S(1)} %collective-permute-done.8.ra_hbm) | copy-start | bytes 147460
  47.8 8.3 %copy-start.1 = (f32[3,32,128]{2,1,0:T(8,128)}, f32[3,32,128]{2,1,0:T(8,128)S(1)}, u32[]{:S(2)}) copy-start(f32[3,32,128]{2,1,0:T(8,128)S(1)} %collective-permute-done.9.rb_hbm) | copy-start | bytes 147460
  52.2 7.0 %collective-permute-start.10 = (f32[23,16,128]{2,1,0:T(8,128)S(1)}, f32[23,16,128]{2,1,0:T(8,128)S(1)}, u32[]{:S(2)}, u32[]{:S(2)}) collective-permute-start(f32[23,16,128]{2,1,0:T(8,128)S(1)} %constant_dynamic-slice_fusion.g), channel_id=1, source_target_pairs={{0,1},{1,0},{2,3},{3,2},{4,5},{5,4},{6,7},{7,6},{8,9},{9,8},{10,11... | collective-permute-start | bytes 565256 | tf_op jit(solution)/shard_map/ppermute | solution.py:36
  52.3 6.9 %collective-permute-start.11 = (f32[23,16,128]{2,1,0:T(8,128)S(1)}, f32[23,16,128]{2,1,0:T(8,128)S(1)}, u32[]{:S(2)}, u32[]{:S(2)}) collective-permute-start(f32[23,16,128]{2,1,0:T(8,128)S(1)} %constant_dynamic-slice_fusion.g), channel_id=1, source_target_pairs={{1,2},{2,1},{3,4},{4,3},{5,6},{6,5},{9,10},{10,9},{11,12},{12,11},... | collective-permute-start | bytes 565256 | tf_op jit(solution)/shard_map/ppermute | solution.py:36

commit v6 on v5

--- a/solution.py
+++ b/solution.py
@@ -14,15 +14,15 @@
 COARSE_LOW = 0.02
 VMEM_LIMIT = 28 * 1024 * 1024
 
-SHAPE0, SHAPE1, SHAPE2, WINDOW_UNROLL = (1,True), (4, True), (8, True), True
+SHAPE0, SHAPE1, SHAPE2, WINDOW_UNROLL = (1, True), (4, True), (4, True), True
 
 WINDOW = 23
 
 PIECES = 4
 
 KX, BX, KY, BY = 7, 6, 13, 12
-PACKED_K = ((0, 9, 14), (9, 9, 14), (18, 4, 14))
-PACKED_B = ((0, 10, 12), (10, 10, 12))
+PACKED_K = ((0, 9), (9, 9), (18, 4))
+PACKED_B = ((0, 10), (10, 10))
 
 
 def pairs(size, offset):
@@ -226,15 +226,17 @@
 
 def strip_kernel(width, source, own, xa, xb, ref, sems):
     odd_x = odd("gx")
-    for copy in pieces(PIECES, source, ref, Copies(sems)):
+    depth = 64 // PIECES
+    for n, copy in enumerate(pieces(PIECES, source, ref, Copies(sems))):
         copy.wait()
-    planes = [ref[pl.ds(i, 64, stride=8), :] for i in range(8)]
-    for i in range(8):
-        own[i] = planes[i]
-    for i in range(width):
-        first, last = planes[i], planes[8 - width + i]
-        xa[i] = jnp.where(odd_x, first, last)
-        xb[i] = jnp.where(odd_x, last, first)
+        z = pl.ds(depth * n, depth)
+        planes = [ref[pl.ds(8 * depth * n + i, depth, stride=8), :] for i in range(8)]
+        for i in range(8):
+            own[i, z] = planes[i]
+        for i in range(width):
+            first, last = planes[i], planes[8 - width + i]
+            xa[i, z] = jnp.where(odd_x, first, last)
+            xb[i, z] = jnp.where(odd_x, last, first)
 
 
 def pack_kernel(packed, width, own, xa, xb, rows_out, ya, yb):
@@ -249,13 +251,15 @@
         planes[halo + i] = own[i]
     for n, plane in enumerate(planes):
         rows_out[n] = plane
-    for n, (start, count, room) in enumerate(packed):
+    for n, (start, count) in enumerate(packed):
         first, last = jnp.zeros((64, 128), F32), jnp.zeros((64, 128), F32)
-        for i in range(count):
-            plane = planes[start + i]
-            here = (lane >= room * i) & (lane < room * i + width)
-            first = jnp.where(here, turn(plane, room * i, 1), first)
-            last = jnp.where(here, turn(plane, room * i + width, 1), last)
+        for i in range(count + 1):
+            this, before = planes[start + min(i, count - 1)], planes[start + max(i - 1, 0)]
+            turned = turn(jnp.where(lane < 64, this, before), width * i, 1)
+            if i < count:
+                first = jnp.where((lane >= width * i) & (lane < width * (i + 1)), turned, first)
+            if i > 0:
+                last = jnp.where((lane >= width * (i - 1)) & (lane < width * i), turned, last)
         ya[n] = jnp.where(odd_y, first, last)
         yb[n] = jnp.where(odd_y, last, first)
 
@@ -263,12 +267,14 @@
 def outer_columns(packed, width, ya, yb):
     odd_y = odd("gy")
     lane = iota((64, 128), 1)
-    for n, (start, count, room) in enumerate(packed):
+    for n, (start, count) in enumerate(packed):
         a, b = ya[n], yb[n]
         left, right = jnp.where(odd_y, a, b), jnp.where(odd_y, b, a)
+        ahead = right
         for i in range(count):
-            ahead, behind = turn(right, -room * i, 1), turn(left, 128 - width - room * i, 1)
+            behind = turn(jnp.where(lane < width * (i + 1), left, right), -width * (i + 1), 1)
             yield start + i, jnp.where(lane < width, ahead, jnp.where(lane >= 128 - width, behind, 0.0))
+            ahead = behind
 
 
 def weights_kernel(
@@ -278,13 +284,12 @@
     for q, outer in outer_columns(PACKED_K, KY, ya, yb):
         k_out[q, :, 0:128] = k_rows[q]
         k_out[q, :, 128:256] = outer
-    flying = [copies.start(k_out.at[pl.ds(4, 14)], k_hbm)]
     for m in range(10):
         wide[m] = k_out[2 * m + 1] + k_out[2 * m + 2]
     thin[...] = dot(wide[...].reshape(10 * 64, 256), coarsen_matrix(256, 128, 140, 12, 0.125))
     for m in range(10):
         k1[m] = thin[pl.ds(64 * m, 32, stride=2), :] + thin[pl.ds(64 * m + 1, 32, stride=2), :]
-    flying.append(copies.start(k1, k1_hbm))
+    flying = [copies.start(k_out.at[pl.ds(4, 14)], k_hbm), copies.start(k1, k1_hbm)]
     Level(k_out, weights, None, None, None, 1.0, *SHAPE0).set_up(1, 21, None, diagonal, inverse)
     Level(k1, w1, None, None, None, 0.25, *SHAPE1).set_up(1, 9, None, diagonal1, inverse1)
     for copy in flying:
@@ -404,11 +409,12 @@
         at = jnp.clip(device - start, 0, g.shape[0] - 1)
         own, a, b = g[at], ga[at], gb[at]
         left, right = jnp.where(odd_y, a, b), jnp.where(odd_y, b, a)
-        for n, out in ((0, b2), (2, k2)):
-            for m in range(2):
-                s = -32 * (n + m)
-                value = jnp.where(lane < 32, turn(own, s, 1), jnp.where(lane < 64, turn(right, s + 32, 1), jnp.where(lane >= 96, turn(left, s + 96, 1), 0.0)))
-                out[2 * j + m] = jnp.where(inside, value, 0.0)
+        by32 = turn(jnp.where(lane < 32, left, jnp.where(lane < 64, own, right)), -32, 1)
+        by64 = turn(jnp.where(lane < 64, left, jnp.where(lane < 96, own, right)), -64, 1)
+        by96 = turn(jnp.where(lane < 32, right, jnp.where(lane < 96, left, own)), -96, 1)
+        for out, m, parts in ((b2, 0, (own, by96, by32)), (b2, 1, (by32, right, by64)), (k2, 0, (by64, by32, by96)), (k2, 1, (by96, by64, left))):
+            value = jnp.where(lane < 32, parts[0], jnp.where(lane < 64, parts[1], jnp.where(lane >= 96, parts[2], 0.0)))
+            out[2 * j + m] = jnp.where(inside, value, 0.0) if out is k2 else value
         return carry
 
     lax.fori_loop(0, WINDOW, window, 0, unroll=WINDOW_UNROLL)
@@ -427,27 +433,22 @@
     both = coarse2[pl.ds(0, 46 * 8, stride=2), :] + coarse2[pl.ds(1, 46 * 8, stride=2), :]
     both = both.reshape(46, 8, 128)
     b3, k3 = both[:23], both[23:]
-    none = jnp.zeros((1, 8, 128), F32)
-
-    def after(value):
-        return jnp.concatenate([value[1:], none], axis=0)
-
-    def before(value):
-        return jnp.concatenate([none, value[:-1]], axis=0)
-
-    w3, inverse, _ = weights_row(k3, before(k3), after(k3), 0.015625)
+    w3, inverse, _ = weights_row(k3[2:21], k3[1:20], k3[3:22], 0.015625)
     middle, steps = chebyshev(COARSE, COARSE_LOW)
-    source = b3 * inverse
+    source = b3[2:21] * inverse
     update = source * (1 / middle)
     e3 = update
-    for c1, c2 in steps:
-        update = c1 * update + c2 * (source - e3 + neighbour_sum(w3, before(e3), e3, after(e3)))
-        e3 = e3 + update
+    for n, (c1, c2) in enumerate(steps):
+        inner = slice(n + 1, 18 - n)
+        below, centre, above = e3[:-2], e3[1:-1], e3[2:]
+        total = neighbour_sum([w[inner] for w in w3], below, centre, above)
+        update = c1 * update[1:-1] + c2 * (source[inner] - centre + total)
+        e3 = centre + update
 
     tall = coarse2
     for m in range(5):
         for half in range(2):
-            tall[pl.ds(16 * m + half, 8, stride=2), :] = e3[9 + m]
+            tall[pl.ds(16 * m + half, 8, stride=2), :] = e3[m]
     fine = dot(tall[0 : 5 * 16, :], refine_matrix(128, 128, 64, 32))
     for m in range(10):
         part = fine[16 * (m // 2) : 16 * (m // 2) + 16]

time: 66 us -> 65.3 us (0.989)
  Pallas kernels: 18.3 us -> 17.5 us
    pallas_call x8, Pallas kernels: 18.3 us -> 17.5 us  [call(): pl.pallas_call(body, out_shape=[pltpu.HBM(s, F32) if n < hbm_out else jax...]
  transfers between devices with their start and end apart: 13 -> 13, of which waited for: 2 -> 2; matrix products, arithmetic and copies ran while one was open for 0% -> 0% of each run, Pallas kernels for 12% -> 11%
where the time goes in v6:
time: 65.3 us; the launch traced here: 64.5 us
  starting transfers between devices  36 us (55%)
  Pallas kernels  17.5 us (27%)
  waiting for transfers between devices  10 us (15%)
  between operations  1.02 us (2%)
    ppermute x12, starting transfers between devices, swap(): return lax.ppermute(value, axis, pairs(lax.axis_size(axis), offset))  22.7 us
    pallas_call x8, Pallas kernels, call(): pl.pallas_call(body, out_shape=[pltpu.HBM(s, F32) if n < hbm_out else jax...  17.5 us
    all_to_all x1, starting transfers between devices, on_device(): g = lax.all_to_all(g, 'gx', 0, 0, tiled=True)  13.3 us
    ppermute x12, waiting for transfers between devices, swap(): return lax.ppermute(value, axis, pairs(lax.axis_size(axis), offset))  5.68 us
    all_to_all x1, waiting for transfers between devices, on_device(): g = lax.all_to_all(g, 'gx', 0, 0, tiled=True)  4.35 us
  transfers between devices with their start and end apart: 13, of which 2 were waited for; matrix products, arithmetic and copies ran while one was open for 0% of the time, Pallas kernels for 11%

profile of v6, /device:TPU:1, one launch (start us, length us, event | category | flops | bytes accessed | tf_op | source)
XLA Modules:
  0.0 64.5 jit_solution(1690185982771368632)
XLA Ops:
  0.6 1.0 %shard_map.43 = (f32[8,64,128]{2,1,0:T(8,128)S(1)}, f32[7,64,128]{2,1,0:T(8,128)S(1)}, f32[7,64,128]{2,1,0:T(8,128)S(1)}) custom-call(f32[512,128]{1,0:T(8,128)} %bitcast.4), custom_call_target="tpu_custom_call" | custom-call | tf_op jit(solution)/shard_map/pallas_call | solution.py:196
  1.6 2.6 %collective-permute-start.4 = (f32[7,64,128]{2,1,0:T(8,128)S(1)}, f32[7,64,128]{2,1,0:T(8,128)S(1)}, u32[]{:S(2)}, u32[]{:S(2)}) collective-permute-start(f32[7,64,128]{2,1,0:T(8,128)S(1)} %get-tuple-element.55), channel_id=1, source_target_pairs={{0,8},{8,0},{16,24},{24,16},{32,40},{40,32},{48,56},{56,48},{64,72... | collective-permute-start | bytes 688136 | tf_op jit(solution)/shard_map/ppermute | solution.py:36
  4.2 0.7 %collective-permute-start.5 = (f32[7,64,128]{2,1,0:T(8,128)S(1)}, f32[7,64,128]{2,1,0:T(8,128)S(1)}, u32[]{:S(2)}, u32[]{:S(2)}) collective-permute-start(f32[7,64,128]{2,1,0:T(8,128)S(1)} %get-tuple-element.56), channel_id=1, source_target_pairs={{8,16},{16,8},{24,32},{32,24},{40,48},{48,40},{56,64},{64,56},{72,... | collective-permute-start | bytes 688136 | tf_op jit(solution)/shard_map/ppermute | solution.py:36
  4.9 1.0 %shard_map.41 = (f32[8,64,128]{2,1,0:T(8,128)S(1)}, f32[6,64,128]{2,1,0:T(8,128)S(1)}, f32[6,64,128]{2,1,0:T(8,128)S(1)}) custom-call(f32[512,128]{1,0:T(8,128)} %bitcast.5), custom_call_target="tpu_custom_call" | custom-call | tf_op jit(solution)/shard_map/pallas_call | solution.py:196
  5.8 4.6 %collective-permute-start = (f32[6,64,128]{2,1,0:T(8,128)S(1)}, f32[6,64,128]{2,1,0:T(8,128)S(1)}, u32[]{:S(2)}, u32[]{:S(2)}) collective-permute-start(f32[6,64,128]{2,1,0:T(8,128)S(1)} %get-tuple-element.49), channel_id=1, source_target_pairs={{0,8},{8,0},{16,24},{24,16},{32,40},{40,32},{48,56},{56,48},{64,72... | collective-permute-start | bytes 589832 | tf_op jit(solution)/shard_map/ppermute | solution.py:36
  10.4 0.7 %collective-permute-start.1 = (f32[6,64,128]{2,1,0:T(8,128)S(1)}, f32[6,64,128]{2,1,0:T(8,128)S(1)}, u32[]{:S(2)}, u32[]{:S(2)}) collective-permute-start(f32[6,64,128]{2,1,0:T(8,128)S(1)} %get-tuple-element.50), channel_id=1, source_target_pairs={{8,16},{16,8},{24,32},{32,24},{40,48},{48,40},{56,64},{64,56},{72,... | collective-permute-start | bytes 589832 | tf_op jit(solution)/shard_map/ppermute | solution.py:36
  11.1 0.0 collective-permute-done.4.xa
  11.1 0.0 collective-permute-done.5.xb
  11.1 0.3 shard_map.44
  11.4 1.6 %collective-permute-start.6 = (f32[3,64,128]{2,1,0:T(8,128)S(1)}, f32[3,64,128]{2,1,0:T(8,128)S(1)}, u32[]{:S(2)}, u32[]{:S(2)}) collective-permute-start(f32[3,64,128]{2,1,0:T(8,128)S(1)} %get-tuple-element.58), channel_id=1, source_target_pairs={{0,1},{1,0},{2,3},{3,2},{4,5},{5,4},{6,7},{7,6},{8,9},{9,8},{10,11... | collective-permute-start | bytes 294920 | tf_op jit(solution)/shard_map/ppermute | solution.py:36
  13.0 3.0 %collective-permute-start.7 = (f32[3,64,128]{2,1,0:T(8,128)S(1)}, f32[3,64,128]{2,1,0:T(8,128)S(1)}, u32[]{:S(2)}, u32[]{:S(2)}) collective-permute-start(f32[3,64,128]{2,1,0:T(8,128)S(1)} %get-tuple-element.59), channel_id=1, source_target_pairs={{1,2},{2,1},{3,4},{4,3},{5,6},{6,5},{9,10},{10,9},{11,12},{12,11},... | collective-permute-start | bytes 294920 | tf_op jit(solution)/shard_map/ppermute | solution.py:36
  16.1 0.0 collective-permute-done.xa
  16.1 0.0 collective-permute-done.1.xb
  16.1 0.3 shard_map.42
  16.4 0.3 collective-permute-start.2
  16.7 3.3 %collective-permute-start.3 = (f32[2,64,128]{2,1,0:T(8,128)S(1)}, f32[2,64,128]{2,1,0:T(8,128)S(1)}, u32[]{:S(2)}, u32[]{:S(2)}) collective-permute-start(f32[2,64,128]{2,1,0:T(8,128)S(1)} %get-tuple-element.53), channel_id=1, source_target_pairs={{1,2},{2,1},{3,4},{4,3},{5,6},{6,5},{9,10},{10,9},{11,12},{12,11},... | collective-permute-start | bytes 196616 | tf_op jit(solution)/shard_map/ppermute | solution.py:36
  20.0 0.0 collective-permute-done.6.ya
  20.0 0.0 collective-permute-done.7.yb
  20.0 2.7 %shard_map.45 = (f32[14,64,256]{2,1,0:T(8,128)}, f32[10,32,128]{2,1,0:T(8,128)}, f32[6,22,64,256]{3,2,1,0:T(8,128)S(1)}, f32[22,64,256]{2,1,0:T(8,128)S(1)}, f32...) custom-call(f32[22,64,128]{2,1,0:T(8,128)S(1)} %get-tuple-element.57, ...), custom_call_target="tpu_custom_call" | custom-call | flops 20000000 | bytes 8000000 | tf_op jit(solution)/shard_map/pallas_call | solution.py:196
  22.7 0.0 collective-permute-done.2.ya
  22.7 0.0 collective-permute-done.3.yb
  22.8 3.6 %shard_map.46 = (f32[12,64,256]{2,1,0:T(8,128)}, f32[14,64,256]{2,1,0:T(8,128)}, f32[10,32,128]{2,1,0:T(8,128)}, f32[10,32,128]{2,1,0:T(8,128)}, f32[3,32,128]{2...) custom-call(f32[20,64,128]{2,1,0:T(8,128)S(1)} %get-tuple-element.51.b_rows, ...), custom_call_target="tpu_custom_call" | custom-call | tf_op jit(solution)/shard_map/pallas_call | solution.py:196
  26.4 13.3 %all-to-all-start = ((f32[32,16,128]{2,1,0:T(8,128)}), f32[32,16,128]{2,1,0:T(8,128)S(1)}, u32[]{:S(2)}, u32[]{:S(2)}) async-start(f32[32,16,128]{2,1,0:T(8,128)} %get-tuple-element.67), calls=%async_computation | async-start | bytes 524288 | tf_op jit(solution)/shard_map/all_to_all | solution.py:539
  39.7 1.3 %collective-permute-start.8 = (f32[3,32,128]{2,1,0:T(8,128)}, f32[3,32,128]{2,1,0:T(8,128)S(1)}, u32[]{:S(2)}, u32[]{:S(2)}) collective-permute-start(f32[3,32,128]{2,1,0:T(8,128)} %get-tuple-element.68), channel_id=1, source_target_pairs={{0,8},{8,0},{16,24},{24,16},{32,40},{40,32},{48,56},{56,48},{64,72... | collective-permute-start | bytes 147464 | tf_op jit(solution)/shard_map/ppermute | solution.py:36
  41.1 0.7 %collective-permute-start.9 = (f32[3,32,128]{2,1,0:T(8,128)}, f32[3,32,128]{2,1,0:T(8,128)S(1)}, u32[]{:S(2)}, u32[]{:S(2)}) collective-permute-start(f32[3,32,128]{2,1,0:T(8,128)} %get-tuple-element.69), channel_id=1, source_target_pairs={{8,16},{16,8},{24,32},{32,24},{40,48},{48,40},{56,64},{64,56},{72,... | collective-permute-start | bytes 147464 | tf_op jit(solution)/shard_map/ppermute | solution.py:36
  41.7 5.7 %collective-permute-done.8.ra_hbm = f32[3,32,128]{2,1,0:T(8,128)S(1)} collective-permute-done((f32[3,32,128]{2,1,0:T(8,128)}, f32[3,32,128]{2,1,0:T(8,128)S(1)}, u32[]{:S(2)}, u32[]{:S(2)}) %collective-permute-start.8) | collective-permute-done | bytes 49184 | tf_op jit(solution)/shard_map/ppermute | solution.py:36
  47.4 0.0 copy-start
  47.4 0.0 collective-permute-done.9.rb_hbm
  47.4 0.0 copy-start.1
  47.4 4.4 %all-to-all-done = f32[32,16,128]{2,1,0:T(8,128)S(1)} async-done(((f32[32,16,128]{2,1,0:T(8,128)}), f32[32,16,128]{2,1,0:T(8,128)S(1)}, u32[]{:S(2)}, u32[]{:S(2)}) %all-to-all-start) | async-done | bytes 262176 | tf_op jit(solution)/shard_map/all_to_all | solution.py:539
  51.7 0.1 collective-permute-start.10
  51.8 3.9 %collective-permute-start.11 = (f32[23,16,128]{2,1,0:T(8,128)S(1)}, f32[23,16,128]{2,1,0:T(8,128)S(1)}, u32[]{:S(2)}, u32[]{:S(2)}) collective-permute-start(f32[23,16,128]{2,1,0:T(8,128)S(1)} %constant_dynamic-slice_fusion.g), channel_id=1, source_target_pairs={{1,2},{2,1},{3,4},{4,3},{5,6},{6,5},{9,10},{10,9},{11,12},{12,11},... | collective-permute-start | bytes 565256 | tf_op jit(solution)/shard_map/ppermute | solution.py:36
  55.8 0.0 copy-done
  55.8 0.0 copy-done.1
  55.8 3.1 %shard_map.47 = (f32[6,14,64,256]{3,2,1,0:T(8,128)S(1)}, f32[14,64,256]{2,1,0:T(8,128)S(1)}, f32[14,64,256]{2,1,0:T(8,128)S(1)}, f32[14,64,256]{2,1,0:T(8,128)S(...) custom-call(f32[3,32,128]{2,1,0:T(8,128)} %copy-done, ...), custom_call_target="tpu_custom_call" | custom-call | flops 20000000 | bytes 8000000 | tf_op jit(solution)/shard_map/pallas_call | solution.py:196
  58.9 0.0 collective-permute-done.10.ga
  58.9 0.0 collective-permute-done.11.gb
  58.9 5.5 %shard_map.48 = (f32[512,128]{1,0:T(8,128)}, f32[512,128]{1,0:T(8,128)}) custom-call(f32[6,14,64,256]{3,2,1,0:T(8,128)S(1)} %get-tuple-element.84.w0, f32[14,64,256]{2,1,0:T(8,128)S(1)} %get-tuple-element.85.bh0, f32[14,64,256]{2,1,0:T(8,128)S(1)} %get-tuple-element.86.d0, f32[14,64,256]{2,1,0:T(8,128)S(1)} %get-tuple-element.87.x0, ...), custom_call_target="tpu_custom_call" | custom-call | tf_op jit(solution)/shard_map/pallas_call | solution.py:196
  (1 shorter events, 0.0 us)
Async XLA Ops:
  1.6 9.5 %collective-permute-start.4 = (f32[7,64,128]{2,1,0:T(8,128)S(1)}, f32[7,64,128]{2,1,0:T(8,128)S(1)}, u32[]{:S(2)}, u32[]{:S(2)}) collective-permute-start(f32[7,64,128]{2,1,0:T(8,128)S(1)} %get-tuple-element.55), channel_id=1, source_target_pairs={{0,8},{8,0},{16,24},{24,16},{32,40},{40,32},{48,56},{56,48},{64,72... | collective-permute-start | bytes 688136 | tf_op jit(solution)/shard_map/ppermute | solution.py:36
  4.2 6.9 %collective-permute-start.5 = (f32[7,64,128]{2,1,0:T(8,128)S(1)}, f32[7,64,128]{2,1,0:T(8,128)S(1)}, u32[]{:S(2)}, u32[]{:S(2)}) collective-permute-start(f32[7,64,128]{2,1,0:T(8,128)S(1)} %get-tuple-element.56), channel_id=1, source_target_pairs={{8,16},{16,8},{24,32},{32,24},{40,48},{48,40},{56,64},{64,56},{72,... | collective-permute-start | bytes 688136 | tf_op jit(solution)/shard_map/ppermute | solution.py:36
  5.8 10.2 %collective-permute-start = (f32[6,64,128]{2,1,0:T(8,128)S(1)}, f32[6,64,128]{2,1,0:T(8,128)S(1)}, u32[]{:S(2)}, u32[]{:S(2)}) collective-permute-start(f32[6,64,128]{2,1,0:T(8,128)S(1)} %get-tuple-element.49), channel_id=1, source_target_pairs={{0,8},{8,0},{16,24},{24,16},{32,40},{40,32},{48,56},{56,48},{64,72... | collective-permute-start | bytes 589832 | tf_op jit(solution)/shard_map/ppermute | solution.py:36
  10.4 5.6 %collective-permute-start.1 = (f32[6,64,128]{2,1,0:T(8,128)S(1)}, f32[6,64,128]{2,1,0:T(8,128)S(1)}, u32[]{:S(2)}, u32[]{:S(2)}) collective-permute-start(f32[6,64,128]{2,1,0:T(8,128)S(1)} %get-tuple-element.50), channel_id=1, source_target_pairs={{8,16},{16,8},{24,32},{32,24},{40,48},{48,40},{56,64},{64,56},{72,... | collective-permute-start | bytes 589832 | tf_op jit(solution)/shard_map/ppermute | solution.py:36
  11.4 8.5 %collective-permute-start.6 = (f32[3,64,128]{2,1,0:T(8,128)S(1)}, f32[3,64,128]{2,1,0:T(8,128)S(1)}, u32[]{:S(2)}, u32[]{:S(2)}) collective-permute-start(f32[3,64,128]{2,1,0:T(8,128)S(1)} %get-tuple-element.58), channel_id=1, source_target_pairs={{0,1},{1,0},{2,3},{3,2},{4,5},{5,4},{6,7},{7,6},{8,9},{9,8},{10,11... | collective-permute-start | bytes 294920 | tf_op jit(solution)/shard_map/ppermute | solution.py:36
  13.0 6.9 %collective-permute-start.7 = (f32[3,64,128]{2,1,0:T(8,128)S(1)}, f32[3,64,128]{2,1,0:T(8,128)S(1)}, u32[]{:S(2)}, u32[]{:S(2)}) collective-permute-start(f32[3,64,128]{2,1,0:T(8,128)S(1)} %get-tuple-element.59), channel_id=1, source_target_pairs={{1,2},{2,1},{3,4},{4,3},{5,6},{6,5},{9,10},{10,9},{11,12},{12,11},... | collective-permute-start | bytes 294920 | tf_op jit(solution)/shard_map/ppermute | solution.py:36
  16.4 6.4 %collective-permute-start.2 = (f32[2,64,128]{2,1,0:T(8,128)S(1)}, f32[2,64,128]{2,1,0:T(8,128)S(1)}, u32[]{:S(2)}, u32[]{:S(2)}) collective-permute-start(f32[2,64,128]{2,1,0:T(8,128)S(1)} %get-tuple-element.52), channel_id=1, source_target_pairs={{0,1},{1,0},{2,3},{3,2},{4,5},{5,4},{6,7},{7,6},{8,9},{9,8},{10,11... | collective-permute-start | bytes 196616 | tf_op jit(solution)/shard_map/ppermute | solution.py:36
  16.7 6.1 %collective-permute-start.3 = (f32[2,64,128]{2,1,0:T(8,128)S(1)}, f32[2,64,128]{2,1,0:T(8,128)S(1)}, u32[]{:S(2)}, u32[]{:S(2)}) collective-permute-start(f32[2,64,128]{2,1,0:T(8,128)S(1)} %get-tuple-element.53), channel_id=1, source_target_pairs={{1,2},{2,1},{3,4},{4,3},{5,6},{6,5},{9,10},{10,9},{11,12},{12,11},... | collective-permute-start | bytes 196616 | tf_op jit(solution)/shard_map/ppermute | solution.py:36
  26.4 25.3 %all-to-all-start = ((f32[32,16,128]{2,1,0:T(8,128)}), f32[32,16,128]{2,1,0:T(8,128)S(1)}, u32[]{:S(2)}, u32[]{:S(2)}) async-start(f32[32,16,128]{2,1,0:T(8,128)} %get-tuple-element.67), calls=%async_computation | async-start | bytes 524288 | tf_op jit(solution)/shard_map/all_to_all | solution.py:539
  39.7 7.6 %collective-permute-start.8 = (f32[3,32,128]{2,1,0:T(8,128)}, f32[3,32,128]{2,1,0:T(8,128)S(1)}, u32[]{:S(2)}, u32[]{:S(2)}) collective-permute-start(f32[3,32,128]{2,1,0:T(8,128)} %get-tuple-element.68), channel_id=1, source_target_pairs={{0,8},{8,0},{16,24},{24,16},{32,40},{40,32},{48,56},{56,48},{64,72... | collective-permute-start | bytes 147464 | tf_op jit(solution)/shard_map/ppermute | solution.py:36
  41.1 6.3 %collective-permute-start.9 = (f32[3,32,128]{2,1,0:T(8,128)}, f32[3,32,128]{2,1,0:T(8,128)S(1)}, u32[]{:S(2)}, u32[]{:S(2)}) collective-permute-start(f32[3,32,128]{2,1,0:T(8,128)} %get-tuple-element.69), channel_id=1, source_target_pairs={{8,16},{16,8},{24,32},{32,24},{40,48},{48,40},{56,64},{64,56},{72,... | collective-permute-start | bytes 147464 | tf_op jit(solution)/shard_map/ppermute | solution.py:36
  47.4 8.4 %copy-start = (f32[3,32,128]{2,1,0:T(8,128)}, f32[3,32,128]{2,1,0:T(8,128)S(1)}, u32[]{:S(2)}) copy-start(f32[3,32,128]{2,1,0:T(8,128)S(1)} %collective-permute-done.8.ra_hbm) | copy-start | bytes 147460
  47.4 8.4 %copy-start.1 = (f32[3,32,128]{2,1,0:T(8,128)}, f32[3,32,128]{2,1,0:T(8,128)S(1)}, u32[]{:S(2)}) copy-start(f32[3,32,128]{2,1,0:T(8,128)S(1)} %collective-permute-done.9.rb_hbm) | copy-start | bytes 147460
  51.7 7.1 %collective-permute-start.10 = (f32[23,16,128]{2,1,0:T(8,128)S(1)}, f32[23,16,128]{2,1,0:T(8,128)S(1)}, u32[]{:S(2)}, u32[]{:S(2)}) collective-permute-start(f32[23,16,128]{2,1,0:T(8,128)S(1)} %constant_dynamic-slice_fusion.g), channel_id=1, source_target_pairs={{0,1},{1,0},{2,3},{3,2},{4,5},{5,4},{6,7},{7,6},{8,9},{9,8},{10,11... | collective-permute-start | bytes 565256 | tf_op jit(solution)/shard_map/ppermute | solution.py:36
  51.8 7.0 %collective-permute-start.11 = (f32[23,16,128]{2,1,0:T(8,128)S(1)}, f32[23,16,128]{2,1,0:T(8,128)S(1)}, u32[]{:S(2)}, u32[]{:S(2)}) collective-permute-start(f32[23,16,128]{2,1,0:T(8,128)S(1)} %constant_dynamic-slice_fusion.g), channel_id=1, source_target_pairs={{1,2},{2,1},{3,4},{4,3},{5,6},{6,5},{9,10},{10,9},{11,12},{12,11},... | collective-permute-start | bytes 565256 | tf_op jit(solution)/shard_map/ppermute | solution.py:36

commit v7 on v6

--- a/solution.py
+++ b/solution.py
@@ -15,6 +15,8 @@
 VMEM_LIMIT = 28 * 1024 * 1024
 
 SHAPE0, SHAPE1, SHAPE2, WINDOW_UNROLL = (1, True), (4, True), (4, True), True
+
+SHAPE_K = (1, 5)
 
 WINDOW = 23
 
@@ -290,7 +292,7 @@
     for m in range(10):
         k1[m] = thin[pl.ds(64 * m, 32, stride=2), :] + thin[pl.ds(64 * m + 1, 32, stride=2), :]
     flying = [copies.start(k_out.at[pl.ds(4, 14)], k_hbm), copies.start(k1, k1_hbm)]
-    Level(k_out, weights, None, None, None, 1.0, *SHAPE0).set_up(1, 21, None, diagonal, inverse)
+    Level(k_out, weights, None, None, None, 1.0, *SHAPE_K).set_up(1, 21, None, diagonal, inverse)
     Level(k1, w1, None, None, None, 0.25, *SHAPE1).set_up(1, 9, None, diagonal1, inverse1)
     for copy in flying:
         copy.wait()

time: 65.3 us -> 65.2 us (level)
  starting transfers between devices: 36 us -> 36.9 us
    ppermute x12, starting transfers between devices: 22.7 us -> 23.5 us  [swap(): return lax.ppermute(value, axis, pairs(lax.axis_size(axis), offset))]
where the time goes in v7:
time: 65.2 us; the launch traced here: 64.7 us
  starting transfers between devices  36.9 us (57%)
  Pallas kernels  17.1 us (26%)
  waiting for transfers between devices  9.71 us (15%)
  between operations  1.02 us (2%)
    ppermute x12, starting transfers between devices, swap(): return lax.ppermute(value, axis, pairs(lax.axis_size(axis), offset))  23.5 us
    pallas_call x8, Pallas kernels, call(): pl.pallas_call(body, out_shape=[pltpu.HBM(s, F32) if n < hbm_out else jax...  17.1 us
    all_to_all x1, starting transfers between devices, on_device(): g = lax.all_to_all(g, 'gx', 0, 0, tiled=True)  13.4 us
    ppermute x12, waiting for transfers between devices, swap(): return lax.ppermute(value, axis, pairs(lax.axis_size(axis), offset))  5.65 us
    all_to_all x1, waiting for transfers between devices, on_device(): g = lax.all_to_all(g, 'gx', 0, 0, tiled=True)  4.06 us
  transfers between devices with their start and end apart: 13, of which 2 were waited for; matrix products, arithmetic and copies ran while one was open for 0% of the time, Pallas kernels for 11%

profile of v7, /device:TPU:1, one launch (start us, length us, event | category | flops | bytes accessed | tf_op | source)
XLA Modules:
  0.0 64.7 jit_solution(15740011990037861103)
XLA Ops:
  0.6 1.0 %shard_map.43 = (f32[8,64,128]{2,1,0:T(8,128)S(1)}, f32[7,64,128]{2,1,0:T(8,128)S(1)}, f32[7,64,128]{2,1,0:T(8,128)S(1)}) custom-call(f32[512,128]{1,0:T(8,128)} %bitcast.4), custom_call_target="tpu_custom_call" | custom-call | tf_op jit(solution)/shard_map/pallas_call | solution.py:198
  1.6 2.6 %collective-permute-start.4 = (f32[7,64,128]{2,1,0:T(8,128)S(1)}, f32[7,64,128]{2,1,0:T(8,128)S(1)}, u32[]{:S(2)}, u32[]{:S(2)}) collective-permute-start(f32[7,64,128]{2,1,0:T(8,128)S(1)} %get-tuple-element.55), channel_id=1, source_target_pairs={{0,8},{8,0},{16,24},{24,16},{32,40},{40,32},{48,56},{56,48},{64,72... | collective-permute-start | bytes 688136 | tf_op jit(solution)/shard_map/ppermute | solution.py:38
  4.2 0.7 %collective-permute-start.5 = (f32[7,64,128]{2,1,0:T(8,128)S(1)}, f32[7,64,128]{2,1,0:T(8,128)S(1)}, u32[]{:S(2)}, u32[]{:S(2)}) collective-permute-start(f32[7,64,128]{2,1,0:T(8,128)S(1)} %get-tuple-element.56), channel_id=1, source_target_pairs={{8,16},{16,8},{24,32},{32,24},{40,48},{48,40},{56,64},{64,56},{72,... | collective-permute-start | bytes 688136 | tf_op jit(solution)/shard_map/ppermute | solution.py:38
  4.9 1.0 %shard_map.41 = (f32[8,64,128]{2,1,0:T(8,128)S(1)}, f32[6,64,128]{2,1,0:T(8,128)S(1)}, f32[6,64,128]{2,1,0:T(8,128)S(1)}) custom-call(f32[512,128]{1,0:T(8,128)} %bitcast.5), custom_call_target="tpu_custom_call" | custom-call | tf_op jit(solution)/shard_map/pallas_call | solution.py:198
  5.8 4.6 %collective-permute-start = (f32[6,64,128]{2,1,0:T(8,128)S(1)}, f32[6,64,128]{2,1,0:T(8,128)S(1)}, u32[]{:S(2)}, u32[]{:S(2)}) collective-permute-start(f32[6,64,128]{2,1,0:T(8,128)S(1)} %get-tuple-element.49), channel_id=1, source_target_pairs={{0,8},{8,0},{16,24},{24,16},{32,40},{40,32},{48,56},{56,48},{64,72... | collective-permute-start | bytes 589832 | tf_op jit(solution)/shard_map/ppermute | solution.py:38
  10.4 0.7 %collective-permute-start.1 = (f32[6,64,128]{2,1,0:T(8,128)S(1)}, f32[6,64,128]{2,1,0:T(8,128)S(1)}, u32[]{:S(2)}, u32[]{:S(2)}) collective-permute-start(f32[6,64,128]{2,1,0:T(8,128)S(1)} %get-tuple-element.50), channel_id=1, source_target_pairs={{8,16},{16,8},{24,32},{32,24},{40,48},{48,40},{56,64},{64,56},{72,... | collective-permute-start | bytes 589832 | tf_op jit(solution)/shard_map/ppermute | solution.py:38
  11.1 0.0 collective-permute-done.4.xa
  11.1 0.0 collective-permute-done.5.xb
  11.1 0.3 shard_map.44
  11.4 1.6 %collective-permute-start.6 = (f32[3,64,128]{2,1,0:T(8,128)S(1)}, f32[3,64,128]{2,1,0:T(8,128)S(1)}, u32[]{:S(2)}, u32[]{:S(2)}) collective-permute-start(f32[3,64,128]{2,1,0:T(8,128)S(1)} %get-tuple-element.58), channel_id=1, source_target_pairs={{0,1},{1,0},{2,3},{3,2},{4,5},{5,4},{6,7},{7,6},{8,9},{9,8},{10,11... | collective-permute-start | bytes 294920 | tf_op jit(solution)/shard_map/ppermute | solution.py:38
  13.0 3.0 %collective-permute-start.7 = (f32[3,64,128]{2,1,0:T(8,128)S(1)}, f32[3,64,128]{2,1,0:T(8,128)S(1)}, u32[]{:S(2)}, u32[]{:S(2)}) collective-permute-start(f32[3,64,128]{2,1,0:T(8,128)S(1)} %get-tuple-element.59), channel_id=1, source_target_pairs={{1,2},{2,1},{3,4},{4,3},{5,6},{6,5},{9,10},{10,9},{11,12},{12,11},... | collective-permute-start | bytes 294920 | tf_op jit(solution)/shard_map/ppermute | solution.py:38
  16.1 0.0 collective-permute-done.xa
  16.1 0.0 collective-permute-done.1.xb
  16.1 0.3 shard_map.42
  16.4 0.3 collective-permute-start.2
  16.7 3.3 %collective-permute-start.3 = (f32[2,64,128]{2,1,0:T(8,128)S(1)}, f32[2,64,128]{2,1,0:T(8,128)S(1)}, u32[]{:S(2)}, u32[]{:S(2)}) collective-permute-start(f32[2,64,128]{2,1,0:T(8,128)S(1)} %get-tuple-element.53), channel_id=1, source_target_pairs={{1,2},{2,1},{3,4},{4,3},{5,6},{6,5},{9,10},{10,9},{11,12},{12,11},... | collective-permute-start | bytes 196616 | tf_op jit(solution)/shard_map/ppermute | solution.py:38
  20.0 0.0 collective-permute-done.6.ya
  20.0 0.0 collective-permute-done.7.yb
  20.0 2.4 %shard_map.45 = (f32[14,64,256]{2,1,0:T(8,128)}, f32[10,32,128]{2,1,0:T(8,128)}, f32[6,22,64,256]{3,2,1,0:T(8,128)S(1)}, f32[22,64,256]{2,1,0:T(8,128)S(1)}, f32...) custom-call(f32[22,64,128]{2,1,0:T(8,128)S(1)} %get-tuple-element.57, ...), custom_call_target="tpu_custom_call" | custom-call | flops 20000000 | bytes 8000000 | tf_op jit(solution)/shard_map/pallas_call | solution.py:198
  22.4 0.0 collective-permute-done.2.ya
  22.4 0.0 collective-permute-done.3.yb
  22.4 3.6 %shard_map.46 = (f32[12,64,256]{2,1,0:T(8,128)}, f32[14,64,256]{2,1,0:T(8,128)}, f32[10,32,128]{2,1,0:T(8,128)}, f32[10,32,128]{2,1,0:T(8,128)}, f32[3,32,128]{2...) custom-call(f32[20,64,128]{2,1,0:T(8,128)S(1)} %get-tuple-element.51.b_rows, ...), custom_call_target="tpu_custom_call" | custom-call | tf_op jit(solution)/shard_map/pallas_call | solution.py:198
  26.0 13.4 %all-to-all-start = ((f32[32,16,128]{2,1,0:T(8,128)}), f32[32,16,128]{2,1,0:T(8,128)S(1)}, u32[]{:S(2)}, u32[]{:S(2)}) async-start(f32[32,16,128]{2,1,0:T(8,128)} %get-tuple-element.67), calls=%async_computation | async-start | bytes 524288 | tf_op jit(solution)/shard_map/all_to_all | solution.py:541
  39.4 1.3 %collective-permute-start.8 = (f32[3,32,128]{2,1,0:T(8,128)}, f32[3,32,128]{2,1,0:T(8,128)S(1)}, u32[]{:S(2)}, u32[]{:S(2)}) collective-permute-start(f32[3,32,128]{2,1,0:T(8,128)} %get-tuple-element.68), channel_id=1, source_target_pairs={{0,8},{8,0},{16,24},{24,16},{32,40},{40,32},{48,56},{56,48},{64,72... | collective-permute-start | bytes 147464 | tf_op jit(solution)/shard_map/ppermute | solution.py:38
  40.7 0.7 %collective-permute-start.9 = (f32[3,32,128]{2,1,0:T(8,128)}, f32[3,32,128]{2,1,0:T(8,128)S(1)}, u32[]{:S(2)}, u32[]{:S(2)}) collective-permute-start(f32[3,32,128]{2,1,0:T(8,128)} %get-tuple-element.69), channel_id=1, source_target_pairs={{8,16},{16,8},{24,32},{32,24},{40,48},{48,40},{56,64},{64,56},{72,... | collective-permute-start | bytes 147464 | tf_op jit(solution)/shard_map/ppermute | solution.py:38
  41.4 5.6 %collective-permute-done.8.ra_hbm = f32[3,32,128]{2,1,0:T(8,128)S(1)} collective-permute-done((f32[3,32,128]{2,1,0:T(8,128)}, f32[3,32,128]{2,1,0:T(8,128)S(1)}, u32[]{:S(2)}, u32[]{:S(2)}) %collective-permute-start.8) | collective-permute-done | bytes 49184 | tf_op jit(solution)/shard_map/ppermute | solution.py:38
  47.0 0.0 copy-start
  47.0 0.0 collective-permute-done.9.rb_hbm
  47.0 0.0 copy-start.1
  47.0 4.1 %all-to-all-done = f32[32,16,128]{2,1,0:T(8,128)S(1)} async-done(((f32[32,16,128]{2,1,0:T(8,128)}), f32[32,16,128]{2,1,0:T(8,128)S(1)}, u32[]{:S(2)}, u32[]{:S(2)}) %all-to-all-start) | async-done | bytes 262176 | tf_op jit(solution)/shard_map/all_to_all | solution.py:541
  51.1 0.1 collective-permute-start.10
  51.2 4.8 %collective-permute-start.11 = (f32[23,16,128]{2,1,0:T(8,128)S(1)}, f32[23,16,128]{2,1,0:T(8,128)S(1)}, u32[]{:S(2)}, u32[]{:S(2)}) collective-permute-start(f32[23,16,128]{2,1,0:T(8,128)S(1)} %constant_dynamic-slice_fusion.g), channel_id=1, source_target_pairs={{1,2},{2,1},{3,4},{4,3},{5,6},{6,5},{9,10},{10,9},{11,12},{12,11},... | collective-permute-start | bytes 565256 | tf_op jit(solution)/shard_map/ppermute | solution.py:38
  56.0 0.0 copy-done
  56.0 0.0 copy-done.1
  56.0 3.1 %shard_map.47 = (f32[6,14,64,256]{3,2,1,0:T(8,128)S(1)}, f32[14,64,256]{2,1,0:T(8,128)S(1)}, f32[14,64,256]{2,1,0:T(8,128)S(1)}, f32[14,64,256]{2,1,0:T(8,128)S(...) custom-call(f32[3,32,128]{2,1,0:T(8,128)} %copy-done, ...), custom_call_target="tpu_custom_call" | custom-call | flops 20000000 | bytes 8000000 | tf_op jit(solution)/shard_map/pallas_call | solution.py:198
  59.1 0.0 collective-permute-done.10.ga
  59.1 0.0 collective-permute-done.11.gb
  59.1 5.5 %shard_map.48 = (f32[512,128]{1,0:T(8,128)}, f32[512,128]{1,0:T(8,128)}) custom-call(f32[6,14,64,256]{3,2,1,0:T(8,128)S(1)} %get-tuple-element.84.w0, f32[14,64,256]{2,1,0:T(8,128)S(1)} %get-tuple-element.85.bh0, f32[14,64,256]{2,1,0:T(8,128)S(1)} %get-tuple-element.86.d0, f32[14,64,256]{2,1,0:T(8,128)S(1)} %get-tuple-element.87.x0, ...), custom_call_target="tpu_custom_call" | custom-call | tf_op jit(solution)/shard_map/pallas_call | solution.py:198
  (1 shorter events, 0.0 us)
Async XLA Ops:
  1.6 9.5 %collective-permute-start.4 = (f32[7,64,128]{2,1,0:T(8,128)S(1)}, f32[7,64,128]{2,1,0:T(8,128)S(1)}, u32[]{:S(2)}, u32[]{:S(2)}) collective-permute-start(f32[7,64,128]{2,1,0:T(8,128)S(1)} %get-tuple-element.55), channel_id=1, source_target_pairs={{0,8},{8,0},{16,24},{24,16},{32,40},{40,32},{48,56},{56,48},{64,72... | collective-permute-start | bytes 688136 | tf_op jit(solution)/shard_map/ppermute | solution.py:38
  4.2 6.9 %collective-permute-start.5 = (f32[7,64,128]{2,1,0:T(8,128)S(1)}, f32[7,64,128]{2,1,0:T(8,128)S(1)}, u32[]{:S(2)}, u32[]{:S(2)}) collective-permute-start(f32[7,64,128]{2,1,0:T(8,128)S(1)} %get-tuple-element.56), channel_id=1, source_target_pairs={{8,16},{16,8},{24,32},{32,24},{40,48},{48,40},{56,64},{64,56},{72,... | collective-permute-start | bytes 688136 | tf_op jit(solution)/shard_map/ppermute | solution.py:38
  5.8 10.2 %collective-permute-start = (f32[6,64,128]{2,1,0:T(8,128)S(1)}, f32[6,64,128]{2,1,0:T(8,128)S(1)}, u32[]{:S(2)}, u32[]{:S(2)}) collective-permute-start(f32[6,64,128]{2,1,0:T(8,128)S(1)} %get-tuple-element.49), channel_id=1, source_target_pairs={{0,8},{8,0},{16,24},{24,16},{32,40},{40,32},{48,56},{56,48},{64,72... | collective-permute-start | bytes 589832 | tf_op jit(solution)/shard_map/ppermute | solution.py:38
  10.4 5.6 %collective-permute-start.1 = (f32[6,64,128]{2,1,0:T(8,128)S(1)}, f32[6,64,128]{2,1,0:T(8,128)S(1)}, u32[]{:S(2)}, u32[]{:S(2)}) collective-permute-start(f32[6,64,128]{2,1,0:T(8,128)S(1)} %get-tuple-element.50), channel_id=1, source_target_pairs={{8,16},{16,8},{24,32},{32,24},{40,48},{48,40},{56,64},{64,56},{72,... | collective-permute-start | bytes 589832 | tf_op jit(solution)/shard_map/ppermute | solution.py:38
  11.4 8.5 %collective-permute-start.6 = (f32[3,64,128]{2,1,0:T(8,128)S(1)}, f32[3,64,128]{2,1,0:T(8,128)S(1)}, u32[]{:S(2)}, u32[]{:S(2)}) collective-permute-start(f32[3,64,128]{2,1,0:T(8,128)S(1)} %get-tuple-element.58), channel_id=1, source_target_pairs={{0,1},{1,0},{2,3},{3,2},{4,5},{5,4},{6,7},{7,6},{8,9},{9,8},{10,11... | collective-permute-start | bytes 294920 | tf_op jit(solution)/shard_map/ppermute | solution.py:38
  13.0 6.9 %collective-permute-start.7 = (f32[3,64,128]{2,1,0:T(8,128)S(1)}, f32[3,64,128]{2,1,0:T(8,128)S(1)}, u32[]{:S(2)}, u32[]{:S(2)}) collective-permute-start(f32[3,64,128]{2,1,0:T(8,128)S(1)} %get-tuple-element.59), channel_id=1, source_target_pairs={{1,2},{2,1},{3,4},{4,3},{5,6},{6,5},{9,10},{10,9},{11,12},{12,11},... | collective-permute-start | bytes 294920 | tf_op jit(solution)/shard_map/ppermute | solution.py:38
  16.4 6.0 %collective-permute-start.2 = (f32[2,64,128]{2,1,0:T(8,128)S(1)}, f32[2,64,128]{2,1,0:T(8,128)S(1)}, u32[]{:S(2)}, u32[]{:S(2)}) collective-permute-start(f32[2,64,128]{2,1,0:T(8,128)S(1)} %get-tuple-element.52), channel_id=1, source_target_pairs={{0,1},{1,0},{2,3},{3,2},{4,5},{5,4},{6,7},{7,6},{8,9},{9,8},{10,11... | collective-permute-start | bytes 196616 | tf_op jit(solution)/shard_map/ppermute | solution.py:38
  16.7 5.7 %collective-permute-start.3 = (f32[2,64,128]{2,1,0:T(8,128)S(1)}, f32[2,64,128]{2,1,0:T(8,128)S(1)}, u32[]{:S(2)}, u32[]{:S(2)}) collective-permute-start(f32[2,64,128]{2,1,0:T(8,128)S(1)} %get-tuple-element.53), channel_id=1, source_target_pairs={{1,2},{2,1},{3,4},{4,3},{5,6},{6,5},{9,10},{10,9},{11,12},{12,11},... | collective-permute-start | bytes 196616 | tf_op jit(solution)/shard_map/ppermute | solution.py:38
  26.0 25.1 %all-to-all-start = ((f32[32,16,128]{2,1,0:T(8,128)}), f32[32,16,128]{2,1,0:T(8,128)S(1)}, u32[]{:S(2)}, u32[]{:S(2)}) async-start(f32[32,16,128]{2,1,0:T(8,128)} %get-tuple-element.67), calls=%async_computation | async-start | bytes 524288 | tf_op jit(solution)/shard_map/all_to_all | solution.py:541
  39.4 7.6 %collective-permute-start.8 = (f32[3,32,128]{2,1,0:T(8,128)}, f32[3,32,128]{2,1,0:T(8,128)S(1)}, u32[]{:S(2)}, u32[]{:S(2)}) collective-permute-start(f32[3,32,128]{2,1,0:T(8,128)} %get-tuple-element.68), channel_id=1, source_target_pairs={{0,8},{8,0},{16,24},{24,16},{32,40},{40,32},{48,56},{56,48},{64,72... | collective-permute-start | bytes 147464 | tf_op jit(solution)/shard_map/ppermute | solution.py:38
  40.7 6.3 %collective-permute-start.9 = (f32[3,32,128]{2,1,0:T(8,128)}, f32[3,32,128]{2,1,0:T(8,128)S(1)}, u32[]{:S(2)}, u32[]{:S(2)}) collective-permute-start(f32[3,32,128]{2,1,0:T(8,128)} %get-tuple-element.69), channel_id=1, source_target_pairs={{8,16},{16,8},{24,32},{32,24},{40,48},{48,40},{56,64},{64,56},{72,... | collective-permute-start | bytes 147464 | tf_op jit(solution)/shard_map/ppermute | solution.py:38
  47.0 9.0 %copy-start = (f32[3,32,128]{2,1,0:T(8,128)}, f32[3,32,128]{2,1,0:T(8,128)S(1)}, u32[]{:S(2)}) copy-start(f32[3,32,128]{2,1,0:T(8,128)S(1)} %collective-permute-done.8.ra_hbm) | copy-start | bytes 147460
  47.0 9.0 %copy-start.1 = (f32[3,32,128]{2,1,0:T(8,128)}, f32[3,32,128]{2,1,0:T(8,128)S(1)}, u32[]{:S(2)}) copy-start(f32[3,32,128]{2,1,0:T(8,128)S(1)} %collective-permute-done.9.rb_hbm) | copy-start | bytes 147460
  51.1 8.0 %collective-permute-start.10 = (f32[23,16,128]{2,1,0:T(8,128)S(1)}, f32[23,16,128]{2,1,0:T(8,128)S(1)}, u32[]{:S(2)}, u32[]{:S(2)}) collective-permute-start(f32[23,16,128]{2,1,0:T(8,128)S(1)} %constant_dynamic-slice_fusion.g), channel_id=1, source_target_pairs={{0,1},{1,0},{2,3},{3,2},{4,5},{5,4},{6,7},{7,6},{8,9},{9,8},{10,11... | collective-permute-start | bytes 565256 | tf_op jit(solution)/shard_map/ppermute | solution.py:38
  51.2 7.9 %collective-permute-start.11 = (f32[23,16,128]{2,1,0:T(8,128)S(1)}, f32[23,16,128]{2,1,0:T(8,128)S(1)}, u32[]{:S(2)}, u32[]{:S(2)}) collective-permute-start(f32[23,16,128]{2,1,0:T(8,128)S(1)} %constant_dynamic-slice_fusion.g), channel_id=1, source_target_pairs={{1,2},{2,1},{3,4},{4,3},{5,6},{6,5},{9,10},{10,9},{11,12},{12,11},... | collective-permute-start | bytes 565256 | tf_op jit(solution)/shard_map/ppermute | solution.py:38
